TPU v7x, 32 devices: a whole 2x2x4 slice. The times are simulated.
32 devices in a mesh: dp: 4 (over y, x), blk: 8 (over z, core).
Axes of the slice: x: 2, y: 2, z: 4, core: 2. Of those that a mesh axis runs over, the one named last changes fastest.
Arguments:
- tokens: bfloat16 [32, 64, 64, 320], P('dp', 'blk'), may hold values from -6 to 6
- mask: int32 [32, 64, 64], P('dp', 'blk'), may hold values from 0 to 1, as said below
- labels: int32 [32, 64, 64], P('dp', 'blk'), may hold values from 0 to 18
- predicted: int32 [32, 64, 64], P('dp', 'blk'), may hold values from 0 to 18
- cotangent: bfloat16 [32, 64, 64, 320], P('dp', 'blk'), may hold values from -6 to 6
- norm1_gain: float32 [320], replicated, may hold values from 0.1 to 1.9
- norm1_bias: float32 [320], replicated, may hold values from -3 to 3
- query_weight: bfloat16 [320, 320], replicated, may hold values from -0.3125 to 0.3125
- query_bias: float32 [320], replicated, may hold values from -3 to 3
- reduce_weight: bfloat16 [1280, 320], replicated, may hold values from -0.15625 to 0.15625
- reduce_bias: float32 [320], replicated, may hold values from -3 to 3
- rnorm_gain: float32 [320], replicated, may hold values from 0.1 to 1.9
- rnorm_bias: float32 [320], replicated, may hold values from -3 to 3
- kv_weight: bfloat16 [320, 640], replicated, may hold values from -0.3125 to 0.3125
- value_bias: float32 [320], replicated, may hold values from -3 to 3
- proj_weight: bfloat16 [320, 320], replicated, may hold values from -6 to 6
- proj_bias: float32 [320], replicated, may hold values from -3 to 3
- norm2_gain: float32 [320], replicated, may hold values from 0.1 to 1.9
- norm2_bias: float32 [320], replicated, may hold values from -3 to 3
- expand_weight: bfloat16 [320, 1280], replicated, may hold values from -0.3125 to 0.3125
- expand_bias: float32 [1280], replicated, may hold values from -3 to 3
- depth_weight: float32 [9, 1280], replicated, may hold values from -2 to 2
- depth_bias: float32 [1280], replicated, may hold values from -3 to 3
- shrink_weight: bfloat16 [1280, 320], replicated, may hold values from -0.15625 to 0.15625
- shrink_bias: float32 [320], replicated, may hold values from -3 to 3
Outputs:
- output: bfloat16 [32, 64, 64, 320], P('dp', 'blk')
- input_grad: float32 [32, 64, 64, 320], P('dp', 'blk')
- norm1_gain_grad: float32 [320], replicated
- norm1_bias_grad: float32 [320], replicated
- query_weight_grad: float32 [320, 320], replicated
- query_bias_grad: float32 [320], replicated
- reduce_weight_grad: float32 [1280, 320], replicated
- reduce_bias_grad: float32 [320], replicated
- rnorm_gain_grad: float32 [320], replicated
- rnorm_bias_grad: float32 [320], replicated
- kv_weight_grad: float32 [320, 640], replicated
- value_bias_grad: float32 [320], replicated
- proj_weight_grad: float32 [320, 320], replicated
- proj_bias_grad: float32 [320], replicated
- norm2_gain_grad: float32 [320], replicated
- norm2_bias_grad: float32 [320], replicated
- expand_weight_grad: float32 [320, 1280], replicated
- expand_bias_grad: float32 [1280], replicated
- depth_weight_grad: float32 [9, 1280], replicated
- depth_bias_grad: float32 [1280], replicated
- shrink_weight_grad: float32 [1280, 320], replicated
- shrink_bias_grad: float32 [320], replicated
- confusion: int32 [19, 19], replicated
Inputs may be any that keep to these rules, and one draw needn't show every extreme that they name: `mask`: in every scene the 1s fill a rectangle at the top left: the first rows, from 32 to 48 of them, and in these rows the first columns, from 32 to 63 of them; all other entries are 0.
All inputs are finite; a program needn't handle non-finite values.
Results may differ from a plain program's by a relative error of at most 0.018.
Values may be sent and summed in bfloat16 or wider, within the bound.
A program may use at most 448 MiB of HBM per device.

v0:
```python
import jax
import jax.numpy as jnp
from jax import lax
from jax.sharding import PartitionSpec as P

HEADS = 5
CLASSES = 19


EPSILON = 1e-06
NEGATIVE = -32768.0


def extended(cells, sides, width):
    for axis, dim in sides:
        count = lax.axis_size(axis)
        ends = count - 1
        head = lax.slice_in_dim(cells, 0, width, axis=dim)
        tail = lax.slice_in_dim(cells, cells.shape[dim] - width, cells.shape[dim], axis=dim)
        cells = jnp.concatenate(
            [
                lax.ppermute(tail, axis, [(i, (i + 1) % count) for i in range(ends)]),
                cells,
                lax.ppermute(head, axis, [((i + 1) % count, i) for i in range(ends)]),
            ],
            axis=dim,
        )
    return cells


def layer_norm(value, gain, shift):
    center = value - jnp.mean(value, -1, keepdims=True)
    spread = jnp.mean(center * center, -1, keepdims=True)
    return center * lax.rsqrt(spread + EPSILON) * gain + shift


def gelu_exact(value):
    return jax.nn.gelu(value, approximate=False)


def pad_columns(value):
    return jnp.pad(value, ((0, 0), (0, 0), (1, 1), (0, 0)))


def depth_apply(padded, taps, height, width):
    total = jnp.zeros((padded.shape[0], height, width, padded.shape[3]), jnp.float32)
    for index in range(9):
        window = padded[:, index // 3 : index // 3 + height, index % 3 : index % 3 + width]
        total = total + taps[index] * window.astype(jnp.float32)
    return total


def split_keys(keyval):
    channels = keyval.shape[2] // 2
    return keyval[:, :, :channels].reshape(
        keyval.shape[0], keyval.shape[1], HEADS, channels // HEADS
    )


def split_values(keyval):
    channels = keyval.shape[2] // 2
    return keyval[:, :, channels:].reshape(
        keyval.shape[0], keyval.shape[1], HEADS, channels // HEADS
    )


def head_scores(query_heads, keyval, keybias, scale):
    raw = jnp.einsum(
        "sqhd,skhd->shqk", query_heads, split_keys(keyval), preferred_element_type=jnp.float32
    )
    return raw * scale + keybias.astype(jnp.float32)[:, None, None, :]


def body(
    tokens,
    mask,
    labels,
    predicted,
    cotangent,
    norm1_gain,
    norm1_bias,
    query_weight,
    query_bias,
    reduce_weight,
    reduce_bias,
    rnorm_gain,
    rnorm_bias,
    kv_weight,
    value_bias,
    proj_weight,
    proj_bias,
    norm2_gain,
    norm2_bias,
    expand_weight,
    expand_bias,
    depth_weight,
    depth_bias,
    shrink_weight,
    shrink_bias,
):
    scenes, height, width, channels = tokens.shape
    number = scenes * height * width
    local_rows = height * width
    half_rows, half_cols = (height // 2, width // 2)
    keys_local = half_rows * half_cols
    head_size = channels // HEADS
    scale = head_size ** (-0.5)
    hidden_width = expand_weight.shape[1]
    flat = tokens.astype(jnp.float32).reshape(number, channels)
    normed_low = layer_norm(flat, norm1_gain, norm1_bias).astype(jnp.bfloat16)
    query_low = (
        jnp.dot(normed_low, query_weight, preferred_element_type=jnp.float32) + query_bias
    ).astype(jnp.bfloat16)
    query_heads = query_low.reshape(scenes, local_rows, HEADS, head_size)
    patches = normed_low.reshape(scenes, half_rows, 2, half_cols, 2, channels).transpose(
        0, 1, 3, 2, 4, 5
    )
    patches = patches.reshape(scenes * keys_local, 4 * channels)
    reduced = jnp.dot(patches, reduce_weight, preferred_element_type=jnp.float32) + reduce_bias
    rnormed_low = layer_norm(reduced, rnorm_gain, rnorm_bias).astype(jnp.bfloat16)
    offsets = jnp.concatenate([jnp.zeros_like(value_bias), value_bias])
    keyval_low = (
        jnp.dot(rnormed_low, kv_weight, preferred_element_type=jnp.float32) + offsets
    ).astype(jnp.bfloat16)
    keyval_rows = keyval_low.reshape(scenes, keys_local, 2 * channels)
    covered = jnp.sum(mask.reshape(scenes, half_rows, 2, half_cols, 2), axis=(2, 4)) > 0
    keybias_low = jnp.where(covered, 0.0, NEGATIVE).astype(jnp.bfloat16).reshape(scenes, keys_local)
    start_top = jnp.full((scenes, HEADS, local_rows), -jnp.inf, jnp.float32)
    start_total = jnp.zeros((scenes, HEADS, local_rows), jnp.float32)
    start_sum = jnp.zeros((scenes, HEADS, local_rows, head_size), jnp.float32)
    piece = (
        lax.all_gather(keyval_rows, "blk", axis=1, tiled=True),
        lax.all_gather(keybias_low, "blk", axis=1, tiled=True),
    )
    run_total = start_total
    block = head_scores(query_heads, piece[0], piece[1], scale)
    new_top = jnp.max(block, -1)
    factor = jnp.exp(start_top - new_top)
    powers = jnp.exp(block - new_top[..., None])
    run_total = run_total * factor + jnp.sum(powers, -1)
    update = jnp.einsum(
        "shqk,skhd->shqd",
        powers.astype(jnp.bfloat16),
        split_values(piece[0]),
        preferred_element_type=jnp.float32,
    )
    folded = start_sum * factor[..., None] + update
    attended = (folded / run_total[..., None]).transpose(0, 2, 1, 3)
    attended_low = attended.reshape(number, channels).astype(jnp.bfloat16)
    resid = (
        flat + jnp.dot(attended_low, proj_weight, preferred_element_type=jnp.float32) + proj_bias
    )
    cnormed_low = layer_norm(resid, norm2_gain, norm2_bias).astype(jnp.bfloat16)
    hidden_low = (
        jnp.dot(cnormed_low, expand_weight, preferred_element_type=jnp.float32) + expand_bias
    ).astype(jnp.bfloat16)
    hidden_low = hidden_low.reshape(scenes, height, width, hidden_width)
    hidden_pad = pad_columns(extended(hidden_low, (("blk", 1),), 1))
    mixed = depth_apply(hidden_pad, depth_weight, height, width) + depth_bias
    active, gelu_back = jax.vjp(gelu_exact, mixed)
    active_low = active.astype(jnp.bfloat16).reshape(number, hidden_width)
    output = (
        resid + jnp.dot(active_low, shrink_weight, preferred_element_type=jnp.float32) + shrink_bias
    )
    output_low = output.astype(jnp.bfloat16).reshape(scenes, height, width, channels)
    upstream = cotangent.reshape(number, channels)
    shrink_weight_grad = jnp.einsum(
        "nf,nc->fc", active_low, upstream, preferred_element_type=jnp.float32
    )
    shrink_bias_grad = jnp.sum(upstream.astype(jnp.float32), 0)
    grad_active = jnp.einsum(
        "nc,fc->nf", upstream, shrink_weight, preferred_element_type=jnp.float32
    )
    grad_mixed_low = gelu_back(grad_active.reshape(scenes, height, width, hidden_width))[0].astype(
        jnp.bfloat16
    )
    grad_mixed = grad_mixed_low.astype(jnp.float32)
    depth_bias_grad = jnp.sum(grad_mixed, (0, 1, 2))
    tap_grads = []
    for index in range(9):
        window = hidden_pad[
            :, index // 3 : index // 3 + height, index % 3 : index % 3 + width
        ].astype(jnp.float32)
        tap_grads.append(jnp.sum(window * grad_mixed, (0, 1, 2)))
    depth_weight_grad = jnp.stack(tap_grads)
    grad_pad = pad_columns(extended(grad_mixed_low, (("blk", 1),), 1))
    grad_hidden = jnp.zeros((scenes, height, width, hidden_width), jnp.float32)
    for index in range(9):
        row_off, col_off = (2 - index // 3, 2 - index % 3)
        window = grad_pad[:, row_off : row_off + height, col_off : col_off + width].astype(
            jnp.float32
        )
        grad_hidden = grad_hidden + depth_weight[index] * window
    grad_hidden_low = grad_hidden.astype(jnp.bfloat16).reshape(number, hidden_width)
    expand_weight_grad = jnp.einsum(
        "nc,nf->cf", cnormed_low, grad_hidden_low, preferred_element_type=jnp.float32
    )
    expand_bias_grad = jnp.sum(grad_hidden_low.astype(jnp.float32), 0)
    grad_cnormed = jnp.einsum(
        "nf,cf->nc", grad_hidden_low, expand_weight, preferred_element_type=jnp.float32
    )
    norm2_out, norm2_back = jax.vjp(layer_norm, resid, norm2_gain, norm2_bias)
    resid_part, norm2_gain_grad, norm2_bias_grad = norm2_back(grad_cnormed)
    grad_resid = upstream.astype(jnp.float32) + resid_part
    grad_branch_low = grad_resid.astype(jnp.bfloat16)
    proj_weight_grad = jnp.einsum(
        "nc,ne->ce", attended_low, grad_branch_low, preferred_element_type=jnp.float32
    )
    proj_bias_grad = jnp.sum(grad_branch_low.astype(jnp.float32), 0)
    grad_attended_low = jnp.einsum(
        "ne,ce->nc", grad_branch_low, proj_weight, preferred_element_type=jnp.float32
    ).astype(jnp.bfloat16)
    grad_attended_heads = grad_attended_low.reshape(scenes, local_rows, HEADS, head_size)
    gathered = (
        lax.all_gather(keyval_rows, "blk", axis=1, tiled=True),
        lax.all_gather(keybias_low, "blk", axis=1, tiled=True),
    )
    scores = head_scores(query_heads, gathered[0], gathered[1], scale)
    weights = jnp.exp(scores - new_top[..., None]) / run_total[..., None]
    key_heads = split_keys(gathered[0])
    value_heads = split_values(gathered[0])
    grad_weights = jnp.einsum(
        "sqhd,skhd->shqk", grad_attended_heads, value_heads, preferred_element_type=jnp.float32
    )
    inner = jnp.sum(weights * grad_weights, -1, keepdims=True)
    grad_scores_low = (weights * (grad_weights - inner)).astype(jnp.bfloat16)
    grad_query = (
        jnp.einsum(
            "shqk,skhd->sqhd", grad_scores_low, key_heads, preferred_element_type=jnp.float32
        )
        * scale
    )
    grad_query_low = grad_query.astype(jnp.bfloat16).reshape(number, channels)
    grad_keys = (
        jnp.einsum(
            "shqk,sqhd->skhd", grad_scores_low, query_heads, preferred_element_type=jnp.float32
        )
        * scale
    )
    grad_values = jnp.einsum(
        "shqk,sqhd->skhd",
        weights.astype(jnp.bfloat16),
        grad_attended_heads,
        preferred_element_type=jnp.float32,
    )
    key_count = grad_keys.shape[1]
    term = jnp.concatenate(
        [
            grad_keys.reshape(scenes, key_count, channels),
            grad_values.reshape(scenes, key_count, channels),
        ],
        -1,
    )
    grad_keyval = lax.psum_scatter(
        term.astype(jnp.bfloat16), "blk", scatter_dimension=1, tiled=True
    )
    grad_keyval_low = grad_keyval.reshape(scenes * keys_local, 2 * channels)
    kv_weight_grad = jnp.einsum(
        "mc,me->ce", rnormed_low, grad_keyval_low, preferred_element_type=jnp.float32
    )
    value_bias_grad = jnp.sum(grad_keyval_low[:, channels:].astype(jnp.float32), 0)
    grad_rnormed = jnp.einsum(
        "me,ce->mc", grad_keyval_low, kv_weight, preferred_element_type=jnp.float32
    )
    rnorm_out, rnorm_back = jax.vjp(layer_norm, reduced, rnorm_gain, rnorm_bias)
    grad_reduced, rnorm_gain_grad, rnorm_bias_grad = rnorm_back(grad_rnormed)
    grad_reduced_low = grad_reduced.astype(jnp.bfloat16)
    reduce_weight_grad = jnp.einsum(
        "mp,mc->pc", patches, grad_reduced_low, preferred_element_type=jnp.float32
    )
    reduce_bias_grad = jnp.sum(grad_reduced_low.astype(jnp.float32), 0)
    grad_patches = jnp.einsum(
        "mc,pc->mp", grad_reduced_low, reduce_weight, preferred_element_type=jnp.float32
    )
    grad_patches = grad_patches.reshape(scenes, half_rows, half_cols, 2, 2, channels).transpose(
        0, 1, 3, 2, 4, 5
    )
    grad_patches = grad_patches.reshape(number, channels)
    query_weight_grad = jnp.einsum(
        "nc,ne->ce", normed_low, grad_query_low, preferred_element_type=jnp.float32
    )
    query_bias_grad = jnp.sum(grad_query_low.astype(jnp.float32), 0)
    grad_normed = (
        jnp.einsum("ne,ce->nc", grad_query_low, query_weight, preferred_element_type=jnp.float32)
        + grad_patches
    )
    norm1_out, norm1_back = jax.vjp(layer_norm, flat, norm1_gain, norm1_bias)
    flat_part, norm1_gain_grad, norm1_bias_grad = norm1_back(grad_normed)
    input_grad = (grad_resid + flat_part).reshape(scenes, height, width, channels)
    classes = jnp.arange(CLASSES, dtype=jnp.int32)[None, :]
    real_tokens = mask.reshape(number, 1).astype(jnp.bfloat16)
    label_hot = (labels.reshape(number, 1) == classes).astype(jnp.bfloat16) * real_tokens
    pred_hot = (predicted.reshape(number, 1) == classes).astype(jnp.bfloat16)
    local_counts = jnp.einsum("nl,np->lp", label_hot, pred_hot, preferred_element_type=jnp.float32)
    summed = lax.psum(
        (
            norm1_gain_grad,
            norm1_bias_grad,
            query_weight_grad,
            query_bias_grad,
            reduce_weight_grad,
            reduce_bias_grad,
            rnorm_gain_grad,
            rnorm_bias_grad,
            kv_weight_grad,
            value_bias_grad,
            proj_weight_grad,
            proj_bias_grad,
            norm2_gain_grad,
            norm2_bias_grad,
            expand_weight_grad,
            expand_bias_grad,
            depth_weight_grad,
            depth_bias_grad,
            shrink_weight_grad,
            shrink_bias_grad,
            local_counts,
        ),
        ("dp", "blk"),
    )
    return (
        output_low,
        input_grad,
        summed[0],
        summed[1],
        summed[2],
        summed[3],
        summed[4],
        summed[5],
        summed[6],
        summed[7],
        summed[8],
        summed[9],
        summed[10],
        summed[11],
        summed[12],
        summed[13],
        summed[14],
        summed[15],
        summed[16],
        summed[17],
        summed[18],
        summed[19],
        summed[20].astype(jnp.int32),
    )


def solution(mesh):
    in_specs = (
        P("dp", "blk", None, None),
        P("dp", "blk", None),
        P("dp", "blk", None),
        P("dp", "blk", None),
        P("dp", "blk", None, None),
        P(),
        P(),
        P(),
        P(),
        P(),
        P(),
        P(),
        P(),
        P(),
        P(),
        P(),
        P(),
        P(),
        P(),
        P(),
        P(),
        P(),
        P(),
        P(),
        P(),
    )
    out_specs = (
        P("dp", "blk", None, None),
        P("dp", "blk", None, None),
        P(),
        P(),
        P(),
        P(),
        P(),
        P(),
        P(),
        P(),
        P(),
        P(),
        P(),
        P(),
        P(),
        P(),
        P(),
        P(),
        P(),
        P(),
        P(),
        P(),
        P(),
    )
    return jax.shard_map(body, mesh=mesh, in_specs=in_specs, out_specs=out_specs, check_vma=False)
```

profile of v0, /device:TPU:0, one launch (start us, length us, event | category | flops | bytes accessed | tf_op | source)
XLA Modules:
  0.0 1261.2 jit_solution(15513714056020822906)
XLA Ops:
  7.3 3.9 convert_reduce_fusion.4
  11.1 6.5 copy_convert_fusion
  17.9 5.1 multiply_reduce_fusion.1
  23.6 5.2 fusion.48
  28.9 4.8 copy.245
  33.7 6.6 reshape.335
  40.4 2.9 fusion.96
  46.7 6.6 copy.235
  53.8 15.5 %all_gather.9 = bf16[8,1024]{1,0:T(8,128)(2,1)S(1)} all-gather(bf16[8,128]{1,0:T(8,128)(2,1)S(1)} %copy.249), channel_id=1, replica_groups=mesh['dp'=4,'blk'=8] {'blk'}, dimensions={1}, use_global_device_ids=true | all-gather | bytes 18432 | tf_op jit(solution)/shard_map/all_gather | solution.py:133
  69.3 6.8 copy.252
  76.1 4.3 fusion.45
  81.6 67.3 %all-gather.2.cloned.1.call-done = bf16[8,1024,640]{2,1,0:T(8,128)(2,1)} async-done(((bf16[8,128,640]{2,1,0:T(8,128)(2,1)}), bf16[8,1024,640]{2,1,0:T(8,128)(2,1)}) %all-gather.2.cloned.1.call-update) | async-done | bytes 10485776 | tf_op jit(solution)/shard_map/all_gather | solution.py:132
  148.9 11.9 fusion.95
  160.8 8.2 copy.246
  169.0 32.6 %fusion = (f32[8,5,512]{2,1,0:T(8,128)}, f32[8,5,512,1024]{3,2,1,0:T(8,128)}) fusion(f32[8,1024]{1,0:T(8,128)S(1)} %convert_element_type.201, bf16[8,1024,5,64]{1,3,2,0:T(8,128)(2,1)} %bitcast.122, bf16[8,512,5,64]{1,0,3,2:T(8,128)(2,1)S(1)} %bitcast.128), kind=kOutput, calls=%fused_computation.4 | convolution fusion | flops 2747248640 | bytes 91865088 | tf_op jit(solution)/shard_map/sqhd,skhd->shqk/dot_general | solution.py:68
  201.6 26.4 %fusion.2 = f32[8,5,512]{2,1,0:T(8,128)S(1)} fusion(f32[8,5,512,1024]{3,2,1,0:T(8,128)} %get-tuple-element.129, f32[8,5,512]{2,1,0:T(8,128)} %get-tuple-element.128, f32[8,1024]{1,0:T(8,128)S(1)} %convert_element_type.201), kind=kLoop, calls=%fused_computation.19 | loop fusion | flops 83865600 | bytes 84082688 | tf_op jit(solution)/shard_map/reduce_sum | solution.py:140
  228.7 8.2 copy.250
  236.9 31.8 %fusion.47 = bf16[8,512,5,64]{1,3,2,0:T(8,128)(2,1)} fusion(f32[8,512,5]{1,2,0:T(8,128)S(1)} %bitcast_add_fusion.1, f32[8,512,5]{1,2,0:T(8,128)S(1)} %get-tuple-element.123, bf16[8,1024,5,64]{1,3,2,0:T(8,128)(2,1)} %bitcast.143, f32[8,5,512,1024]{3,2,1,0:T(8,128)} %get-tuple-element.129, f32[8,5,512]{2,1,0:T(8,128)S(1)} %copy-done.22, ...), kind=kOutput, calls=%fused_computation.106 | convolution fusion | flops 2772172800 | bytes 92028928 | tf_op jit(solution)/shard_map/shqk,skhd->shqd/dot_general | solution.py:141
  268.7 3.3 copy.251
  273.3 5.1 fusion.97
  280.2 6.3 add_convert_fusion.1
  291.6 2.4 collective-permute-done.1
  294.0 6.3 select_maximum_fusion.2
  300.3 79.1 %multiply_convert_fusion.1 = (bf16[8,8,64,1280]{3,2,1,0:T(8,128)(2,1)}, f32[8,8,64,1280]{3,2,1,0:T(8,128)}, f32[8,8,64,1280]{3,2,1,0:T(8,128)}) fusion(f32[1280]{0:T(1024)S(1)} %copy-done.86, bf16[8,10,66,1280]{3,2,1,0:T(8,128)(2,1)} %select_maximum_fusion.2, f32[1280]{0:T(1024)S(1)} %get-tuple-element.82, bf16[8,1,64,1280]{3,2,1,0:T(8,128)(2,1)} %copy-done.17, ...), kind=kLoop, calls=%fused_computation.62 | loop fusion | flops 492830720 | bytes 128501760 | tf_op jit(solution)/shard_map/convert_element_type | solution.py:161
  379.3 58.1 %convert_reduce_fusion = (f32[1280]{0:T(1024)}, f32[1280]{0:T(1024)}, f32[1280]{0:T(1024)}, f32[1280]{0:T(1024)}, f32[1280]{0:T(1024)}, /*index=5*/f32[1280]{0:T...) fusion(bf16[4096,1280]{1,0:T(8,128)(2,1)} %copy-done.4, ...), kind=kOutput, calls=%fused_computation.5 | convolution fusion | flops 3591360000 | bytes 142428160 | tf_op jit(solution)/shard_map/nc,fc->nf/dot_general | solution.py:171
  437.4 3.9 copy-done.3
  443.1 15.9 %collective-permute-start.2 = (bf16[8,1,64,1280]{3,2,1,0:T(8,128)(2,1)}, bf16[8,1,64,1280]{3,2,1,0:T(8,128)(2,1)S(1)}, u32[]{:S(2)}, u32[]{:S(2)}) collective-permute-start(bf16[8,1,64,1280]{3,2,1,0:T(8,128)(2,1)} %get-tuple-element.116), channel_id=1, source_target_pairs={{0,1},{1,2},{2,3},{3,4},{4,5},{5,6},{6,7},{8,9},{9,10},{10,11},{11... | collective-permute-start | bytes 3932168 | tf_op jit(solution)/shard_map/ppermute | solution.py:22
  460.7 5.1 copy.254
  465.8 11.8 select_maximum_fusion
  477.6 42.2 %convert_reduce_fusion.1 = (f32[1280]{0:T(1024)}, bf16[8,8,64,1280]{3,2,1,0:T(8,128)(2,1)}) fusion(bf16[8,10,66,1280]{3,2,1,0:T(8,128)(2,1)} %select_maximum_fusion, f32[1280]{0:T(1024)S(1)} %get-tuple-element.82, bf16[8,8,64,1280]{3,2,1,0:T(8,128)(2,1)} %copy-done.3, bf16[8,1,64,1280]{3,2,1,0:T(8,128)(2,1)S(1)} %collective-permute-done.2, ...), kind=kLoop, calls=%fused_computation.60 | loop fusion | flops 162528000 | bytes 86558720 | tf_op jit(solution)/shard_map/reduce_sum | solution.py:198
  519.9 8.1 multiply_reduce_fusion.2
  534.1 2.7 copy.272
  536.8 33.2 %fusion.49 = bf16[8,5,64,1024]{3,2,1,0:T(8,128)(2,1)} fusion(bf16[8,512,5,64]{1,0,3,2:T(8,128)(2,1)} %bitcast.152, f32[8,5,512,1024]{3,2,1,0:T(8,128)} %get-tuple-element.129, f32[8,5,512]{2,1,0:T(8,128)S(1)} %copy-done.36, f32[8,5,512]{2,1,0:T(8,128)S(1)} %copy-done.23, f32[8,1024]{1,0:T(8,128)S(1)} %copy-done.21), kind=kOutput, calls=%fused_computation.122 | convolution fusion | flops 2791833600 | bytes 91947008 | tf_op jit(solution)/shard_map/shqk,sqhd->skhd/dot_general | solution.py:240
  570.0 65.2 %multiply_reduce_fusion = (f32[8,5,512]{2,1,0:T(8,128)}, f32[8,5,512,1024]{3,2,1,0:T(8,128)}) fusion(f32[8,5,512]{2,1,0:T(8,128)S(1)} %copy-done.36, f32[8,5,512]{2,1,0:T(8,128)S(1)} %copy-done.23, f32[8,1024]{1,0:T(8,128)S(1)} %copy-done.21, f32[8,5,512,1024]{3,2,1,0:T(8,128)} %get-tuple-element.129, bf16[8,1024,5,64]{1,3,2,0:T(8,128)(2,1)} %bitcast.144, ...), kind=kOutput, calls=%fused_computation.1 | convolution fusion | flops 2810163200 | bytes 175915008 | tf_op jit(solution)/shard_map/sqhd,skhd->shqk/dot_general | solution.py:222
  635.2 8.1 copy.260
  643.4 65.8 %multiply_convert_fusion = bf16[8,5,512,1024]{3,2,1,0:T(8,128)(2,1)} fusion(f32[8,5,512,1024]{3,2,1,0:T(8,128)} %get-tuple-element.134, f32[8,5,512]{2,1,0:T(8,128)} %get-tuple-element.133, f32[8,5,512]{2,1,0:T(8,128)} %get-tuple-element.122, f32[8,5,512]{2,1,0:T(8,128)} %get-tuple-element.128, f32[8,1024]{1,0:T(8,128)S(1)} %copy-done.21, ...), kind=kLoop, calls=%fused_computation | loop fusion | flops 146800640 | bytes 209993728 | tf_op jit(solution)/shard_map/convert_element_type | solution.py:226
  709.2 18.5 %multiply_convert_fusion.2 = bf16[8,5,64,1024]{3,2,1,0:T(8,128)(2,1)} fusion(bf16[8,5,512,1024]{3,2,1,0:T(8,128)(2,1)} %multiply_convert_fusion, bf16[8,512,5,64]{1,0,3,2:T(8,128)(2,1)S(1)} %bitcast.129), kind=kOutput, calls=%fused_computation.87 | convolution fusion | flops 2689597440 | bytes 49807360 | tf_op jit(solution)/shard_map/shqk,sqhd->skhd/dot_general | solution.py:235
  727.6 8.1 copy.259
  735.8 12.9 %pad_maximum_fusion.4 = bf16[8,1024,640]{2,1,0:T(8,128)(2,1)} fusion(bf16[8,1024,320]{2,1,0:T(8,128)(2,1)} %copy.260, bf16[8,1024,320]{2,1,0:T(8,128)(2,1)} %copy.259), kind=kLoop, calls=%fused_computation.86 | loop fusion | flops 20971520 | bytes 20971520 | tf_op jit(solution)/shard_map/concatenate | solution.py:247
  749.8 4.6 add_convert_fusion.2
  754.5 2.3 copy.265
  760.3 9.8 convolution_bitcast_fusion
  770.1 20.5 %convert_reduce_fusion.3 = (f32[5,64]{1,0:T(8,128)S(1)}, bf16[8,512,5,64]{1,3,2,0:T(8,128)(2,1)}) fusion(bf16[8,1024,5,64]{1,3,2,0:T(8,128)(2,1)S(1)} %bitcast.125, bf16[8,5,512,1024]{3,2,1,0:T(8,128)(2,1)} %multiply_convert_fusion), kind=kOutput, calls=%fused_computation.109 | convolution fusion | flops 2689597184 | bytes 49808640 | tf_op jit(solution)/shard_map/shqk,skhd->sqhd/dot_general | solution.py:228
  791.2 3.5 copy.256
  796.1 2.3 fusion.100
  798.4 2.7 fusion.99
  801.1 9.3 fusion.84
  810.4 58.6 %reduce-scatter.2.cloned.1.call-done = bf16[8,128,640]{2,1,0:T(8,128)(2,1)} async-done(((bf16[8,1024,640]{2,1,0:T(8,128)(2,1)}), bf16[8,128,640]{2,1,0:T(8,128)(2,1)}) %reduce-scatter.2.cloned.1.call-update) | async-done | bytes 1310736 | tf_op jit(solution)/shard_map/reduce_scatter | solution.py:254
  871.3 2.8 fusion.87
  878.5 4.1 fusion.98
  882.7 8.5 reshape.349
  891.2 8.4 copy.303
  899.5 8.5 reshape.350
  908.0 6.4 copy.262
  914.4 7.4 fusion.86
  921.9 3.5 multiply_reduce_fusion.3
  925.5 3.0 fusion.83
  928.5 12.2 add_convert_fusion.3
  940.7 2.7 copy.253
  943.4 10.9 add_add_fusion.2
  954.4 6.3 copy.263
  960.7 96.6 %all-reduce.8.cloned.1.call-done = (f32[320]{0:T(512)}, f32[320]{0:T(512)}, f32[320]{0:T(512)}, f32[320]{0:T(512)}, f32[320]{0:T(512)}, /*index=5*/f32[320]{0:T(...) async-done(((f32[320]{0:T(512)}, f32[320]{0:T(512)}, ...) | async-done | bytes 71860 | tf_op jit(solution)/shard_map/psum | solution.py:295
  1058.7 173.1 %all-reduce.10.cloned.1.call-done = (f32[320,320]{1,0:T(8,128)}, f32[1280,320]{0,1:T(8,128)}, f32[320,640]{1,0:T(8,128)}, f32[320,320]{1,0:T(8,128)}, f32[320,1280]{1,0:T(8,128)}, /*index=5*/f32[1280,320]{0,1:T(8,128)}) async-done(((f32[320,320]{1,0:T(8,128)}, f32[1280,320]{0,1:T(8,128)}, f32[320,640]{1,0:T(8,128)}, f32[320,320]{1,0:T(8,128)}, f32[320,1280]{1,0:T(8,128)}, /*index=5*/f32[1280,320]{0,1:T(8,128)}), ...) | async-done | bytes 6553616 | tf_op jit(solution)/shard_map/psum | solution.py:295
  1237.4 2.7 copy.329
  (323 shorter events, 58.8 us)
Async XLA Ops:
  7.2 372.1 %copy-start = (bf16[1280,320]{0,1:T(8,128)(2,1)S(1)}, bf16[1280,320]{0,1:T(8,128)(2,1)}, u32[]{:S(2)}) copy-start(bf16[1280,320]{0,1:T(8,128)(2,1)} %param.48) | copy-start | bytes 2457604
  7.2 141.7 %all-gather.2.cloned.1.call-start = ((), (), s32[]{:S(2)}) async-start(), calls=%async_computation.1 | async-start | bytes 11796480 | tf_op jit(solution)/shard_map/all_gather | solution.py:132
  11.1 12.5 copy-start.53
  11.1 12.5 copy-start.73
  17.9 11.0 copy-start.18
  28.9 11.5 copy-start.97
  33.7 10.4 copy-start.90
  33.7 10.6 copy-start.70
  33.7 10.6 copy-start.101
  46.5 822.5 %reduce-scatter.2.cloned.1.call-start = ((), (), s32[]{:S(2)}) async-start(), calls=%async_computation.2 | async-start | bytes 11796480 | tf_op jit(solution)/shard_map/reduce_scatter | solution.py:254
  46.7 29.4 %copy-start.38 = (f32[4096]{0:T(1024)}, f32[4096]{0:T(1024)S(1)}, u32[]{:S(2)}) copy-start(f32[4096]{0:T(1024)S(1)} %div.82) | copy-start | bytes 49156
  53.3 22.8 %copy-start.34 = (bf16[320,320]{1,0:T(8,128)(2,1)S(1)}, bf16[320,320]{1,0:T(8,128)(2,1)}, u32[]{:S(2)}) copy-start(bf16[320,320]{1,0:T(8,128)(2,1)} %param.32) | copy-start | bytes 614404
  53.3 22.8 %copy-start.98 = (f32[320]{0:T(512)S(1)}, f32[320]{0:T(512)}, u32[]{:S(2)}) copy-start(f32[320]{0:T(512)} %param.33) | copy-start | bytes 3844
  69.2 167.7 %copy-start.20 = (f32[8,1024]{1,0:T(8,128)}, f32[8,1024]{1,0:T(8,128)S(1)}, u32[]{:S(2)}) copy-start(f32[8,1024]{1,0:T(8,128)S(1)} %convert_element_type.201) | copy-start | bytes 98308
  69.3 11.1 copy-start.48
  69.3 11.1 copy-start.42
  81.6 87.5 %copy-start.7 = (bf16[40,8,8,512]{3,2,1,0:T(8,128)(2,1)}, bf16[40,8,8,512]{3,2,1,0:T(8,128)(2,1)S(1)}, u32[]{:S(2)}) copy-start(bf16[40,8,8,512]{3,2,1,0:T(8,128)(2,1)S(1)} %copy.270) | copy-start | bytes 7864324
  201.6 26.4 %copy-start.22 = (f32[8,5,512]{2,1,0:T(8,128)S(1)}, f32[8,5,512]{2,1,0:T(8,128)}, u32[]{:S(2)}) copy-start(f32[8,5,512]{2,1,0:T(8,128)} %get-tuple-element.128) | copy-start | bytes 245764
  273.2 6.9 copy-start.87
  273.3 6.9 copy-start.95
  273.3 6.9 copy-start.96
  278.4 8.1 copy-start.1
  278.5 8.1 copy-start.50
  280.2 10.4 copy-start.69
  286.6 13.7 %copy-start.4 = (bf16[4096,1280]{1,0:T(8,128)(2,1)}, bf16[4096,1280]{1,0:T(8,128)(2,1)S(1)}, u32[]{:S(2)}) copy-start(bf16[4096,1280]{1,0:T(8,128)(2,1)S(1)} %add_convert_fusion.1) | copy-start | bytes 31457284
  286.8 4.8 collective-permute-start
  289.1 4.9 collective-permute-start.1
  290.7 9.5 copy-start.86
  443.1 22.7 %collective-permute-start.2 = (bf16[8,1,64,1280]{3,2,1,0:T(8,128)(2,1)}, bf16[8,1,64,1280]{3,2,1,0:T(8,128)(2,1)S(1)}, u32[]{:S(2)}, u32[]{:S(2)}) collective-permute-start(bf16[8,1,64,1280]{3,2,1,0:T(8,128)(2,1)} %get-tuple-element.116), channel_id=1, source_target_pairs={{0,1},{1,2},{2,3},{3,4},{4,5},{5,6},{6,7},{8,9},{9,10},{10,11},{11... | collective-permute-start | bytes 3932168 | tf_op jit(solution)/shard_map/ppermute | solution.py:22
  459.0 6.8 collective-permute-start.3
  465.8 54.0 %slice-start.2 = ((s8[5242880]{0:T(1024)(128)(4,1)}), s8[4194304]{0:T(1024)(128)(4,1)S(1)}, s32[]{:S(2)}) async-start(s8[5242880]{0:T(1024)(128)(4,1)} %bitcast.113), calls=%async_computation.7 | async-start | bytes 8388608
  477.6 42.2 %slice-start.3 = ((s8[5242880]{0:T(1024)(128)(4,1)}), s8[1048576]{0:T(1024)(128)(4,1)S(1)}, s32[]{:S(2)}) async-start(s8[5242880]{0:T(1024)(128)(4,1)} %bitcast.113), calls=%async_computation.8 | async-start | bytes 2097152
  477.6 42.2 %copy-start.51 = (f32[4096]{0:T(1024)S(1)}, f32[4096]{0:T(1024)}, u32[]{:S(2)}) copy-start(f32[4096]{0:T(1024)} %copy-done.50) | copy-start | bytes 49156
  477.6 42.2 %copy-start.61 = (f32[4096]{0:T(1024)S(1)}, f32[4096]{0:T(1024)}, u32[]{:S(2)}) copy-start(f32[4096]{0:T(1024)} %copy-done.60) | copy-start | bytes 49156
  477.6 42.2 %copy-start.88 = (f32[320]{0:T(512)S(1)}, f32[320]{0:T(512)}, u32[]{:S(2)}) copy-start(f32[320]{0:T(512)} %param.42) | copy-start | bytes 3844
  519.8 8.1 copy-start.47
  643.4 65.8 %copy-start.8 = (bf16[40,8,8,512]{3,2,1,0:T(8,128)(2,1)S(1)}, bf16[40,8,8,512]{3,2,1,0:T(8,128)(2,1)}, u32[]{:S(2)}) copy-start(bf16[40,8,8,512]{3,2,1,0:T(8,128)(2,1)} %copy-done.7) | copy-start | bytes 7864324
  748.7 308.5 %all-reduce.8.cloned.1.call-start = ((), (), s32[]{:S(2)}) async-start(), calls=%async_computation.3 | async-start | bytes 266240 | tf_op jit(solution)/shard_map/psum | solution.py:295
  749.7 7.9 copy-start.13
  756.8 13.3 %slice-start.6 = ((s8[5242880]{0:T(1024)(128)(4,1)}), s8[1048576]{0:T(1024)(128)(4,1)S(1)}, s32[]{:S(2)}) async-start(s8[5242880]{0:T(1024)(128)(4,1)} %bitcast.123), calls=%async_computation.11 | async-start | bytes 2097152
  760.3 9.8 slice-start.7
  801.1 70.2 %copy-start.10 = (f32[1024,320]{0,1:T(8,128)S(1)}, f32[1024,320]{0,1:T(8,128)}, u32[]{:S(2)}) copy-start(f32[1024,320]{0,1:T(8,128)} %copy-done.9) | copy-start | bytes 3932164
  801.1 70.2 %copy-start.41 = (bf16[320,640]{1,0:T(8,128)(2,1)S(1)}, bf16[320,640]{1,0:T(8,128)(2,1)}, u32[]{:S(2)}) copy-start(bf16[320,640]{1,0:T(8,128)(2,1)} %param.38) | copy-start | bytes 1228804
  801.1 70.2 %copy-start.58 = (f32[1024]{0:T(1024)S(1)}, f32[1024]{0:T(1024)}, u32[]{:S(2)}) copy-start(f32[1024]{0:T(1024)} %copy-done.57) | copy-start | bytes 12292
  801.1 70.2 %copy-start.71 = (f32[320]{0:T(512)S(1)}, f32[320]{0:T(512)}, u32[]{:S(2)}) copy-start(f32[320]{0:T(512)} %param.36) | copy-start | bytes 3844
  801.1 72.9 %copy-start.66 = (f32[1024]{0:T(1024)S(1)}, f32[1024]{0:T(1024)}, u32[]{:S(2)}) copy-start(f32[1024]{0:T(1024)} %copy-done.65) | copy-start | bytes 12292
  801.1 72.9 %copy-start.64 = (f32[1024]{0:T(1024)S(1)}, f32[1024]{0:T(1024)}, u32[]{:S(2)}) copy-start(f32[1024]{0:T(1024)} %copy-done.63) | copy-start | bytes 12292
  869.0 7.3 copy-start.26
  908.0 13.8 %slice-start = ((s8[5242880]{0:T(1024)(128)(4,1)}), s8[1048576]{0:T(1024)(128)(4,1)S(1)}, s32[]{:S(2)}) async-start(s8[5242880]{0:T(1024)(128)(4,1)} %bitcast.111), calls=%async_computation.5 | async-start | bytes 2097152
  914.4 7.4 copy-start.49
  914.4 7.5 slice-start.1
  914.4 7.5 copy-start.43
  925.4 306.3 %all-reduce.10.cloned.1.call-start = ((), (), s32[]{:S(2)}) async-start(), calls=%async_computation.4 | async-start | bytes 13434880 | tf_op jit(solution)/shard_map/psum | solution.py:295
  928.5 15.0 %copy-start.45 = (f32[4096]{0:T(1024)S(1)}, f32[4096]{0:T(1024)}, u32[]{:S(2)}) copy-start(f32[4096]{0:T(1024)} %copy-done.44) | copy-start | bytes 49156
  1057.3 190.7 %copy-start.94 = (f32[320]{0:T(512)S(1)}, f32[320]{0:T(512)}, u32[]{:S(2)}) copy-start(f32[320]{0:T(512)} %get-tuple-element.153) | copy-start | bytes 3844
  1057.3 191.3 %copy-start.93 = (f32[320]{0:T(512)S(1)}, f32[320]{0:T(512)}, u32[]{:S(2)}) copy-start(f32[320]{0:T(512)} %get-tuple-element.154) | copy-start | bytes 3844
  1057.3 191.8 %copy-start.92 = (f32[320]{0:T(512)S(1)}, f32[320]{0:T(512)}, u32[]{:S(2)}) copy-start(f32[320]{0:T(512)} %get-tuple-element.155) | copy-start | bytes 3844
  1057.3 193.6 %copy-start.76 = (f32[1280]{0:T(1024)S(1)}, f32[1280]{0:T(1024)}, u32[]{:S(2)}) copy-start(f32[1280]{0:T(1024)} %get-tuple-element.157) | copy-start | bytes 15364
  1057.3 194.2 %copy-start.59 = (f32[9,1280]{1,0:T(8,128)S(1)}, f32[9,1280]{1,0:T(8,128)}, u32[]{:S(2)}) copy-start(f32[9,1280]{1,0:T(8,128)} %get-tuple-element.158) | copy-start | bytes 138244
  1057.3 194.8 %copy-start.75 = (f32[1280]{0:T(1024)S(1)}, f32[1280]{0:T(1024)}, u32[]{:S(2)}) copy-start(f32[1280]{0:T(1024)} %get-tuple-element.159) | copy-start | bytes 15364
  1231.7 15.4 %copy-start.37 = (f32[320,320]{1,0:T(8,128)S(1)}, f32[320,320]{1,0:T(8,128)}, u32[]{:S(2)}) copy-start(f32[320,320]{1,0:T(8,128)} %get-tuple-element.152) | copy-start | bytes 1228804
  1231.7 17.9 %copy-start.30 = (f32[320,1280]{1,0:T(8,128)S(1)}, f32[320,1280]{1,0:T(8,128)}, u32[]{:S(2)}) copy-start(f32[320,1280]{1,0:T(8,128)} %get-tuple-element.156) | copy-start | bytes 4915204
  1231.7 21.0 %copy-start.29 = (f32[1280,320]{0,1:T(8,128)S(1)}, f32[1280,320]{0,1:T(8,128)}, u32[]{:S(2)}) copy-start(f32[1280,320]{0,1:T(8,128)} %get-tuple-element.160) | copy-start | bytes 4915204
  1237.4 16.4 %copy-start.91 = (f32[320]{0:T(512)S(1)}, f32[320]{0:T(512)}, u32[]{:S(2)}) copy-start(f32[320]{0:T(512)} %get-tuple-element.161) | copy-start | bytes 3844
  (56 other events, 217.5 us)
Sparse Core Ops, SparseCore 0:
  46.7 102.1 all-gather.1
  748.9 120.1 reduce-scatter.1
  925.5 131.6 all-reduce.7
  1065.3 166.4 all-reduce.9
where the time goes:
time: 1270 us; the launch traced here: 1260 us
  waiting for transfers between devices  399 us (31%)
  matrix products  347 us (27%)
  other arithmetic  296 us (23%)
  local copies, waits for them, and re-layouts  167 us (13%)
  starting transfers between devices  21.5 us (2%)
  blocking collectives  15.5 us (1%)
  between operations  15.4 us (1%)
    psum x2, waiting for transfers between devices, body(): lax.psum((norm1_gain_grad, norm1_bias_grad, query_weight_grad, query_bias...  270 us
    convert_element_type x1, other arithmetic, body(): active_low = active.astype(jnp.bfloat16).reshape(number, hidden_width)  79.1 us
    all_gather x1, waiting for transfers between devices, body(): lax.all_gather(keyval_rows, 'blk', axis=1, tiled=True)  67.3 us
    convert_element_type x1, other arithmetic, body(): grad_scores_low = (weights * (grad_weights - inner)).astype(jnp.bfloat16)  65.8 us
    dot_general x1, matrix products, body(): jnp.einsum('sqhd,skhd->shqk', grad_attended_heads, value_heads, preferred...  65.2 us
    reduce_scatter x1, waiting for transfers between devices, body(): lax.psum_scatter(term.astype(jnp.bfloat16), 'blk', scatter_dimension=1, t...  58.6 us
    dot_general x1, matrix products, body(): jnp.einsum('nc,fc->nf', upstream, shrink_weight, preferred_element_type=j...  58.1 us
    reduce_sum x1, other arithmetic, body(): expand_bias_grad = jnp.sum(grad_hidden_low.astype(jnp.float32), 0)  42.2 us
  transfers between devices with their start and end apart: 8, of which 6 were waited for; matrix products, arithmetic and copies ran while one was open for 10% of the time, Pallas kernels for 0%

commit v1 on v0

v1 whole, which is shorter than its diff:
```python
import functools

import jax
import jax.numpy as jnp
from jax import lax
from jax.experimental import pallas as pl
from jax.experimental.pallas import tpu as pltpu
from jax.sharding import PartitionSpec as P
import ml_dtypes
import numpy as np

HEADS = 5
CLASSES = 19
EPSILON = 1e-06
NEGATIVE = -32768.0
LOG2E = 1.4426950408889634
LN2 = 0.6931471805599453
F32 = jnp.float32
BF16 = jnp.bfloat16
LANE = 128
HALF = 64
KEY_CHUNK = 256
MASK_ROWS = 48
VMEM = 62 * 2**20
FF_CHUNK = 256


def up_to(value, step):
    return -(-value // step) * step


def dot(a, b):
    return lax.dot_general(a, b, (((1,), (0,)), ((), ())), preferred_element_type=F32)


def dot_nt(a, b):
    return lax.dot_general(a, b, (((1,), (1,)), ((), ())), preferred_element_type=F32)


def dot_tn(a, b):
    return lax.dot_general(a, b, (((0,), (0,)), ((), ())), preferred_element_type=F32)


def lanes(shape):
    return lax.broadcasted_iota(jnp.int32, shape, len(shape) - 1)


def whole(shape):
    return pl.BlockSpec(shape, lambda *_: (0,) * len(shape))


def per_scene(shape):
    return pl.BlockSpec((1,) + shape, lambda s: (s,) + (0,) * len(shape))


def centered(value, channels):
    mean = jnp.sum(value, -1, keepdims=True) * (1.0 / channels)
    center = jnp.where(lanes(value.shape) < channels, value - mean, 0.0)
    var = jnp.sum(center * center, -1, keepdims=True) * (1.0 / channels)
    rstd = lax.rsqrt(var + EPSILON)
    return center * rstd, rstd


def norm_back(up, gain, xhat, rstd, channels):
    u = up * gain
    mean = jnp.sum(u, -1, keepdims=True) * (1.0 / channels)
    proj = jnp.sum(u * xhat, -1, keepdims=True) * (1.0 / channels)
    return (u - mean - xhat * proj) * rstd


def ext_lane(head):
    return HALF if head % 2 == 0 else 0


def widen(value, width):
    pad = width - value.shape[-1]
    return jnp.concatenate([value, jnp.zeros(value.shape[:-1] + (pad,), value.dtype)], -1)


def place(blk):
    me = lax.axis_index("blk")
    core = lax.rem(me, 2)
    chip = me // 2
    return chip, core, {"blk": me + 2}, {"blk": me - 2}, {"blk": me + 1 - 2 * core}


def greet(chip, chips, up, down, sib):
    barrier = pltpu.get_barrier_semaphore()
    MESH = pl.DeviceIdType.MESH
    has_up, has_down = chip < chips - 1, chip > 0
    pl.semaphore_signal(barrier, inc=1, device_id=sib, device_id_type=MESH)

    @pl.when(has_up)
    def _():
        pl.semaphore_signal(barrier, inc=1, device_id=up, device_id_type=MESH)

    @pl.when(has_down)
    def _():
        pl.semaphore_signal(barrier, inc=1, device_id=down, device_id_type=MESH)

    pl.semaphore_wait(barrier, 1 + has_up.astype(jnp.int32) + has_down.astype(jnp.int32))


def remote(src, dst, send, recv, device):
    return pltpu.make_async_remote_copy(
        src_ref=src, dst_ref=dst, send_sem=send, recv_sem=recv, device_id=device,
        device_id_type=pl.DeviceIdType.MESH,
    )


def attend_kernel(
    dims, blk, used, tok_ref, mask_ref, label_ref, pred_ref, tok2_ref, vec_ref, wr_ref, wq_ref,
    one_ref, wk_ref, wv_ref, wp_ref,
    red_ref, cnt_ref, q_ref, att_ref, ke_ref, ve_ref, rn_ref, res_ref,
    scr, qbuf, oe, rnbuf, up_send, down_send, sib_send, line_recv, sib_recv,
):
    scenes, height, width, channels, cp = dims
    n = height * width
    keys = n // 4
    chips = blk // 2
    lag = chips
    step = pl.program_id(0)
    head_size = channels // HEADS
    chip, core, up, down, sib = place(blk)

    @pl.when(step == 0)
    def _():
        greet(chip, chips, up, down, sib)
        cnt_ref[...] = jnp.zeros(cnt_ref.shape, F32)

    def slot(origin, c):
        return c * used + origin

    def send_up(s, origin):
        place_ = rnbuf.at[s, slot(origin, core)]
        return remote(place_, place_, up_send.at[s, origin], line_recv.at[s, origin], up)

    def send_down(s, origin):
        place_ = rnbuf.at[s, slot(origin, core)]
        return remote(place_, place_, down_send.at[s, origin], line_recv.at[s, origin], down)

    def send_sib(s, origin):
        place_ = rnbuf.at[s, slot(origin, core)]
        return remote(place_, place_, sib_send.at[s, origin], sib_recv.at[s, origin], sib)

    @pl.when(step < scenes)
    def _():
        s = step
        x = widen(tok_ref[0].astype(F32), cp)
        xhat, _ = centered(x, channels)
        low = (xhat * vec_ref[0:1] + vec_ref[1:2]).astype(BF16)
        lowf = low.astype(F32)
        for t in range(cp // LANE):
            scr[t] = lowf[:, t * LANE : (t + 1) * LANE]
        total = jnp.zeros((keys, cp), F32)
        for b in range(2):
            part = [scr[t, pl.ds(b, n // 2, stride=2), :] for t in range(cp // LANE)]
            part = jnp.concatenate(part, -1).reshape(height // 2, 2, width // 2, cp)
            for a in range(2):
                total = total + dot(part[:, a].reshape(keys, cp).astype(BF16), wr_ref[2 * a + b])
        red_ref[0] = total
        rhat, _ = centered(total, channels)
        m = mask_ref[0].astype(F32)
        shape = (width // 2, width)
        near = lanes(shape) // 2 == lax.broadcasted_iota(jnp.int32, shape, 0)
        flags = []
        for i in range(height // 2):
            both = m[2 * i : 2 * i + 1] + m[2 * i + 1 : 2 * i + 2]
            flags.append(jnp.sum(jnp.where(near, both, 0.0), -1, keepdims=True))
        unc = jnp.where(jnp.concatenate(flags, 0) > 0.0, 0.0, 1.0)
        flag = jnp.where(lanes((keys, cp)) == channels, unc, 0.0)
        own = (rhat * vec_ref[2:3] + vec_ref[3:4] + flag).astype(BF16)

        @pl.when(chip < used)
        def _():
            rnbuf[s, slot(chip, core)] = own
            send_sib(s, chip).start()

            @pl.when(chip < chips - 1)
            def _():
                send_up(s, chip).start()

            @pl.when(chip > 0)
            def _():
                send_down(s, chip).start()

        qf = dot(low, wq_ref[...]) * (LOG2E * head_size**-0.5) + one_ref[...]
        qbuf[lax.rem(s, lag + 1)] = qf.astype(BF16)
        shape = (cnt_ref.shape[0], width)
        classes = lax.broadcasted_iota(jnp.int32, shape, 0)
        wide = lax.broadcasted_iota(jnp.int32, (LANE, width), 0)
        total = jnp.zeros(cnt_ref.shape, F32)
        for r in range(height):
            label = jnp.where(mask_ref[0, r : r + 1] > 0, label_ref[0, r : r + 1], -1)
            hot = jnp.where(label == classes, 1.0, 0.0).astype(BF16)
            pred = jnp.where(pred_ref[0, r : r + 1] == wide, 1.0, 0.0).astype(BF16)
            total = total + dot_nt(hot, pred)
        cnt_ref[...] += total

    for age in range(1, chips):
        s = step - age

        @pl.when(jnp.logical_and(s >= 0, s < scenes))
        def _(s=s, age=age):
            below = chip - age

            @pl.when(jnp.logical_and(below >= 0, below < used))
            def _():
                send_up(s, below).wait_recv()
                send_sib(s, below).start()

                @pl.when(chip < chips - 1)
                def _():
                    send_up(s, below).start()

            above = chip + age

            @pl.when(above < used)
            def _():
                send_down(s, above).wait_recv()
                send_sib(s, above).start()

                @pl.when(chip > 0)
                def _():
                    send_down(s, above).start()

    @pl.when(step >= lag)
    def _():
        s = step - lag

        for origin in range(used):
            send_sib(s, origin).wait_recv()

        rn_all = rnbuf[s].reshape(2 * used * keys, cp)
        rn_ref[0] = rn_all
        ke_ref[0] = dot(rn_all, wk_ref[...]).astype(BF16)
        ve_ref[0] = dot(rn_all, wv_ref[...]).astype(BF16)
        mine = lax.rem(s, lag + 1)
        count = 2 * used * keys // KEY_CHUNK
        for h in range(HEADS):
            block = slice(h * LANE, (h + 1) * LANE)
            e = ext_lane(h)
            q = qbuf[mine, :, block]
            parts = [
                dot_nt(q, ke_ref[0, j * KEY_CHUNK : (j + 1) * KEY_CHUNK, block])
                for j in range(count)
            ]
            top = functools.reduce(jnp.maximum, parts)
            top = jnp.max(top, -1, keepdims=True)
            out = jnp.zeros((n, LANE), F32)
            for j in range(count):
                p = jnp.exp2(parts[j] - top).astype(BF16)
                out = out + dot(p, ve_ref[0, j * KEY_CHUNK : (j + 1) * KEY_CHUNK, block])
            total = out[:, e : e + 1]
            oe[h] = out / total
            lse = top + jnp.log2(total)
            hi = lse.astype(BF16).astype(F32)
            mid = (lse - hi).astype(BF16).astype(F32)
            lo = lse - hi - mid
            lane = lanes((n, LANE))
            q2 = q.astype(F32)
            q2 = jnp.where(lane == e + 3, -hi, q2)
            q2 = jnp.where(lane == e + 4, -mid, q2)
            q2 = jnp.where(lane == e + 5, -lo, q2)
            q_ref[0, :, block] = q2.astype(BF16)

        tiles = []
        low_half = lanes((n, LANE)) < HALF
        for t in range(cp // LANE):
            other = oe[2 * t + 1] if 2 * t + 1 < HEADS else jnp.zeros((n, LANE), F32)
            tiles.append(jnp.where(low_half, oe[2 * t], other))
        att = jnp.concatenate(tiles, -1)
        att_ref[0] = att
        x = widen(tok2_ref[0].astype(F32), cp)
        resid = x + dot(att.astype(BF16), wp_ref[...]) + vec_ref[4:5]
        for t in range(cp // LANE):
            for r in range(height):
                for half in range(2):
                    base = r * width + half * (width // 2)
                    at = r * scenes * width + half * scenes + s
                    res_ref[t, pl.ds(at, width // 2, stride=2 * scenes), :] = resid[
                        base : base + width // 2, t * LANE : (t + 1) * LANE
                    ]

    @pl.when(step == scenes + lag - 1)
    def _():
        @pl.loop(0, scenes)
        def _(s):
            for origin in range(used):
                send_sib(s, origin).wait_send()

                @pl.when(jnp.logical_and(origin <= chip, chip < chips - 1))
                def _(origin=origin):
                    send_up(s, origin).wait_send()

                @pl.when(jnp.logical_and(origin >= chip, chip > 0))
                def _(origin=origin):
                    send_down(s, origin).wait_send()


def attend(dims, blk, used, cid, tok, mask, labels, predicted, vec, wr, wq, ones, wk, wv, wp):
    scenes, height, width, channels, cp = dims
    n = height * width
    keys = n // 4
    chips = blk // 2
    lag = chips
    k = blk * keys
    live = 2 * used * keys
    he = HEADS * LANE

    def early(shape):
        return pl.BlockSpec(
            (1,) + shape, lambda t: (jnp.minimum(t, scenes - 1),) + (0,) * len(shape)
        )

    def late(shape):
        return pl.BlockSpec((1,) + shape, lambda t: (jnp.maximum(t - lag, 0),) + (0,) * len(shape))

    return pl.pallas_call(
        functools.partial(attend_kernel, dims, blk, used),
        grid=(scenes + lag,),
        in_specs=[early((n, channels))]
        + [early((height, width))] * 3
        + [late((n, channels))]
        + [whole(v.shape) for v in (vec, wr, wq, ones, wk, wv, wp)],
        out_specs=[
            early((keys, cp)),
            whole((32, LANE)),
            late((n, he)),
            late((n, cp)),
            late((live, he)),
            late((live, he)),
            late((live, cp)),
            whole((cp // LANE, scenes * n, LANE)),
        ],
        out_shape=[
            jax.ShapeDtypeStruct((scenes, keys, cp), F32),
            jax.ShapeDtypeStruct((32, LANE), F32),
            jax.ShapeDtypeStruct((scenes, n, he), BF16),
            jax.ShapeDtypeStruct((scenes, n, cp), F32),
            jax.ShapeDtypeStruct((scenes, k, he), BF16),
            jax.ShapeDtypeStruct((scenes, k, he), BF16),
            jax.ShapeDtypeStruct((scenes, k, cp), BF16),
            jax.ShapeDtypeStruct((cp // LANE, scenes * n, LANE), F32),
        ],
        scratch_shapes=[
            pltpu.VMEM((cp // LANE, n, LANE), F32),
            pltpu.VMEM((lag + 1, n, he), BF16),
            pltpu.VMEM((HEADS, n, LANE), F32),
            pltpu.VMEM((scenes, 2 * used, keys, cp), BF16),
        ]
        + [pltpu.SemaphoreType.DMA((scenes, used))] * 5,
        compiler_params=pltpu.CompilerParams(
            vmem_limit_bytes=VMEM, collective_id=cid, has_side_effects=True
        ),
    )(tok, mask, labels, predicted, tok, vec, wr, wq, ones, wk, wv, wp)


def ffn_kernel(
    dims, ff, blk, res_ref, ct_ref, vec_ref, we_ref, ws_ref, taps_ref, tb_ref,
    out_hbm, gres_hbm, dwe_ref, dwst, dtap_ref, dtb_ref, dvec_ref,
    cn, cnt, ctt, ctx, oacc, gacc, hid, gm, halo, tapacc, out_stage, gres_stage,
    out_sem, gres_sem, cn_send, cn_recv, gm_send, gm_recv,
):
    scenes, height, width, channels, cp = dims
    n = height * width
    rw = scenes * width
    lt = cp // LANE
    fc = FF_CHUNK
    nchunk = ff // fc
    cols = width // 2
    pair = 2 * scenes
    me = lax.axis_index("blk")
    has_left = me > 0
    has_right = me < blk - 1
    left, right = {"blk": me - 1}, {"blk": me + 1}
    MESH = pl.DeviceIdType.MESH

    barrier = pltpu.get_barrier_semaphore()

    @pl.when(has_left)
    def _():
        pl.semaphore_signal(barrier, inc=1, device_id=left, device_id_type=MESH)

    @pl.when(has_right)
    def _():
        pl.semaphore_signal(barrier, inc=1, device_id=right, device_id_type=MESH)

    pl.semaphore_wait(barrier, has_left.astype(jnp.int32) + has_right.astype(jnp.int32))

    def row(r, size=rw):
        return pl.ds(pl.multiple_of(r * rw, rw), size)

    g2, b2 = vec_ref[5:6], vec_ref[6:7]

    def load3(ref, r):
        return jnp.concatenate([ref[t, row(r), :] for t in range(lt)], -1)

    def store3(ref, r, value):
        for t in range(lt):
            ref[t, row(r), :] = value[:, t * LANE : (t + 1) * LANE]

    @pl.loop(0, height)
    def _(r):
        x = load3(res_ref, r)
        xhat, _ = centered(x, channels)
        c = (xhat * g2 + b2).astype(BF16)
        cn[row(r + 1), :] = c
        cnt[:, row(r)] = c.T
        store3(oacc, r, x + vec_ref[7:8])

    def cn_copy(up):
        return pltpu.make_async_remote_copy(
            src_ref=cn.at[row(1 if up else height), :],
            dst_ref=cn.at[row(height + 1 if up else 0), :],
            send_sem=cn_send.at[0 if up else 1],
            recv_sem=cn_recv.at[0 if up else 1],
            device_id=left if up else right,
            device_id_type=MESH,
        )

    @pl.when(has_left)
    def _():
        cn_copy(True).start()

    @pl.when(has_right)
    def _():
        cn_copy(False).start()

    @pl.loop(0, scenes)
    def _(s):
        c = widen(ct_ref[s].astype(F32), cp)
        for t in range(lt):
            for r in range(height):
                for half in range(2):
                    base = r * width + half * cols
                    gacc[t, pl.ds(r * rw + half * scenes + s, cols, stride=pair), :] = c[
                        base : base + cols, t * LANE : (t + 1) * LANE
                    ]

    dvec_ref[...] = jnp.zeros(dvec_ref.shape, F32)

    @pl.loop(0, height)
    def _(r):
        c = load3(gacc, r)
        dvec_ref[2:3] += jnp.sum(c, 0, keepdims=True)
        low = c.astype(BF16)
        ctt[row(r), :] = low
        ctx[:, row(r)] = low.T
        store3(gacc, r, jnp.zeros((rw, cp), F32))

    dwe_ref[...] = jnp.zeros(dwe_ref.shape, F32)
    dwst[...] = jnp.zeros(dwst.shape, F32)

    @pl.when(has_left)
    def _():
        cn_copy(False).wait_recv()

    @pl.when(jnp.logical_not(has_left))
    def _():
        cn[row(0), :] = jnp.zeros((rw, cp), BF16)

    @pl.when(has_right)
    def _():
        cn_copy(True).wait_recv()

    @pl.when(jnp.logical_not(has_right))
    def _():
        cn[row(height + 1), :] = jnp.zeros((rw, cp), BF16)

    def put(ref, slot, r, value):
        v = value.reshape(cols, pair, fc)
        z = jnp.zeros((scenes, fc), F32)
        ref[slot, r, 1 : cols + 1] = v.astype(BF16)
        ref[slot, r, 0] = jnp.concatenate([z, v[cols - 1, :scenes]], 0).astype(BF16)
        ref[slot, r, cols + 1] = jnp.concatenate([v[0, scenes:], z], 0).astype(BF16)

    def gm_copy(k, slot, up):
        return pltpu.make_async_remote_copy(
            src_ref=gm.at[slot, 1 if up else height],
            dst_ref=halo.at[k, 1 if up else 0],
            send_sem=gm_send.at[k, 0 if up else 1],
            recv_sem=gm_recv.at[k, 0 if up else 1],
            device_id=left if up else right,
            device_id_type=MESH,
        )

    def phase_a(k, slot):
        span = pl.ds(pl.multiple_of(k * fc, fc), fc)

        @pl.loop(0, height + 2)
        def _(r):
            put(hid, slot, r, dot(cn[row(r), :], we_ref[:, span]))

        @pl.loop(0, height)
        def _(r):
            acc = None
            for a in range(3):
                line = hid[slot, r + a]
                for b in range(3):
                    tap = taps_ref[pl.ds(3 * a + b, 1), span].astype(BF16).reshape(1, 1, fc)
                    term = line[b : b + cols] * tap
                    acc = term if acc is None else acc + term
            mixed = acc.astype(F32).reshape(rw, fc) + tb_ref[:, span]
            phi = 0.5 + 0.5 * lax.erf(mixed * 0.7071067811865476)
            dens = jnp.exp2(mixed * mixed * (-0.5 * LOG2E)) * 0.3989422804014327
            active = (mixed * phi).astype(BF16)
            slope = phi + mixed * dens
            grad = dot(ctt[row(r), :], ws_ref[:, span]) * slope
            put(gm, slot, r + 1, grad)
            dtb_ref[:, span] += jnp.sum(grad.reshape(rw // 8, 8, fc), 0)
            o = dot_nt(active, ws_ref[:, span])
            for t in range(lt):
                oacc[t, row(r), :] += o[:, t * LANE : (t + 1) * LANE]
            dwst[:, span] += dot(ctx[:, row(r)], active)

        @pl.when(has_left)
        def _():
            gm_copy(k, slot, True).start()

        @pl.when(has_right)
        def _():
            gm_copy(k, slot, False).start()

    def phase_b(k, slot):
        span = pl.ds(pl.multiple_of(k * fc, fc), fc)

        @pl.when(has_left)
        def _():
            gm_copy(k, slot, False).wait_recv()
            gm[slot, 0] = halo[k, 0]

        @pl.when(jnp.logical_not(has_left))
        def _():
            gm[slot, 0] = jnp.zeros((cols + 2, pair, fc), BF16)

        @pl.when(has_right)
        def _():
            gm_copy(k, slot, True).wait_recv()
            gm[slot, height + 1] = halo[k, 1]

        @pl.when(jnp.logical_not(has_right))
        def _():
            gm[slot, height + 1] = jnp.zeros((cols + 2, pair, fc), BF16)

        tapacc[...] = jnp.zeros(tapacc.shape, F32)

        @pl.loop(0, height)
        def _(r):
            acc = None
            own = hid[slot, r + 1, 1 : cols + 1]
            for a in range(3):
                line = gm[slot, r + 2 - a]
                for b in range(3):
                    tap = taps_ref[pl.ds(3 * a + b, 1), span].astype(BF16).reshape(1, 1, fc)
                    window = line[2 - b : 2 - b + cols]
                    term = window * tap
                    acc = term if acc is None else acc + term
                    prod = own * window
                    q = cols // 4
                    prod = (prod[:q] + prod[q : 2 * q]) + (prod[2 * q : 3 * q] + prod[3 * q :])
                    tapacc[3 * a + b] += jnp.sum(prod.astype(F32), 0)
            low = acc.reshape(rw, fc)
            dwe_ref[:, span] += dot(cnt[:, row(r)], low)
            g = dot_nt(low, we_ref[:, span])
            for t in range(lt):
                gacc[t, row(r), :] += g[:, t * LANE : (t + 1) * LANE]

        for tap in range(9):
            dtap_ref[pl.ds(tap, 1), span] = jnp.sum(tapacc[tap], 0, keepdims=True)

        @pl.when(has_left)
        def _():
            gm_copy(k, slot, True).wait_send()

        @pl.when(has_right)
        def _():
            gm_copy(k, slot, False).wait_send()

    dtb_ref[...] = jnp.zeros(dtb_ref.shape, F32)

    @pl.loop(0, nchunk + 1)
    def _(k):
        slot = lax.rem(k, 2)

        @pl.when(k < nchunk)
        def _():
            phase_a(k, slot)

        @pl.when(k > 0)
        def _():
            phase_b(k - 1, 1 - slot)

    @pl.when(has_left)
    def _():
        cn_copy(True).wait_send()

    @pl.when(has_right)
    def _():
        cn_copy(False).wait_send()

    @pl.loop(0, height)
    def _(r):
        x = load3(res_ref, r)
        xhat, rstd = centered(x, channels)
        upstream = load3(gacc, r)
        dvec_ref[0:1] += jnp.sum(upstream * xhat, 0, keepdims=True)
        dvec_ref[1:2] += jnp.sum(upstream, 0, keepdims=True)
        g = ctt[row(r), :].astype(F32) + norm_back(upstream, g2, xhat, rstd, channels)
        store3(gacc, r, g)

    def gather(ref, s):
        rows = []
        for r in range(height):
            for half in range(2):
                rows.append(
                    jnp.concatenate(
                        [
                            ref[t, pl.ds(r * rw + half * scenes + s, cols, stride=pair), :]
                            for t in range(lt)
                        ],
                        -1,
                    )
                )
        return jnp.concatenate(rows, 0)[:, :channels]

    def out_copy(s, slot):
        return pltpu.make_async_copy(out_stage.at[slot], out_hbm.at[s], out_sem.at[slot])

    def gres_copy(s, slot):
        return pltpu.make_async_copy(gres_stage.at[slot], gres_hbm.at[s], gres_sem.at[slot])

    @pl.loop(0, scenes)
    def _(s):
        slot = lax.rem(s, 2)

        @pl.when(s >= 2)
        def _():
            out_copy(s - 2, slot).wait()
            gres_copy(s - 2, slot).wait()

        out_stage[slot] = gather(oacc, s).astype(BF16)
        gres_stage[slot] = gather(gacc, s)
        out_copy(s, slot).start()
        gres_copy(s, slot).start()

    for s in range(scenes - 2, scenes):
        out_copy(s, s % 2).wait()
        gres_copy(s, s % 2).wait()


def ffn(dims, blk, res, ct, vec, we, ws, taps, tb):
    scenes, height, width, channels, cp = dims
    n = height * width
    total = scenes * n
    rw = scenes * width
    ff = ws.shape[1]
    lt = cp // LANE
    nchunk = ff // FF_CHUNK
    strip = (width // 2 + 2, 2 * scenes, FF_CHUNK)
    vm = pl.BlockSpec(memory_space=pltpu.VMEM)
    hbm = pl.BlockSpec(memory_space=pl.ANY)
    return pl.pallas_call(
        functools.partial(ffn_kernel, dims, ff, blk),
        in_specs=[vm] * 7,
        out_specs=[hbm, hbm] + [vm] * 5,
        out_shape=[
            jax.ShapeDtypeStruct((scenes, n, channels), BF16),
            jax.ShapeDtypeStruct((scenes, n, channels), F32),
            jax.ShapeDtypeStruct((cp, ff), F32),
            jax.ShapeDtypeStruct((cp, ff), F32),
            jax.ShapeDtypeStruct((9, ff), F32),
            jax.ShapeDtypeStruct((8, ff), F32),
            jax.ShapeDtypeStruct((8, cp), F32),
        ],
        scratch_shapes=[
            pltpu.VMEM((total + 2 * rw, cp), BF16),
            pltpu.VMEM((cp, total), BF16),
            pltpu.VMEM((total, cp), BF16),
            pltpu.VMEM((cp, total), BF16),
            pltpu.VMEM((lt, total, LANE), F32),
            pltpu.VMEM((lt, total, LANE), F32),
            pltpu.VMEM((2, height + 2) + strip, BF16),
            pltpu.VMEM((2, height + 2) + strip, BF16),
            pltpu.VMEM((nchunk, 2) + strip, BF16),
            pltpu.VMEM((9, 2 * scenes, FF_CHUNK), F32),
            pltpu.VMEM((2, n, channels), BF16),
            pltpu.VMEM((2, n, channels), F32),
            pltpu.SemaphoreType.DMA((2,)),
            pltpu.SemaphoreType.DMA((2,)),
            pltpu.SemaphoreType.DMA((2,)),
            pltpu.SemaphoreType.DMA((2,)),
            pltpu.SemaphoreType.DMA((nchunk, 2)),
            pltpu.SemaphoreType.DMA((nchunk, 2)),
        ],
        compiler_params=pltpu.CompilerParams(
            vmem_limit_bytes=VMEM, collective_id=0, has_side_effects=True
        ),
    )(res, ct, vec, we, ws, taps, tb)


def attback_kernel(
    dims, blk, used, q_ref, att_ref, gres_ref, ke_ref, ve_ref, rn_ref, wpe_ref, wkv_ref,
    grn_ref, gqt_ref, dwp_ref, dwkv_ref, dbp_ref,
    ge, dqt, own, acc, sib_land, up_land, down_land,
    sib_send, sib_recv, up_send, up_recv, down_send, down_recv,
):
    scenes, height, width, channels, cp = dims
    n = height * width
    keys = n // 4
    chips = blk // 2
    lt = cp // LANE
    head_size = channels // HEADS
    step = pl.program_id(0)
    chip, core, up, down, sib = place(blk)
    count = 2 * used * keys // KEY_CHUNK

    @pl.when(step == 0)
    def _():
        greet(chip, chips, up, down, sib)
        dwp_ref[...] = jnp.zeros(dwp_ref.shape, F32)
        dwkv_ref[...] = jnp.zeros(dwkv_ref.shape, F32)
        dbp_ref[...] = jnp.zeros(dbp_ref.shape, F32)

    def to_sib(s):
        return remote(
            own.at[lax.rem(s, 2), 1 - core], sib_land.at[s], sib_send.at[s], sib_recv.at[s], sib
        )

    def to_up(s, target):
        return remote(
            acc.at[s, target], up_land.at[s, target], up_send.at[s, target], up_recv.at[s, target], up
        )

    def to_down(s, target):
        return remote(
            acc.at[s, target], down_land.at[s, target], down_send.at[s, target],
            down_recv.at[s, target], down,
        )

    def plus(a, b):
        return (a.astype(F32) + b.astype(F32)).astype(BF16)

    def chunk(j):
        s = step
        per = KEY_CHUNK // keys
        span = slice(j * KEY_CHUNK, (j + 1) * KEY_CHUNK)
        dks, dvs = [], []
        for h in range(HEADS):
            block = slice(h * LANE, (h + 1) * LANE)
            k, v = ke_ref[0, span, block], ve_ref[0, span, block]
            q, g = q_ref[0, :, block], ge[:, block]
            p = jnp.exp2(dot_nt(k, q))
            gs = (p * dot_nt(v, g)).astype(BF16)
            dvs.append(dot(p.astype(BF16), g))
            dks.append(dot(gs, q))
            dqt[block, :] += dot_tn(k, gs)
        low_half = lanes((KEY_CHUNK, LANE)) < HALF
        tiles = []
        for group, scale in ((dks, LN2), (dvs, 1.0)):
            for t in range(lt):
                other = (
                    group[2 * t + 1] if 2 * t + 1 < HEADS else jnp.zeros((KEY_CHUNK, LANE), F32)
                )
                tiles.append((jnp.where(low_half, group[2 * t], other) * scale).astype(BF16))
        gkv = jnp.concatenate(tiles, -1)
        grn = dot_nt(gkv, wkv_ref[...]).astype(BF16)
        for i in range(per):
            at = j * per + i
            own[lax.rem(s, 2), at // used, at % used] = grn[i * keys : (i + 1) * keys]
        dwkv_ref[...] += dot(rn_ref[0, span].T, gkv)

    @pl.when(step < scenes)
    def _():
        s = step
        gb = widen(gres_ref[0], cp).astype(BF16)
        dbp_ref[...] += jnp.sum(gb.astype(F32).reshape(n // 8, 8, cp), 0)
        att = att_ref[0]
        dwp_ref[...] += dot(att.astype(BF16).T, gb)
        gatt = dot_nt(gb, wpe_ref[...])
        lane = lanes((n, LANE))
        for h in range(HEADS):
            e = ext_lane(h)
            g = gatt[:, h * LANE : (h + 1) * LANE].astype(BF16).astype(F32)
            o = att[:, (h // 2) * LANE : (h // 2 + 1) * LANE]
            inner = jnp.sum(g * o, -1, keepdims=True)
            hi = inner.astype(BF16).astype(F32)
            g = jnp.where(lane == e, -hi, g)
            g = jnp.where(lane == e + 1, hi - inner, g)
            ge[:, h * LANE : (h + 1) * LANE] = g.astype(BF16)
        dqt[...] = jnp.zeros(dqt.shape, F32)
        chunk(0)

    s1 = step - 1

    @pl.when(jnp.logical_and(s1 >= 0, s1 < scenes))
    def _():
        to_sib(s1).wait()
        acc[s1] = plus(own[lax.rem(s1, 2), core], sib_land[s1])

    s_up = step - 1 - chip

    @pl.when(jnp.logical_and(s_up >= 0, s_up < scenes))
    def _():
        for target in range(1, used):

            @pl.when(target > chip)
            def _(target=target):
                @pl.when(chip > 0)
                def _():
                    to_up(s_up, target).wait_recv()
                    acc[s_up, target] = plus(acc[s_up, target], up_land[s_up, target])

                to_up(s_up, target).start()

    s_down = step - chips + chip

    @pl.when(jnp.logical_and(s_down >= 0, s_down < scenes))
    def _():
        for target in range(used):

            @pl.when(target < chip)
            def _(target=target):
                @pl.when(chip < chips - 1)
                def _():
                    to_down(s_down, target).wait_recv()
                    acc[s_down, target] = plus(acc[s_down, target], down_land[s_down, target])

                to_down(s_down, target).start()

    s_end = step - chips

    @pl.when(s_end >= 0)
    def _():
        @pl.when(chip < used)
        def _():
            grn_ref[0] = acc[s_end, chip].astype(F32)

            @pl.when(chip > 0)
            def _():
                to_up(s_end, chip).wait_recv()
                grn_ref[0] += up_land[s_end, chip].astype(F32)

            @pl.when(chip < chips - 1)
            def _():
                to_down(s_end, chip).wait_recv()
                grn_ref[0] += down_land[s_end, chip].astype(F32)

        @pl.when(chip >= used)
        def _():
            grn_ref[0] = jnp.zeros((keys, cp), F32)

    @pl.when(step < scenes)
    def _():
        s = step
        for j in range(1, count):
            chunk(j)
        to_sib(s).start()
        for h in range(HEADS):
            base = h * LANE + (0 if h % 2 == 0 else HALF)
            gqt_ref[0, h * HALF : (h + 1) * HALF] = (
                dqt[base : base + HALF, :] * head_size**-0.5
            ).astype(BF16)

    @pl.when(step == scenes + chips - 1)
    def _():
        @pl.loop(0, scenes)
        def _(s):
            for target in range(used):

                @pl.when(target > chip)
                def _(target=target):
                    to_up(s, target).wait_send()

                @pl.when(target < chip)
                def _(target=target):
                    to_down(s, target).wait_send()


def attback(dims, blk, used, cid, q, att, gres, ke, ve, rn, wpe, wkv):
    scenes, height, width, channels, cp = dims
    n = height * width
    keys = n // 4
    chips = blk // 2
    live = 2 * used * keys
    he = HEADS * LANE

    def early(shape):
        return pl.BlockSpec(
            (1,) + shape, lambda t: (jnp.minimum(t, scenes - 1),) + (0,) * len(shape)
        )

    def late(shape):
        return pl.BlockSpec((1,) + shape, lambda t: (jnp.maximum(t - chips, 0),) + (0,) * len(shape))

    land = (scenes, used, keys, cp)
    return pl.pallas_call(
        functools.partial(attback_kernel, dims, blk, used),
        grid=(scenes + chips,),
        in_specs=[
            early((n, he)),
            early((n, cp)),
            early((n, channels)),
            early((live, he)),
            early((live, he)),
            early((live, cp)),
            whole(wpe.shape),
            whole(wkv.shape),
        ],
        out_specs=[
            late((keys, cp)),
            early((channels, n)),
            whole((cp, cp)),
            whole((cp, 2 * cp)),
            whole((8, cp)),
        ],
        out_shape=[
            jax.ShapeDtypeStruct((scenes, keys, cp), F32),
            jax.ShapeDtypeStruct((scenes, channels, n), BF16),
            jax.ShapeDtypeStruct((cp, cp), F32),
            jax.ShapeDtypeStruct((cp, 2 * cp), F32),
            jax.ShapeDtypeStruct((8, cp), F32),
        ],
        scratch_shapes=[
            pltpu.VMEM((n, he), BF16),
            pltpu.VMEM((he, n), F32),
            pltpu.VMEM((2, 2, used, keys, cp), BF16),
            pltpu.VMEM(land, BF16),
            pltpu.VMEM(land, BF16),
            pltpu.VMEM(land, BF16),
            pltpu.VMEM(land, BF16),
            pltpu.SemaphoreType.DMA((scenes,)),
            pltpu.SemaphoreType.DMA((scenes,)),
        ]
        + [pltpu.SemaphoreType.DMA((scenes, used))] * 4,
        compiler_params=pltpu.CompilerParams(
            vmem_limit_bytes=VMEM, collective_id=cid, has_side_effects=True
        ),
    )(q, att, gres, ke, ve, rn, wpe, wkv)


def tail_kernel(
    dims, tok_ref, gqt_ref, gres_ref, grn_ref, red_ref, vec_ref, wq_ref, wr_ref,
    ig_ref, dwqt, dwrt, dvec_ref, scr, gscr,
):
    scenes, height, width, channels, cp = dims
    n = height * width
    keys = n // 4
    lt = cp // LANE
    s_id = pl.program_id(0)

    @pl.when(s_id == 0)
    def _():
        dwqt[...] = jnp.zeros(dwqt.shape, F32)
        dwrt[...] = jnp.zeros(dwrt.shape, F32)
        dvec_ref[...] = jnp.zeros(dvec_ref.shape, F32)

    rhat, rstd = centered(red_ref[0], channels)
    up = grn_ref[0].astype(F32)
    dvec_ref[0:1] += jnp.sum(up * rhat, 0, keepdims=True)
    dvec_ref[1:2] += jnp.sum(up, 0, keepdims=True)
    gred = norm_back(jnp.where(lanes(up.shape) < channels, up, 0.0), vec_ref[2:3], rhat, rstd, channels)
    gred = jnp.where(lanes(up.shape) < channels, gred, 0.0).astype(BF16)
    dvec_ref[2:3] += jnp.sum(gred.astype(F32), 0, keepdims=True)
    gred_t = gred.T

    x = widen(tok_ref[0].astype(F32), cp)
    xhat, xstd = centered(x, channels)
    low = (xhat * vec_ref[0:1] + vec_ref[1:2]).astype(BF16)
    lowf = low.astype(F32)
    for t in range(lt):
        scr[t] = lowf[:, t * LANE : (t + 1) * LANE]
    for b in range(2):
        part = [scr[t, pl.ds(b, n // 2, stride=2), :] for t in range(lt)]
        part = jnp.concatenate(part, -1).reshape(height // 2, 2, width // 2, cp)
        for a in range(2):
            ab = 2 * a + b
            dwrt[ab] += dot(gred_t, part[:, a].reshape(keys, cp).astype(BF16))
            back = dot_nt(gred, wr_ref[ab])
            for t in range(lt):
                for i in range(height // 2):
                    gscr[t, pl.ds((2 * i + a) * width + b, width // 2, stride=2), :] = back[
                        i * (width // 2) : (i + 1) * (width // 2), t * LANE : (t + 1) * LANE
                    ]
    gqt = gqt_ref[0]
    dwqt[...] += dot(gqt, low)
    gn = widen(dot_nt(gqt.T, wq_ref[...]), cp) + jnp.concatenate([gscr[t] for t in range(lt)], -1)
    dvec_ref[3:4] += jnp.sum(gn * xhat, 0, keepdims=True)
    dvec_ref[4:5] += jnp.sum(gn, 0, keepdims=True)
    gx = norm_back(gn, vec_ref[0:1], xhat, xstd, channels)
    ig_ref[0] = gres_ref[0] + gx[:, :channels]


def tail(dims, tok, gqt, gres, grn, red, vec, wqt, wr):
    scenes, height, width, channels, cp = dims
    n = height * width
    keys = n // 4
    lt = cp // LANE
    return pl.pallas_call(
        functools.partial(tail_kernel, dims),
        grid=(scenes,),
        in_specs=[
            per_scene((n, channels)),
            per_scene((channels, n)),
            per_scene((n, channels)),
            per_scene((keys, cp)),
            per_scene((keys, cp)),
            whole(vec.shape),
            whole(wqt.shape),
            whole(wr.shape),
        ],
        out_specs=[
            per_scene((n, channels)),
            whole((channels, cp)),
            whole((4, cp, cp)),
            whole((8, cp)),
        ],
        out_shape=[
            jax.ShapeDtypeStruct((scenes, n, channels), F32),
            jax.ShapeDtypeStruct((channels, cp), F32),
            jax.ShapeDtypeStruct((4, cp, cp), F32),
            jax.ShapeDtypeStruct((8, cp), F32),
        ],
        scratch_shapes=[
            pltpu.VMEM((lt, n, LANE), F32),
            pltpu.VMEM((lt, n, LANE), F32),
        ],
        compiler_params=pltpu.CompilerParams(vmem_limit_bytes=VMEM),
    )(tok, gqt, gres, grn, red, vec, wqt, wr)


def bit_orders(ndp, nblk):
    dp_bits, blk_bits = ndp.bit_length() - 1, nblk.bit_length() - 1
    assert ndp == 1 << dp_bits and nblk == 1 << blk_bits
    core = [("blk", 0)] if blk_bits else []
    xs = [("dp", b) for b in range(dp_bits // 2)]
    ys = [("dp", b) for b in range(dp_bits // 2, dp_bits)]
    zs = [("blk", b) for b in range(1, blk_bits)]
    return [core + xs + ys + zs, core + ys + zs + xs, core + zs + xs + ys]


def pack_plan(channels, ff, ndev):
    cp = up_to(channels, LANE)
    tall = up_to(channels + 2, 16)
    items = [
        ("we", tall, ff // LANE), ("ws", channels, ff // LANE), ("wr", channels, 4 * cp // LANE),
        ("wkv", tall, 2 * cp // LANE), ("wp", channels, cp // LANE), ("wq", channels, cp // LANE),
    ]
    plan, at = {}, 0
    for name, rows, slabs in items:
        plan[name] = (at, rows, slabs)
        at += rows * slabs
    unit = 16 * ndev
    units = -(-at // unit)
    last = units // 3 - (1 if units > 6 else 0)
    mid = (units - last) // 2
    sizes = [(units - last - mid) * unit, mid * unit, last * unit]
    return plan, at, sizes


def small_plan(channels, ff, ndev):
    cp = up_to(channels, LANE)
    plan = {"tap": (0, 16, ff // LANE)}
    at = 16 * (ff // LANE)
    plan["vec"] = (at, 16, cp // LANE)
    at += 16 * (cp // LANE)
    plan["count"] = (at, 32, 1)
    at += 32
    return plan, up_to(at, 8 * ndev)


def reduce_kernel(
    channels, ff, ndp, nblk, dwe, dws, dwr, dwkv, dwp, dwq, dtap, dtb, dvec2, dvec1, dbp, cnt,
    out_hbm, small_hbm, work, recv, done, swork, srecv, sdone, send_sem, recv_sem, out_sem,
):
    ndev = ndp * nblk
    cp = up_to(channels, LANE)
    orders = bit_orders(ndp, nblk)
    rounds = len(orders[0])
    plan, used, sizes = pack_plan(channels, ff, ndev)
    splan, srows = small_plan(channels, ff, ndev)
    MESH = pl.DeviceIdType.MESH
    index = {"dp": lax.axis_index("dp"), "blk": lax.axis_index("blk")}

    def partner(axis, bit):
        step = 1 << bit
        value = lax.rem(index[axis] // step, 2)
        return value, {axis: index[axis] + (1 - 2 * value) * step}

    barrier = pltpu.get_barrier_semaphore()
    for axis, bit in orders[0]:
        pl.semaphore_signal(barrier, inc=1, device_id=partner(axis, bit)[1], device_id_type=MESH)

    def put(name, ref, rows_from=None):
        at, rows, slabs = plan[name]
        for t in range(slabs):
            work[at + t * rows : at + (t + 1) * rows, :] = ref(t, rows).astype(BF16)

    def lane_slabs(ref):
        return lambda t, rows: ref[:rows, t * LANE : (t + 1) * LANE]

    put("we", lane_slabs(dwe))
    put("ws", lane_slabs(dws))
    per = cp // LANE
    put("wr", lambda t, rows: dwr[t // per, :rows, (t % per) * LANE : (t % per + 1) * LANE])
    put("wkv", lane_slabs(dwkv))
    put("wp", lane_slabs(dwp))
    put("wq", lane_slabs(dwq))
    if used < sum(sizes):
        work[used:, :] = jnp.zeros((sum(sizes) - used, LANE), BF16)
    swork[...] = jnp.zeros(swork.shape, F32)
    at, rows, slabs = splan["tap"]
    db = jnp.sum(dtb[...], 0, keepdims=True)
    for t in range(slabs):
        cut = slice(t * LANE, (t + 1) * LANE)
        swork[at + t * rows : at + t * rows + 9, :] = dtap[:, cut]
        swork[at + t * rows + 9 : at + t * rows + 10, :] = db[:, cut]
    at, rows, slabs = splan["vec"]
    pb = jnp.sum(dbp[...], 0, keepdims=True)
    for t in range(slabs):
        cut = slice(t * LANE, (t + 1) * LANE)
        swork[at + t * rows : at + t * rows + 3, :] = dvec2[0:3, cut]
        swork[at + t * rows + 3 : at + t * rows + 8, :] = dvec1[0:5, cut]
        swork[at + t * rows + 8 : at + t * rows + 9, :] = pb[:, cut]
    at, rows, _ = splan["count"]
    swork[at : at + rows, :] = cnt[...]

    pl.semaphore_wait(barrier, rounds)

    parts, at = [], 0
    for size, order in zip(sizes, orders):
        if size:
            parts.append([work, recv, at, size, order])
        at += size
    parts.append([swork, srecv, 0, srows, orders[0]])

    state = [(first, size) for _, _, first, size, _ in parts]
    landing = [first for _, _, first, _, _ in parts]
    for i in range(rounds):
        copies = []
        for p, (buf, land, _, _, order) in enumerate(parts):
            start, size = state[p]
            size //= 2
            bit, device = partner(*order[i])
            unit = 16 if buf is work else 8
            send = pl.multiple_of(start + (1 - bit) * size, unit)
            keep = pl.multiple_of(start + bit * size, unit)
            copy = pltpu.make_async_remote_copy(
                src_ref=buf.at[pl.ds(send, size), :],
                dst_ref=land.at[pl.ds(landing[p], size), :],
                send_sem=send_sem.at[p, i],
                recv_sem=recv_sem.at[p, i],
                device_id=device,
                device_id_type=MESH,
            )
            copy.start()
            copies.append((copy, keep, size, landing[p], unit))
            state[p] = (keep, size)
            landing[p] += size
        for p, (copy, keep, size, low, unit) in enumerate(copies):
            buf, land = parts[p][:2]
            copy.wait()
            step = next(c for c in (256, 128, 64, 32, 16, 8) if size % c == 0)

            @pl.loop(0, size // step)
            def _(j, buf=buf, land=land, keep=keep, low=low, step=step, unit=unit):
                mine = pl.ds(pl.multiple_of(keep + j * step, unit), step)
                theirs = pl.ds(pl.multiple_of(low + j * step, unit), step)
                buf[mine, :] = (buf[mine, :].astype(F32) + land[theirs, :].astype(F32)).astype(buf.dtype)

    for p, (buf, _, _, _, _) in enumerate(parts):
        start, size = state[p]
        unit = 16 if buf is work else 8
        rows = pl.ds(pl.multiple_of(start, unit), size)
        final = done if buf is work else sdone
        final[rows, :] = buf[rows, :]

    for i in reversed(range(rounds)):
        copies = []
        for p, (buf, _, _, _, order) in enumerate(parts):
            start, size = state[p]
            final = done if buf is work else sdone
            bit, device = partner(*order[i])
            unit = 16 if buf is work else 8
            rows = pl.ds(pl.multiple_of(start, unit), size)
            copy = pltpu.make_async_remote_copy(
                src_ref=final.at[rows, :],
                dst_ref=final.at[rows, :],
                send_sem=send_sem.at[p, rounds + i],
                recv_sem=recv_sem.at[p, rounds + i],
                device_id=device,
                device_id_type=MESH,
            )
            copy.start()
            copies.append(copy)
            state[p] = (start - bit * size, 2 * size)
        for copy in copies:
            copy.wait()

    a = pltpu.make_async_copy(done, out_hbm, out_sem.at[0])
    b = pltpu.make_async_copy(sdone, small_hbm, out_sem.at[1])
    a.start()
    b.start()
    a.wait()
    b.wait()


def reduce_all(channels, ff, ndp, nblk, *grads):
    ndev = ndp * nblk
    rounds = len(bit_orders(ndp, nblk)[0])
    _, _, sizes = pack_plan(channels, ff, ndev)
    _, srows = small_plan(channels, ff, ndev)
    total = sum(sizes)
    vm = pl.BlockSpec(memory_space=pltpu.VMEM)
    hbm = pl.BlockSpec(memory_space=pl.ANY)
    return pl.pallas_call(
        functools.partial(reduce_kernel, channels, ff, ndp, nblk),
        in_specs=[vm] * len(grads),
        out_specs=[hbm, hbm],
        out_shape=[
            jax.ShapeDtypeStruct((total, LANE), BF16),
            jax.ShapeDtypeStruct((srows, LANE), F32),
        ],
        scratch_shapes=[
            pltpu.VMEM((total, LANE), BF16),
            pltpu.VMEM((total, LANE), BF16),
            pltpu.VMEM((total, LANE), BF16),
            pltpu.VMEM((srows, LANE), F32),
            pltpu.VMEM((srows, LANE), F32),
            pltpu.VMEM((srows, LANE), F32),
            pltpu.SemaphoreType.DMA((4, 2 * rounds)),
            pltpu.SemaphoreType.DMA((4, 2 * rounds)),
            pltpu.SemaphoreType.DMA((2,)),
        ],
        compiler_params=pltpu.CompilerParams(
            vmem_limit_bytes=VMEM, collective_id=1, has_side_effects=True
        ),
    )(*grads)


def unpack_kernel(channels, ff, ndev, packed, small, *outs):
    cp = up_to(channels, LANE)
    plan, _, _ = pack_plan(channels, ff, ndev)
    splan, _ = small_plan(channels, ff, ndev)
    (g1, b1, wq, qb, wr, rb, rg, rbn, wkv, vb, wp, pb, g2, b2, we, eb, dt, db, ws, sb, cm) = outs
    lt = cp // LANE

    def slab(name, t, first=0, count=None):
        at, rows, _ = plan[name]
        count = rows if count is None else count
        return packed[at + t * rows + first : at + t * rows + first + count, :].astype(F32)

    for t in range(ff // LANE):
        cut = slice(t * LANE, (t + 1) * LANE)
        we[:, cut] = slab("we", t, 0, channels)
        eb[cut] = slab("we", t, channels, 16)[0]
        ws[:, cut] = slab("ws", t)
        at, rows, _ = splan["tap"]
        dt[:, cut] = small[at + t * rows : at + t * rows + 9, :]
        db[cut] = small[at + t * rows + 9, :]

    def wide(name, first, count=None, base=0):
        return jnp.concatenate([slab(name, base + t, first, count) for t in range(lt)], -1)

    parts = [wide("wr", 0, base=ab * lt) for ab in range(4)]
    wr[...] = jnp.concatenate([v[:, :channels] for v in parts], -1)
    rb[...] = parts[0].T[channels]
    turned = wide("wq", 0).T
    wq[...] = turned[:channels]
    qb[...] = turned[channels]
    wp[...] = wide("wp", 0)[:, :channels]
    wkv[...] = jnp.concatenate(
        [wide("wkv", 0, channels)[:, :channels], wide("wkv", 0, channels, lt)[:, :channels]], -1
    )
    vb[...] = wide("wkv", channels, 16, lt)[1, :channels]
    at, rows, _ = splan["vec"]
    vec = jnp.concatenate([small[at + t * rows : at + (t + 1) * rows, :] for t in range(lt)], -1)
    vec = vec[:, :channels]
    for k, ref in enumerate((g2, b2, sb, rg, rbn, None, g1, b1, pb)):
        if ref is not None:
            ref[...] = vec[k]
    at, rows, _ = splan["count"]
    cm[...] = small[at : at + rows, :].astype(jnp.int32)[:CLASSES, :CLASSES]


def unpack(channels, ff, ndev, packed, small):
    one = (channels,)
    shapes = [
        one, one, (channels, channels), one, (channels, 4 * channels), one, one, one,
        (channels, 2 * channels), one, (channels, channels), one, one, one, (channels, ff), (ff,),
        (9, ff), (ff,), (channels, ff), one,
    ]
    outs = [jax.ShapeDtypeStruct(v, F32) for v in shapes]
    outs.append(jax.ShapeDtypeStruct((CLASSES, CLASSES), jnp.int32))
    return pl.pallas_call(
        functools.partial(unpack_kernel, channels, ff, ndev),
        out_shape=outs,
        compiler_params=pltpu.CompilerParams(vmem_limit_bytes=VMEM),
    )(packed, small)


NEG = np.float32(NEGATIVE * LOG2E)
NEG_HI = np.float32(ml_dtypes.bfloat16(NEG))
NEG_MID = np.float32(ml_dtypes.bfloat16(NEG - NEG_HI))
NEG_LO = np.float32(ml_dtypes.bfloat16(NEG - NEG_HI - NEG_MID))


def ext_row(values):
    lane = lanes((1, HEADS * LANE))
    row = jnp.zeros((1, HEADS * LANE), F32)
    for h in range(HEADS):
        for k, value in values.items():
            row = jnp.where(lane == h * LANE + ext_lane(h) + k, value, row)
    return row


def spread(value, cp):
    value = widen(value, cp)
    half = lanes((1, LANE)) // HALF
    blocks = []
    for h in range(HEADS):
        tile = value[:, (h // 2) * LANE : (h // 2 + 1) * LANE]
        blocks.append(jnp.where(half == h % 2, tile, jnp.zeros_like(tile)))
    return jnp.concatenate(blocks, -1)


def split_low(value):
    hi = value.astype(BF16).astype(F32)
    return hi, value - hi


def rows16(*rows):
    width = rows[0].shape[-1]
    at = lax.broadcasted_iota(jnp.int32, (16, width), 0)
    block = jnp.zeros((16, width), F32)
    for k, row in enumerate(rows):
        block = jnp.where(at == k, row, block)
    return block.astype(BF16)


def prep_kernel(
    channels, g1, b1, qw, qb, rw, rb, rg, rbn, kvw, vb, pw, pb, g2, b2, ew, eb, tb, sw, sb,
    vec, wq, wk, wv, wp, wpe, wkv, wr, we, ws, one, dbias, full,
):
    cp = up_to(channels, LANE)
    he = HEADS * LANE
    ff = ew.shape[1]
    head_size = channels // HEADS
    rest = cp - channels - 16

    def row(ref):
        return ref[...].reshape(1, ref.shape[-1])

    lane = lanes((1, cp))

    def padded(ref, *at):
        v = widen(row(ref), cp)
        for k in at:
            v = jnp.where(lane == channels + k, 1.0, v)
        return v

    for k, v in enumerate(
        (
            padded(g1), padded(b1, 0, 1), padded(rg), padded(rbn, 1, 2), padded(pb), padded(g2),
            padded(b2, 0, 1), padded(sb),
        )
    ):
        vec[k : k + 1, :] = v

    def fill(ref, top, *rows):
        width = ref.shape[-1]
        ref[:channels, :] = top
        ref[channels : channels + 16, :] = (
            rows16(*rows) if rows else jnp.zeros((16, width), BF16)
        )
        if rest:
            ref[channels + 16 :, :] = jnp.zeros((rest, width), BF16)

    ones = ext_row({0: 1.0, 1: 1.0, 2: 1.0})
    one[...] = ones
    dbias[...] = row(tb)
    qs = spread(qw[...], cp)
    qb_hi, qb_lo = split_low(row(qb))
    fill(wq, qs, spread(qb_hi, cp), spread(qb_lo, cp))
    kw = widen(kvw[:, :channels], cp)
    vw = widen(kvw[:, channels:], cp)
    ks = spread(kvw[:, :channels], cp)
    nil = jnp.zeros((1, he), F32)
    fill(
        wk, ks, ext_row({0: float(NEG_HI), 1: float(NEG_MID), 2: float(NEG_LO)}),
        ext_row({3: 1.0, 4: 1.0, 5: 1.0}),
    )
    vb_hi, vb_lo = split_low(row(vb))
    fill(wv, spread(kvw[:, channels:], cp), nil, spread(vb_hi, cp) + ones, spread(vb_lo, cp))
    p = widen(pw[...], cp)
    fill(wp, p)
    zero = jnp.zeros((HALF, cp), BF16)
    for h in range(HEADS):
        data, other = (0, HALF) if h % 2 == 0 else (HALF, 0)
        wpe[h * LANE + data : h * LANE + data + HALF, :] = p[h * HALF : (h + 1) * HALF]
        wpe[h * LANE + other : h * LANE + other + HALF, :] = zero
    fill(wkv, jnp.concatenate([kw, vw], -1))
    rb_rows = [widen(v, cp) for v in split_low(row(rb))]
    rw_rows = rw[...].T
    for ab in range(4):
        fill(
            wr.at[ab], widen(rw_rows[ab * channels : (ab + 1) * channels, :], cp),
            *rb_rows[ab : ab + 1],
        )
    fill(we, ew[...], *split_low(row(eb)))
    fill(ws, sw[...])

    def norm(v):
        return jnp.sqrt(jnp.sum(v * v, (0, 1), keepdims=True))

    root = channels**0.5

    def reach(gain, bias):
        top = jnp.max(jnp.abs(row(gain)), (0, 1), keepdims=True)
        return root * top + norm(row(bias))

    query_in, key_in = reach(g1, b1), reach(rg, rbn)
    qb_wide = spread(row(qb), cp)
    bound = jnp.zeros((1, 1), F32)
    for h in range(HEADS):
        cut = slice(h * LANE, (h + 1) * LANE)
        query = query_in * norm(qs[:, cut].astype(F32)) + norm(qb_wide[:, cut])
        key = key_in * norm(ks[:, cut].astype(F32))
        bound = jnp.maximum(bound, query * key)
    bound = bound * (head_size**-0.5 * 1.05)
    full[...] = jnp.where(2.0 * bound + 256.0 < -NEGATIVE, 0, 1).astype(jnp.int32)


def prep(channels, *weights):
    cp = up_to(channels, LANE)
    he = HEADS * LANE
    ff = weights[14].shape[1]
    shapes = [
        ((8, cp), F32), ((cp, he), BF16), ((cp, he), BF16), ((cp, he), BF16), ((cp, cp), BF16),
        ((he, cp), BF16), ((cp, 2 * cp), BF16), ((4, cp, cp), BF16), ((cp, ff), BF16),
        ((cp, ff), BF16), ((1, he), F32), ((1, ff), F32), ((1, 1), jnp.int32),
    ]
    return pl.pallas_call(
        functools.partial(prep_kernel, channels),
        out_shape=[jax.ShapeDtypeStruct(*v) for v in shapes],
        compiler_params=pltpu.CompilerParams(vmem_limit_bytes=VMEM),
    )(*weights)


def body(
    tokens, mask, labels, predicted, cotangent, norm1_gain, norm1_bias, query_weight, query_bias,
    reduce_weight, reduce_bias, rnorm_gain, rnorm_bias, kv_weight, value_bias, proj_weight,
    proj_bias, norm2_gain, norm2_bias, expand_weight, expand_bias, depth_weight, depth_bias,
    shrink_weight, shrink_bias,
):
    scenes, height, width, channels = tokens.shape
    ndp, blk = lax.axis_size("dp"), lax.axis_size("blk")
    n = height * width
    ff = expand_weight.shape[1]
    dims = (scenes, height, width, channels, up_to(channels, LANE))
    chips = blk // 2
    used = min(chips, -(-MASK_ROWS // (2 * height)))

    vec, wq, wk, wv, wp, wpe, wkv, wr, we, ws, ones, tap_bias, full = prep(
        channels, norm1_gain, norm1_bias, query_weight, query_bias, reduce_weight.T, reduce_bias,
        rnorm_gain, rnorm_bias, kv_weight, value_bias, proj_weight, proj_bias, norm2_gain,
        norm2_bias, expand_weight, expand_bias, depth_bias, shrink_weight.T, shrink_bias,
    )
    full = full[0, 0] > 0

    def either(call, cids, *operands):
        if used == chips:
            return call(dims, blk, chips, cids[1], *operands)
        return lax.cond(
            full,
            functools.partial(call, dims, blk, chips, cids[1]),
            functools.partial(call, dims, blk, used, cids[0]),
            *operands,
        )

    tok = tokens.reshape(scenes, n, channels)
    ct = cotangent.reshape(scenes, n, channels)
    red, counts, q, att, ke, ve, rn, res = either(
        attend, (2, 3), tok, mask, labels, predicted, vec, wr, wq, ones, wk, wv, wp
    )
    out, gres, dwe, dwst, dtap, dtb, dvec2 = ffn(
        dims, blk, res, ct, vec, we, ws, depth_weight, tap_bias
    )
    grn, gqt, dwp, dwkv, dbp = either(attback, (4, 5), q, att, gres, ke, ve, rn, wpe, wkv)
    ig, dwqt, dwrt, dvec1 = tail(dims, tok, gqt, gres, grn, red, vec, query_weight, wr)
    packed, small = reduce_all(
        channels, ff, ndp, blk, dwe, dwst, dwrt, dwkv, dwp, dwqt, dtap, dtb, dvec2, dvec1, dbp, counts
    )
    grads = list(unpack(channels, ff, ndp * blk, packed, small))
    grads[4], grads[18] = grads[4].T, grads[18].T
    return (out.reshape(tokens.shape), ig.reshape(tokens.shape), *grads)


def solution(mesh):
    banded = P("dp", "blk", None, None)
    plane = P("dp", "blk", None)
    in_specs = (banded, plane, plane, plane, banded) + (P(),) * 20
    out_specs = (banded, banded) + (P(),) * 21
    return jax.shard_map(body, mesh=mesh, in_specs=in_specs, out_specs=out_specs, check_vma=False)
```

time: 1270 us -> 404 us (0.32)
  waiting for transfers between devices: 399 us -> 0 us
  Pallas kernels: 0 us -> 384 us
  matrix products: 347 us -> 0 us
  other arithmetic: 296 us -> 0 us
  local copies, waits for them, and re-layouts: 167 us -> 3.97 us
  starting transfers between devices: 21.5 us -> 0 us
  blocking collectives: 15.5 us -> 0 us
  between operations: 15.4 us -> 1.91 us
    pallas_call x0 -> x7, Pallas kernels: none -> 384 us  [the longest x1 99.6 us: ffn(): pl.pallas_call(functools.partial(ffn_kernel, dims, ff, blk), in_specs=[vm...]
    dot_general x25 -> x0, matrix products: 347 us -> none  [the longest x1 65.2 us: body(): jnp.einsum('sqhd,skhd->shqk', grad_attended_heads, value_heads, preferred...]
    psum x2 -> x0, waiting for transfers between devices: 270 us -> none  [body(): lax.psum((norm1_gain_grad, norm1_bias_grad, query_weight_grad, query_bias...]
    convert_element_type x8 -> x0, other arithmetic: 157 us -> none  [the longest x1 79.1 us: body(): active_low = active.astype(jnp.bfloat16).reshape(number, hidden_width)]
    reduce_sum x14 -> x0, other arithmetic: 90.8 us -> none  [the longest x1 42.2 us: body(): expand_bias_grad = jnp.sum(grad_hidden_low.astype(jnp.float32), 0)]
    all_gather x1 -> x0, waiting for transfers between devices: 67.3 us -> none  [body(): lax.all_gather(keyval_rows, 'blk', axis=1, tiled=True)]
    reshape x8 -> x0, local copies, waits for them, and re-layouts: 61.4 us -> none  [the longest x2 16.9 us: body(): grad_patches.reshape(scenes, half_rows, half_cols, 2, 2, channels)]
    reduce_scatter x1 -> x0, waiting for transfers between devices: 58.6 us -> none  [body(): lax.psum_scatter(term.astype(jnp.bfloat16), 'blk', scatter_dimension=1, t...]
  transfers between devices with their start and end apart: 8 -> 0, of which waited for: 6 -> 0; matrix products, arithmetic and copies ran while one was open for 10% -> 0% of each run, Pallas kernels for 0% -> 0%
where the time goes in v1:
time: 404 us; the launch traced here: 398 us
  Pallas kernels  384 us (95%)
  loops' own time  8 us (2%)
    pallas_call x1, Pallas kernels, ffn(): pl.pallas_call(functools.partial(ffn_kernel, dims, ff, blk), in_specs=[vm...  99.6 us
    pallas_call x1, Pallas kernels, attback(): pl.pallas_call(functools.partial(attback_kernel, dims, blk, used), grid=(...  99.1 us
    pallas_call x1, Pallas kernels, attend(): pl.pallas_call(functools.partial(attend_kernel, dims, blk, used), grid=(s...  87.9 us
    pallas_call x1, Pallas kernels, reduce_all(): pl.pallas_call(functools.partial(reduce_kernel, channels, ff, ndp, nblk),...  68.6 us
    pallas_call x1, Pallas kernels, tail(): pl.pallas_call(functools.partial(tail_kernel, dims), grid=(scenes,), in_s...  18.7 us

profile of v1, /device:TPU:0, one launch (start us, length us, event | category | flops | bytes accessed | tf_op | source)
XLA Modules:
  0.0 397.9 jit_solution(6110969579606523423)
XLA Ops:
  0.7 0.0 copy-start.3
  0.7 0.0 copy-start.2
  0.7 0.0 copy-start.1
  0.7 4.9 %shard_map.416 = (f32[8,384]{1,0:T(8,128)S(1)}, bf16[384,640]{1,0:T(8,128)(2,1)}, bf16[384,640]{1,0:T(8,128)(2,1)}, bf16[384,640]{1,0:T(8,128)(2,1)}, bf16[384,3...) custom-call(f32[320]{0:T(512)} %g1.1, f32[320]{0:T(512)} %b1.1, ...), custom_call_target="tpu_custom_call" | custom-call | tf_op jit(solution)/shard_map/pallas_call | solution.py:1443
  6.2 0.0 copy-done.3
  6.3 0.0 copy-done.2
  6.3 0.0 copy-done.1
  6.3 88.1 %conditional.2 = ((f32[8,128,384]{2,1,0:T(8,128)}, f32[32,128]{1,0:T(8,128)S(1)}, bf16[8,512,640]{2,1,0:T(8,128)(2,1)}, f32[8,512,384]{2,1,0:T(8,128)}, bf16[8,1...) conditional(s32[]{:T(128)} %bitcast.2, ...), branch_computations={%region_0.0_spmd, %region_1.0_spmd} | conditional | bytes 8 | solution.py:1474
  6.5 87.9 %branch_1_fun.2 = (f32[8,128,384]{2,1,0:T(8,128)}, f32[32,128]{1,0:T(8,128)S(1)}, bf16[8,512,640]{2,1,0:T(8,128)(2,1)}, f32[8,512,384]{2,1,0:T(8,128)}, bf16[8,1...) custom-call(bf16[8,512,320]{2,1,0:T(8,128)(2,1)} %get-tuple-element., ...), custom_call_target="tpu_custom_call" | custom-call | tf_op jit(solution)/shard_map/cond/branch_1_fun/pallas_call | solution.py:319
  94.3 99.6 %shard_map.417 = (bf16[8,512,320]{2,1,0:T(8,128)(2,1)}, f32[8,512,320]{2,1,0:T(8,128)}, f32[384,1280]{1,0:T(8,128)}, f32[384,1280]{1,0:T(8,128)}, f32[9,1280]{1,...) custom-call(f32[3,4096,128]{2,1,0:T(8,128)} %get-tuple-element.205.res_ref, bf16[8,512,320]{2,1,0:T(8,128)(2,1)} %bitcast.13, ...), custom_call_target="tpu_custom_call" | custom-call | tf_op jit(solution)/shard_map/pallas_call | solution.py:663
  194.0 106.9 %conditional.3 = ((f32[8,128,384]{2,1,0:T(8,128)}, bf16[8,320,512]{2,1,0:T(8,128)(2,1)}, f32[384,384]{1,0:T(8,128)}, f32[384,768]{1,0:T(8,128)}, f32[8,384]{1,0:T(8,128)S(1)})) conditional(s32[]{:T(128)} %bitcast.2, (bf16[8,512,640]{2,1,0:T(8,128)(2,1)}, f32[8,512,384]{2,1,0:T(8,128)}, f32[8,512,320]{2,1,0:T(8,128)}, bf16[8,1024,640]{2,1,0:T(8,128)(2,1)}, ...), branch_computations={%region_2.0_spmd, %region_3.0_spmd} | conditional | bytes 8 | solution.py:1474
  201.5 99.1 %branch_1_fun.3 = (f32[8,128,384]{2,1,0:T(8,128)}, bf16[8,320,512]{2,1,0:T(8,128)(2,1)}, f32[384,384]{1,0:T(8,128)}, f32[384,768]{1,0:T(8,128)}, f32[8,384]{1,0:T(8,128)S(1)}) custom-call(bf16[8,512,640]{2,1,0:T(8,128)(2,1)} %get-tuple-element.106.q_ref, f32[8,512,384]{2,1,0:T(8,128)} %get-tuple-element.107.att_ref, ...), custom_call_target="tpu_custom_call" | custom-call | tf_op jit(solution)/shard_map/cond/branch_1_fun/pallas_call | solution.py:897
  300.9 0.0 copy-start
  300.9 18.7 %shard_map.418 = (f32[8,512,320]{2,1,0:T(8,128)}, f32[320,384]{1,0:T(8,128)}, f32[4,384,384]{2,1,0:T(8,128)}, f32[8,384]{1,0:T(8,128)}) custom-call(bf16[8,512,320]{2,1,0:T(8,128)(2,1)} %bitcast.11, bf16[8,320,512]{2,1,0:T(8,128)(2,1)} %get-tuple-element.218.gqt_ref, f32[8,512,320]{2,1,0:T(8,128)} %get-tuple-element.212.gres_ref, ...), custom_call_target="tpu_custom_call" | custom-call | tf_op jit(solution)/shard_map/pallas_call | solution.py:999
  319.6 0.0 copy-done
  319.6 68.6 %shard_map.419 = (bf16[14336,128]{1,0:T(8,128)(2,1)}, f32[256,128]{1,0:T(8,128)}) custom-call(f32[384,1280]{1,0:T(8,128)} %get-tuple-element.222.dwe, f32[384,1280]{1,0:T(8,128)} %get-tuple-element.223.dws, f32[4,384,384]{2,1,0:T(8,128)} %get-tuple-element.224.dwr, f32[384,768]{1,0:T(8,128)} %get-tuple-element.225.dwkv, f32[384,384]{1,0:T(8,128)S(1)} %copy-done, ...), custom_call_target="tpu_custom_call" | custom-call | tf_op jit(solution)/shard_map/pallas_call | solution.py:1216
  388.2 5.3 %shard_map.420 = (f32[320]{0:T(512)}, f32[320]{0:T(512)}, f32[320,320]{1,0:T(8,128)}, f32[320]{0:T(512)}, f32[320,1280]{1,0:T(8,128)}, /*index=5*/f32[320]{0:T(5...) custom-call(bf16[14336,128]{1,0:T(8,128)(2,1)} %get-tuple-element.23, ...), custom_call_target="tpu_custom_call" | custom-call | tf_op jit(solution)/shard_map/pallas_call | solution.py:1295
  393.5 4.0 copy.75
Async XLA Ops:
  0.7 5.6 %copy-start.3 = (s32[8,8,64]{2,1,0:T(8,128)S(1)}, s32[8,8,64]{2,1,0:T(8,128)}, u32[]{:S(2)}) copy-start(s32[8,8,64]{2,1,0:T(8,128)} %param.32) | copy-start | bytes 49156
  0.7 5.6 %copy-start.2 = (s32[8,8,64]{2,1,0:T(8,128)S(1)}, s32[8,8,64]{2,1,0:T(8,128)}, u32[]{:S(2)}) copy-start(s32[8,8,64]{2,1,0:T(8,128)} %param.31) | copy-start | bytes 49156
  0.7 5.6 %copy-start.1 = (s32[8,8,64]{2,1,0:T(8,128)S(1)}, s32[8,8,64]{2,1,0:T(8,128)}, u32[]{:S(2)}) copy-start(s32[8,8,64]{2,1,0:T(8,128)} %param.30) | copy-start | bytes 49156
  300.9 18.7 %copy-start = (f32[384,384]{1,0:T(8,128)S(1)}, f32[384,384]{1,0:T(8,128)}, u32[]{:S(2)}) copy-start(f32[384,384]{1,0:T(8,128)} %get-tuple-element.226.dwp) | copy-start | bytes 1769476

commit v2 on v1

--- a/solution.py
+++ b/solution.py
@@ -23,6 +23,7 @@
 MASK_ROWS = 48
 VMEM = 62 * 2**20
 FF_CHUNK = 256
+GROUP = 8
 
 
 def up_to(value, step):
@@ -106,6 +107,177 @@
         src_ref=src, dst_ref=dst, send_sem=send, recv_sem=recv, device_id=device,
         device_id_type=pl.DeviceIdType.MESH,
     )
+
+
+def groups_of(ndp, nblk):
+    dp_bits, blk_bits = ndp.bit_length() - 1, nblk.bit_length() - 1
+    assert ndp == 1 << dp_bits and nblk == 1 << blk_bits
+    core = [("blk", 0, 2)] if blk_bits else []
+    if dp_bits > 2:
+        plane = [("dp", 0, 1 << dp_bits // 2), ("dp", dp_bits // 2, 1 << (dp_bits - dp_bits // 2))]
+    else:
+        plane = [("dp", 0, ndp)] if dp_bits else []
+    line = [("blk", 1, nblk // 2)] if blk_bits > 1 else []
+    return core, plane, line
+
+
+def lay_out(items, ndev):
+    plan, at = {}, 0
+    for name, rows, slabs in items:
+        plan[name] = (at, rows, slabs)
+        at += rows * slabs
+    unit = 16 * ndev
+    units = -(-at // unit)
+    last = units // 3 - (1 if units > 6 else 0)
+    mid = (units - last) // 2
+    return plan, at, [(units - last - mid) * unit, mid * unit, last * unit]
+
+
+def ffn_plan(channels, ff, ndev):
+    tall = up_to(channels + 2, 16)
+    return lay_out([("we", tall, ff // LANE), ("ws", channels, ff // LANE)], ndev)
+
+
+def rest_plan(channels, ndev):
+    cp = up_to(channels, LANE)
+    tall = up_to(channels + 2, 16)
+    return lay_out(
+        [
+            ("wr", channels, 4 * cp // LANE), ("wkv", tall, 2 * cp // LANE),
+            ("wp", channels, cp // LANE), ("wq", channels, cp // LANE),
+        ],
+        ndev,
+    )
+
+
+def small_plan(channels, ff, ndev):
+    cp = up_to(channels, LANE)
+    plan = {"tap": (0, 16, ff // LANE)}
+    at = 16 * (ff // LANE)
+    plan["vec"] = (at, 16, cp // LANE)
+    at += 16 * (cp // LANE)
+    plan["count"] = (at, 32, 1)
+    at += 32
+    return plan, up_to(at, 8 * ndev)
+
+
+def member(group):
+    axis, bit, size = group
+    return lax.rem(lax.axis_index(axis) // (1 << bit), size)
+
+
+def other(group, index):
+    axis, bit, _ = group
+    return {axis: lax.axis_index(axis) + (index - member(group)) * (1 << bit)}
+
+
+def peers_of(order):
+    return [
+        other(group, lax.rem(member(group) + d, group[2])) for group in order for d in range(1, group[2])
+    ]
+
+
+class Sums:
+    def __init__(self, parts, send_sem, recv_sem):
+        self.parts, self.send_sem, self.recv_sem = parts, send_sem, recv_sem
+        self.rounds = len(parts[0][5])
+        self.ops = 2 * self.rounds
+
+    def unit(self, p):
+        return 16 if self.parts[p][0].dtype == BF16 else 8
+
+    def segment(self, p, i):
+        _, _, _, start, rows, order = self.parts[p]
+        for group in order[:i]:
+            rows //= group[2]
+            start = start + member(group) * rows
+        return start, rows
+
+    def landing(self, p, i):
+        _, _, _, first, rows, order = self.parts[p]
+        for group in order[:i]:
+            first += rows // group[2] * (group[2] - 1)
+            rows //= group[2]
+        return first
+
+    def copies(self, p, k):
+        buf, land, done, _, _, order = self.parts[p]
+        unit = self.unit(p)
+        halving = k < self.rounds
+        i = k if halving else self.ops - 1 - k
+        group = order[i]
+        size = group[2]
+        me = member(group)
+        result = []
+        for d in range(1, size):
+            to = lax.rem(me + d, size)
+            if halving:
+                start, rows = self.segment(p, i)
+                rows //= size
+                src = buf.at[pl.ds(pl.multiple_of(start + to * rows, unit), rows), :]
+                low = self.landing(p, i) + (size - 1 - d) * rows
+                dst = land.at[pl.ds(low, rows), :]
+            else:
+                start, rows = self.segment(p, i + 1)
+                src = done.at[pl.ds(pl.multiple_of(start, unit), rows), :]
+                dst = src
+            result.append(
+                remote(
+                    src, dst, self.send_sem.at[p, k, d - 1], self.recv_sem.at[p, k, d - 1],
+                    other(group, to),
+                )
+            )
+        return result
+
+    def start(self, p, k):
+        for copy in self.copies(p, k):
+            copy.start()
+
+    def finish(self, p, k):
+        for copy in self.copies(p, k):
+            copy.wait()
+        if k >= self.rounds:
+            return
+        buf, land, done, _, _, order = self.parts[p]
+        unit = self.unit(p)
+        keep, rows = self.segment(p, k + 1)
+        low = self.landing(p, k)
+        step = next(c for c in (256, 128, 64, 32, 16, 8) if rows % c == 0)
+        into = done if k == self.rounds - 1 else buf
+
+        @pl.loop(0, rows // step)
+        def _(j):
+            mine = pl.ds(pl.multiple_of(keep + j * step, unit), step)
+            total = buf[mine, :].astype(F32)
+            for d in range(order[k][2] - 1):
+                theirs = pl.ds(pl.multiple_of(low + d * rows + j * step, unit), step)
+                total = total + land[theirs, :].astype(F32)
+            into[mine, :] = total.astype(buf.dtype)
+
+    def advance(self, k):
+        for p in range(len(self.parts)):
+            if k > 0:
+                self.finish(p, k - 1)
+            if k < self.ops:
+                self.start(p, k)
+
+
+def three_parts(buf, land, done, sizes, orders):
+    parts, at = [], 0
+    for size, order in zip(sizes, orders):
+        if size:
+            parts.append((buf, land, done, at, size, order))
+        at += size
+    return parts
+
+
+def orders_of(ndp, nblk):
+    core, plane, line = groups_of(ndp, nblk)
+    return [core + plane + line, core + plane + line, core + line + plane]
+
+
+def widest(ndp, nblk):
+    return max(group[2] for group in orders_of(ndp, nblk)[0]) - 1
 
 
 def attend_kernel(
@@ -357,10 +529,10 @@
 
 
 def ffn_kernel(
-    dims, ff, blk, res_ref, ct_ref, vec_ref, we_ref, ws_ref, taps_ref, tb_ref,
-    out_hbm, gres_hbm, dwe_ref, dwst, dtap_ref, dtb_ref, dvec_ref,
-    cn, cnt, ctt, ctx, oacc, gacc, hid, gm, halo, tapacc, out_stage, gres_stage,
-    out_sem, gres_sem, cn_send, cn_recv, gm_send, gm_recv,
+    dims, ff, blk, ndev, res_hbm, ct_hbm, vec_ref, we_ref, ws_ref, taps_ref, tb_ref,
+    out_hbm, gres_hbm, pack_hbm, dtap_ref, dtb_ref, dvec_ref,
+    dwe_ref, dwst, packed, res_ref, ct_ref, cn, cnt, ctt, ctx, oacc, gacc, hid, gm, halo, act, back, tapacc, out_stage, gres_stage,
+    pack_sem, res_sem, ct_sem, out_sem, gres_sem, cn_send, cn_recv, gm_send, gm_recv,
 ):
     scenes, height, width, channels, cp = dims
     n = height * width
@@ -370,12 +542,25 @@
     nchunk = ff // fc
     cols = width // 2
     pair = 2 * scenes
+    group = GROUP if cols % GROUP == 0 else cols
     me = lax.axis_index("blk")
     has_left = me > 0
     has_right = me < blk - 1
     left, right = {"blk": me - 1}, {"blk": me + 1}
     MESH = pl.DeviceIdType.MESH
 
+    def res_copy(r):
+        rows = pl.ds(pl.multiple_of(r * rw, rw), rw)
+        return pltpu.make_async_copy(res_hbm.at[:, rows, :], res_ref.at[:, rows, :], res_sem.at[r])
+
+    def ct_copy(s):
+        return pltpu.make_async_copy(ct_hbm.at[s], ct_ref.at[s], ct_sem.at[s])
+
+    for r in range(height):
+        res_copy(r).start()
+    for s in range(scenes):
+        ct_copy(s).start()
+
     barrier = pltpu.get_barrier_semaphore()
 
     @pl.when(has_left)
@@ -402,12 +587,14 @@
 
     @pl.loop(0, height)
     def _(r):
+        res_copy(r).wait()
         x = load3(res_ref, r)
-        xhat, _ = centered(x, channels)
+        xhat, rstd = centered(x, channels)
         c = (xhat * g2 + b2).astype(BF16)
         cn[row(r + 1), :] = c
         cnt[:, row(r)] = c.T
         store3(oacc, r, x + vec_ref[7:8])
+        store3(res_ref, r, jnp.where(lanes(xhat.shape) == channels, rstd, xhat))
 
     def cn_copy(up):
         return pltpu.make_async_remote_copy(
@@ -429,6 +616,7 @@
 
     @pl.loop(0, scenes)
     def _(s):
+        ct_copy(s).wait()
         c = widen(ct_ref[s].astype(F32), cp)
         for t in range(lt):
             for r in range(height):
@@ -487,32 +675,55 @@
 
     def phase_a(k, slot):
         span = pl.ds(pl.multiple_of(k * fc, fc), fc)
-
-        @pl.loop(0, height + 2)
-        def _(r):
-            put(hid, slot, r, dot(cn[row(r), :], we_ref[:, span]))
-
-        @pl.loop(0, height)
-        def _(r):
-            acc = None
-            for a in range(3):
-                line = hid[slot, r + a]
-                for b in range(3):
-                    tap = taps_ref[pl.ds(3 * a + b, 1), span].astype(BF16).reshape(1, 1, fc)
-                    term = line[b : b + cols] * tap
-                    acc = term if acc is None else acc + term
-            mixed = acc.astype(F32).reshape(rw, fc) + tb_ref[:, span]
-            phi = 0.5 + 0.5 * lax.erf(mixed * 0.7071067811865476)
-            dens = jnp.exp2(mixed * mixed * (-0.5 * LOG2E)) * 0.3989422804014327
-            active = (mixed * phi).astype(BF16)
-            slope = phi + mixed * dens
-            grad = dot(ctt[row(r), :], ws_ref[:, span]) * slope
-            put(gm, slot, r + 1, grad)
-            dtb_ref[:, span] += jnp.sum(grad.reshape(rw // 8, 8, fc), 0)
+        taps = [
+            taps_ref[pl.ds(i, 1), span].astype(BF16).reshape(1, 1, fc) for i in range(9)
+        ]
+        bias = tb_ref[:, span]
+
+        def hidden(r):
+            put(hid, slot, r, dot(cn[r * rw : (r + 1) * rw, :], we_ref[:, span]))
+
+        def products(r):
+            active = act[r * rw : (r + 1) * rw, :]
             o = dot_nt(active, ws_ref[:, span])
             for t in range(lt):
-                oacc[t, row(r), :] += o[:, t * LANE : (t + 1) * LANE]
-            dwst[:, span] += dot(ctx[:, row(r)], active)
+                oacc[t, r * rw : (r + 1) * rw, :] += o[:, t * LANE : (t + 1) * LANE]
+            dwst[:, span] += dot(ctx[:, r * rw : (r + 1) * rw], active)
+
+        hidden(0)
+        hidden(1)
+        hidden(2)
+        sums = jnp.zeros((8, fc), F32)
+        for r in range(height):
+            if r + 3 < height + 2:
+                hidden(r + 3)
+            back[...] = dot(ctt[r * rw : (r + 1) * rw, :], ws_ref[:, span])
+            if r:
+                products(r - 1)
+            for g in range(0, cols, group):
+                acc = None
+                for a in range(3):
+                    line = hid[slot, r + a, g : g + group + 2]
+                    for b in range(3):
+                        term = line[b : b + group] * taps[3 * a + b]
+                        acc = term if acc is None else acc + term
+                mixed = acc.astype(F32).reshape(group * pair, fc) + bias
+                arg = mixed * 0.7071067811865476
+                phi = 0.5 + 0.5 * lax.erf(arg)
+                dens = jnp.exp2(arg * arg * -LOG2E) * mixed
+                act[r * rw + g * pair : r * rw + (g + group) * pair, :] = (mixed * phi).astype(BF16)
+                slope = phi + dens * 0.3989422804014327
+                grad = back[g * pair : (g + group) * pair, :] * slope
+                sums = sums + jnp.sum(grad.reshape(group * pair // 8, 8, fc), 0)
+                v = grad.reshape(group, pair, fc)
+                gm[slot, r + 1, g + 1 : g + group + 1] = v.astype(BF16)
+                z = jnp.zeros((scenes, fc), F32)
+                if g == 0:
+                    gm[slot, r + 1, cols + 1] = jnp.concatenate([v[0, scenes:], z], 0).astype(BF16)
+                if g + group == cols:
+                    gm[slot, r + 1, 0] = jnp.concatenate([z, v[group - 1, :scenes]], 0).astype(BF16)
+        products(height - 1)
+        dtb_ref[:, span] = sums
 
         @pl.when(has_left)
         def _():
@@ -543,28 +754,41 @@
         def _():
             gm[slot, height + 1] = jnp.zeros((cols + 2, pair, fc), BF16)
 
+        taps = [
+            taps_ref[pl.ds(i, 1), span].astype(BF16).reshape(1, 1, fc) for i in range(9)
+        ]
         tapacc[...] = jnp.zeros(tapacc.shape, F32)
 
-        @pl.loop(0, height)
-        def _(r):
-            acc = None
-            own = hid[slot, r + 1, 1 : cols + 1]
-            for a in range(3):
-                line = gm[slot, r + 2 - a]
-                for b in range(3):
-                    tap = taps_ref[pl.ds(3 * a + b, 1), span].astype(BF16).reshape(1, 1, fc)
-                    window = line[2 - b : 2 - b + cols]
-                    term = window * tap
-                    acc = term if acc is None else acc + term
-                    prod = own * window
-                    q = cols // 4
-                    prod = (prod[:q] + prod[q : 2 * q]) + (prod[2 * q : 3 * q] + prod[3 * q :])
-                    tapacc[3 * a + b] += jnp.sum(prod.astype(F32), 0)
-            low = acc.reshape(rw, fc)
-            dwe_ref[:, span] += dot(cnt[:, row(r)], low)
+        def products(r):
+            low = act[r * rw : (r + 1) * rw, :]
+            dwe_ref[:, span] += dot(cnt[:, r * rw : (r + 1) * rw], low)
             g = dot_nt(low, we_ref[:, span])
             for t in range(lt):
-                gacc[t, row(r), :] += g[:, t * LANE : (t + 1) * LANE]
+                gacc[t, r * rw : (r + 1) * rw, :] += g[:, t * LANE : (t + 1) * LANE]
+
+        for r in range(height):
+            if r:
+                products(r - 1)
+            tapsum = [None] * 9
+            for g in range(0, cols, group):
+                acc = None
+                own = hid[slot, r + 1, g + 1 : g + group + 1]
+                for a in range(3):
+                    line = gm[slot, r + 2 - a, g : g + group + 2]
+                    for b in range(3):
+                        window = line[2 - b : 2 - b + group]
+                        term = window * taps[3 * a + b]
+                        acc = term if acc is None else acc + term
+                        prod = own * window
+                        while prod.shape[0] > 1:
+                            cut = prod.shape[0] // 2
+                            prod = prod[:cut] + prod[cut:]
+                        i = 3 * a + b
+                        tapsum[i] = prod[0] if tapsum[i] is None else tapsum[i] + prod[0]
+                act[r * rw + g * pair : r * rw + (g + group) * pair, :] = acc.reshape(group * pair, fc)
+            for i in range(9):
+                tapacc[i] += tapsum[i].astype(F32)
+        products(height - 1)
 
         for tap in range(9):
             dtap_ref[pl.ds(tap, 1), span] = jnp.sum(tapacc[tap], 0, keepdims=True)
@@ -577,8 +801,6 @@
         def _():
             gm_copy(k, slot, False).wait_send()
 
-    dtb_ref[...] = jnp.zeros(dtb_ref.shape, F32)
-
     @pl.loop(0, nchunk + 1)
     def _(k):
         slot = lax.rem(k, 2)
@@ -599,15 +821,17 @@
     def _():
         cn_copy(False).wait_send()
 
-    @pl.loop(0, height)
-    def _(r):
-        x = load3(res_ref, r)
-        xhat, rstd = centered(x, channels)
-        upstream = load3(gacc, r)
-        dvec_ref[0:1] += jnp.sum(upstream * xhat, 0, keepdims=True)
-        dvec_ref[1:2] += jnp.sum(upstream, 0, keepdims=True)
-        g = ctt[row(r), :].astype(F32) + norm_back(upstream, g2, xhat, rstd, channels)
-        store3(gacc, r, g)
+    plan, filled, _ = ffn_plan(channels, ff, ndev)
+    for name, ref in (("we", dwe_ref), ("ws", dwst)):
+        at, rows, slabs = plan[name]
+        for t in range(slabs):
+            packed[at + t * rows : at + (t + 1) * rows, :] = ref[
+                :rows, t * LANE : (t + 1) * LANE
+            ].astype(BF16)
+    if filled < packed.shape[0]:
+        packed[filled:, :] = jnp.zeros((packed.shape[0] - filled, LANE), BF16)
+    pack_copy = pltpu.make_async_copy(packed, pack_hbm, pack_sem.at[0])
+    pack_copy.start()
 
     def gather(ref, s):
         rows = []
@@ -637,19 +861,39 @@
         @pl.when(s >= 2)
         def _():
             out_copy(s - 2, slot).wait()
+
+        out_stage[slot] = gather(oacc, s).astype(BF16)
+        out_copy(s, slot).start()
+
+    @pl.loop(0, height)
+    def _(r):
+        kept = load3(res_ref, r)
+        rstd = kept[:, channels : channels + 1]
+        xhat = jnp.where(lanes(kept.shape) < channels, kept, 0.0)
+        upstream = load3(gacc, r)
+        dvec_ref[0:1] += jnp.sum(upstream * xhat, 0, keepdims=True)
+        dvec_ref[1:2] += jnp.sum(upstream, 0, keepdims=True)
+        g = ctt[row(r), :].astype(F32) + norm_back(upstream, g2, xhat, rstd, channels)
+        store3(gacc, r, g)
+
+    @pl.loop(0, scenes)
+    def _(s):
+        slot = lax.rem(s, 2)
+
+        @pl.when(s >= 2)
+        def _():
             gres_copy(s - 2, slot).wait()
 
-        out_stage[slot] = gather(oacc, s).astype(BF16)
         gres_stage[slot] = gather(gacc, s)
-        out_copy(s, slot).start()
         gres_copy(s, slot).start()
 
     for s in range(scenes - 2, scenes):
         out_copy(s, s % 2).wait()
         gres_copy(s, s % 2).wait()
-
-
-def ffn(dims, blk, res, ct, vec, we, ws, taps, tb):
+    pack_copy.wait()
+
+
+def ffn(dims, blk, ndev, res, ct, vec, we, ws, taps, tb):
     scenes, height, width, channels, cp = dims
     n = height * width
     total = scenes * n
@@ -658,22 +902,27 @@
     lt = cp // LANE
     nchunk = ff // FF_CHUNK
     strip = (width // 2 + 2, 2 * scenes, FF_CHUNK)
+    pack_rows = sum(ffn_plan(channels, ff, ndev)[2])
     vm = pl.BlockSpec(memory_space=pltpu.VMEM)
     hbm = pl.BlockSpec(memory_space=pl.ANY)
     return pl.pallas_call(
-        functools.partial(ffn_kernel, dims, ff, blk),
-        in_specs=[vm] * 7,
-        out_specs=[hbm, hbm] + [vm] * 5,
+        functools.partial(ffn_kernel, dims, ff, blk, ndev),
+        in_specs=[hbm, hbm] + [vm] * 5,
+        out_specs=[hbm, hbm, hbm] + [vm] * 3,
         out_shape=[
             jax.ShapeDtypeStruct((scenes, n, channels), BF16),
             jax.ShapeDtypeStruct((scenes, n, channels), F32),
-            jax.ShapeDtypeStruct((cp, ff), F32),
-            jax.ShapeDtypeStruct((cp, ff), F32),
+            jax.ShapeDtypeStruct((pack_rows, LANE), BF16),
             jax.ShapeDtypeStruct((9, ff), F32),
             jax.ShapeDtypeStruct((8, ff), F32),
             jax.ShapeDtypeStruct((8, cp), F32),
         ],
         scratch_shapes=[
+            pltpu.VMEM((cp, ff), F32),
+            pltpu.VMEM((cp, ff), F32),
+            pltpu.VMEM((pack_rows, LANE), BF16),
+            pltpu.VMEM((lt, total, LANE), F32),
+            pltpu.VMEM((scenes, n, channels), BF16),
             pltpu.VMEM((total + 2 * rw, cp), BF16),
             pltpu.VMEM((cp, total), BF16),
             pltpu.VMEM((total, cp), BF16),
@@ -683,9 +932,14 @@
             pltpu.VMEM((2, height + 2) + strip, BF16),
             pltpu.VMEM((2, height + 2) + strip, BF16),
             pltpu.VMEM((nchunk, 2) + strip, BF16),
+            pltpu.VMEM((total, FF_CHUNK), BF16),
+            pltpu.VMEM((rw, FF_CHUNK), F32),
             pltpu.VMEM((9, 2 * scenes, FF_CHUNK), F32),
             pltpu.VMEM((2, n, channels), BF16),
             pltpu.VMEM((2, n, channels), F32),
+            pltpu.SemaphoreType.DMA((1,)),
+            pltpu.SemaphoreType.DMA((height,)),
+            pltpu.SemaphoreType.DMA((scenes,)),
             pltpu.SemaphoreType.DMA((2,)),
             pltpu.SemaphoreType.DMA((2,)),
             pltpu.SemaphoreType.DMA((2,)),
@@ -700,10 +954,12 @@
 
 
 def attback_kernel(
-    dims, blk, used, q_ref, att_ref, gres_ref, ke_ref, ve_ref, rn_ref, wpe_ref, wkv_ref,
-    grn_ref, gqt_ref, dwp_ref, dwkv_ref, dbp_ref,
-    ge, dqt, own, acc, sib_land, up_land, down_land,
-    sib_send, sib_recv, up_send, up_recv, down_send, down_recv,
+    dims, ff, ndp, blk, used, q_ref, att_ref, gres_ref, ke_ref, ve_ref, rn_ref, tok_ref, gres2_ref,
+    red_ref, vec_ref, wpe_ref, wkv_ref, wq_ref, wr_ref, first_hbm,
+    ig_ref, dwqt, dwrt, dwp_ref, dwkv_ref, dbp_ref, dvec_ref, sum_hbm,
+    ge, dqt, gqt_ref, grn_ref, scr, gscr, own, acc, sib_land, up_land, down_land,
+    work, land, done,
+    sib_send, sib_recv, up_send, up_recv, down_send, down_recv, sum_send, sum_recv, sum_sem,
 ):
     scenes, height, width, channels, cp = dims
     n = height * width
@@ -714,17 +970,37 @@
     step = pl.program_id(0)
     chip, core, up, down, sib = place(blk)
     count = 2 * used * keys // KEY_CHUNK
+    steps = scenes + chips
+    together = -(-scenes // chips)
+    ndev = ndp * blk
+    order = orders_of(ndp, blk)[0]
+    parts = three_parts(work, land, done, ffn_plan(channels, ff, ndev)[2], [order] * 3)
+    sums = Sums(parts, sum_send, sum_recv)
+    each = -(-(sums.ops + 1) // (steps - 1))
 
     @pl.when(step == 0)
     def _():
-        greet(chip, chips, up, down, sib)
+        load = pltpu.make_async_copy(first_hbm, work, sum_sem.at[0])
+        load.start()
+        barrier = pltpu.get_barrier_semaphore()
+        peers = peers_of(order)
+        for peer in peers:
+            pl.semaphore_signal(barrier, inc=1, device_id=peer, device_id_type=pl.DeviceIdType.MESH)
+        pl.semaphore_wait(barrier, len(peers))
+        load.wait()
+        for k in range(each):
+            sums.advance(k)
+        dwqt[...] = jnp.zeros(dwqt.shape, F32)
+        dwrt[...] = jnp.zeros(dwrt.shape, F32)
+        dvec_ref[...] = jnp.zeros(dvec_ref.shape, F32)
         dwp_ref[...] = jnp.zeros(dwp_ref.shape, F32)
         dwkv_ref[...] = jnp.zeros(dwkv_ref.shape, F32)
         dbp_ref[...] = jnp.zeros(dbp_ref.shape, F32)
 
-    def to_sib(s):
+    def to_sib(s, target):
         return remote(
-            own.at[lax.rem(s, 2), 1 - core], sib_land.at[s], sib_send.at[s], sib_recv.at[s], sib
+            own.at[lax.rem(s, 2), 1 - core, target], sib_land.at[s, target], sib_send.at[s, target],
+            sib_recv.at[s, target], sib,
         )
 
     def to_up(s, target):
@@ -768,6 +1044,11 @@
         for i in range(per):
             at = j * per + i
             own[lax.rem(s, 2), at // used, at % used] = grn[i * keys : (i + 1) * keys]
+
+            @pl.when(core != at // used)
+            def _(at=at):
+                to_sib(s, at % used).start()
+
         dwkv_ref[...] += dot(rn_ref[0, span].T, gkv)
 
     @pl.when(step < scenes)
@@ -795,14 +1076,15 @@
 
     @pl.when(jnp.logical_and(s1 >= 0, s1 < scenes))
     def _():
-        to_sib(s1).wait()
-        acc[s1] = plus(own[lax.rem(s1, 2), core], sib_land[s1])
+        for target in range(used):
+            to_sib(s1, target).wait()
+            acc[s1, target] = plus(own[lax.rem(s1, 2), core, target], sib_land[s1, target])
 
     s_up = step - 1 - chip
 
     @pl.when(jnp.logical_and(s_up >= 0, s_up < scenes))
     def _():
-        for target in range(1, used):
+        for target in reversed(range(1, used)):
 
             @pl.when(target > chip)
             def _(target=target):
@@ -834,36 +1116,87 @@
     def _():
         @pl.when(chip < used)
         def _():
-            grn_ref[0] = acc[s_end, chip].astype(F32)
+            grn_ref[s_end] = acc[s_end, chip].astype(F32)
 
             @pl.when(chip > 0)
             def _():
                 to_up(s_end, chip).wait_recv()
-                grn_ref[0] += up_land[s_end, chip].astype(F32)
+                grn_ref[s_end] += up_land[s_end, chip].astype(F32)
 
             @pl.when(chip < chips - 1)
             def _():
                 to_down(s_end, chip).wait_recv()
-                grn_ref[0] += down_land[s_end, chip].astype(F32)
+                grn_ref[s_end] += down_land[s_end, chip].astype(F32)
 
         @pl.when(chip >= used)
         def _():
-            grn_ref[0] = jnp.zeros((keys, cp), F32)
+            grn_ref[s_end] = jnp.zeros((keys, cp), F32)
+
+    for t in range(1, steps - 1):
+
+        @pl.when(step == t)
+        def _(t=t):
+            for k in range(t * each, min((t + 1) * each, sums.ops + 1)):
+                sums.advance(k)
+            if t * each <= sums.ops < (t + 1) * each:
+                pltpu.make_async_copy(done, sum_hbm, sum_sem.at[0]).start()
+
+    def tail(i, s):
+        rhat, rstd = centered(red_ref[i], channels)
+        inside = lanes((keys, cp)) < channels
+        upstream = jnp.where(inside, grn_ref[s], 0.0)
+        dvec_ref[0:1] += jnp.sum(upstream * rhat, 0, keepdims=True)
+        dvec_ref[1:2] += jnp.sum(upstream, 0, keepdims=True)
+        gred = norm_back(upstream, vec_ref[2:3], rhat, rstd, channels)
+        gred = jnp.where(inside, gred, 0.0).astype(BF16)
+        gred_t = gred.T
+        x = widen(tok_ref[i].astype(F32), cp)
+        xhat, xstd = centered(x, channels)
+        low = (xhat * vec_ref[0:1] + vec_ref[1:2]).astype(BF16)
+        lowf = low.astype(F32)
+        for t in range(lt):
+            scr[i, t] = lowf[:, t * LANE : (t + 1) * LANE]
+        for b in range(2):
+            part = [scr[i, t, pl.ds(b, n // 2, stride=2), :] for t in range(lt)]
+            part = jnp.concatenate(part, -1).reshape(height // 2, 2, width // 2, cp)
+            for a in range(2):
+                ab = 2 * a + b
+                dwrt[ab] += dot(gred_t, part[:, a].reshape(keys, cp).astype(BF16))
+                back = dot_nt(gred, wr_ref[ab])
+                for t in range(lt):
+                    for r in range(height // 2):
+                        gscr[i, t, pl.ds((2 * r + a) * width + b, width // 2, stride=2), :] = back[
+                            r * (width // 2) : (r + 1) * (width // 2), t * LANE : (t + 1) * LANE
+                        ]
+        gqt = gqt_ref[s]
+        dwqt[...] += dot(gqt, low)
+        gn = widen(dot_nt(gqt.T, wq_ref[...]), cp)
+        gn = gn + jnp.concatenate([gscr[i, t] for t in range(lt)], -1)
+        dvec_ref[3:4] += jnp.sum(gn * xhat, 0, keepdims=True)
+        dvec_ref[4:5] += jnp.sum(gn, 0, keepdims=True)
+        gx = norm_back(gn, vec_ref[0:1], xhat, xstd, channels)
+        ig_ref[i] = gres2_ref[i] + gx[:, :channels]
+
+    @pl.when(step >= scenes)
+    def _():
+        for i in range(together):
+            tail(i, (step - scenes) * together + i)
 
     @pl.when(step < scenes)
     def _():
         s = step
         for j in range(1, count):
             chunk(j)
-        to_sib(s).start()
         for h in range(HEADS):
             base = h * LANE + (0 if h % 2 == 0 else HALF)
-            gqt_ref[0, h * HALF : (h + 1) * HALF] = (
+            gqt_ref[s, h * HALF : (h + 1) * HALF] = (
                 dqt[base : base + HALF, :] * head_size**-0.5
             ).astype(BF16)
 
-    @pl.when(step == scenes + chips - 1)
-    def _():
+    @pl.when(step == steps - 1)
+    def _():
+        pltpu.make_async_copy(done, sum_hbm, sum_sem.at[0]).wait()
+
         @pl.loop(0, scenes)
         def _(s):
             for target in range(used):
@@ -877,13 +1210,19 @@
                     to_down(s, target).wait_send()
 
 
-def attback(dims, blk, used, cid, q, att, gres, ke, ve, rn, wpe, wkv):
+def attback(
+    dims, ff, ndp, blk, used, cid, q, att, gres, ke, ve, rn, tok, red, vec, wpe, wkv, wq, wr, first
+):
     scenes, height, width, channels, cp = dims
     n = height * width
     keys = n // 4
     chips = blk // 2
+    lt = cp // LANE
     live = 2 * used * keys
     he = HEADS * LANE
+    together = -(-scenes // chips)
+    assert scenes == together * chips
+    ops = 2 * len(orders_of(ndp, blk)[0])
 
     def early(shape):
         return pl.BlockSpec(
@@ -891,11 +1230,15 @@
         )
 
     def late(shape):
-        return pl.BlockSpec((1,) + shape, lambda t: (jnp.maximum(t - chips, 0),) + (0,) * len(shape))
+        return pl.BlockSpec(
+            (together,) + shape, lambda t: (jnp.maximum(t - scenes, 0),) + (0,) * len(shape)
+        )
 
     land = (scenes, used, keys, cp)
+    hbm = pl.BlockSpec(memory_space=pl.ANY)
+    vm = pl.BlockSpec(memory_space=pltpu.VMEM)
     return pl.pallas_call(
-        functools.partial(attback_kernel, dims, blk, used),
+        functools.partial(attback_kernel, dims, ff, ndp, blk, used),
         grid=(scenes + chips,),
         in_specs=[
             early((n, he)),
@@ -904,194 +1247,57 @@
             early((live, he)),
             early((live, he)),
             early((live, cp)),
-            whole(wpe.shape),
-            whole(wkv.shape),
+            late((n, channels)),
+            late((n, channels)),
+            late((keys, cp)),
+            vm, vm, vm, vm, vm, hbm,
         ],
-        out_specs=[
-            late((keys, cp)),
-            early((channels, n)),
-            whole((cp, cp)),
-            whole((cp, 2 * cp)),
-            whole((8, cp)),
-        ],
+        out_specs=[late((n, channels))] + [vm] * 6 + [hbm],
         out_shape=[
-            jax.ShapeDtypeStruct((scenes, keys, cp), F32),
-            jax.ShapeDtypeStruct((scenes, channels, n), BF16),
+            jax.ShapeDtypeStruct((scenes, n, channels), F32),
+            jax.ShapeDtypeStruct((channels, cp), F32),
+            jax.ShapeDtypeStruct((4, cp, cp), F32),
             jax.ShapeDtypeStruct((cp, cp), F32),
             jax.ShapeDtypeStruct((cp, 2 * cp), F32),
             jax.ShapeDtypeStruct((8, cp), F32),
+            jax.ShapeDtypeStruct((8, cp), F32),
+            jax.ShapeDtypeStruct(first.shape, BF16),
         ],
         scratch_shapes=[
             pltpu.VMEM((n, he), BF16),
             pltpu.VMEM((he, n), F32),
+            pltpu.VMEM((scenes, channels, n), BF16),
+            pltpu.VMEM((scenes, keys, cp), F32),
+            pltpu.VMEM((together, lt, n, LANE), F32),
+            pltpu.VMEM((together, lt, n, LANE), F32),
             pltpu.VMEM((2, 2, used, keys, cp), BF16),
-            pltpu.VMEM(land, BF16),
-            pltpu.VMEM(land, BF16),
-            pltpu.VMEM(land, BF16),
-            pltpu.VMEM(land, BF16),
-            pltpu.SemaphoreType.DMA((scenes,)),
-            pltpu.SemaphoreType.DMA((scenes,)),
         ]
-        + [pltpu.SemaphoreType.DMA((scenes, used))] * 4,
+        + [pltpu.VMEM(land, BF16)] * 4
+        + [pltpu.VMEM(first.shape, BF16)] * 3
+        + [pltpu.SemaphoreType.DMA((scenes, used))] * 6
+        + [pltpu.SemaphoreType.DMA((3, ops, widest(ndp, blk)))] * 2
+        + [pltpu.SemaphoreType.DMA((1,))],
         compiler_params=pltpu.CompilerParams(
             vmem_limit_bytes=VMEM, collective_id=cid, has_side_effects=True
         ),
-    )(q, att, gres, ke, ve, rn, wpe, wkv)
-
-
-def tail_kernel(
-    dims, tok_ref, gqt_ref, gres_ref, grn_ref, red_ref, vec_ref, wq_ref, wr_ref,
-    ig_ref, dwqt, dwrt, dvec_ref, scr, gscr,
-):
-    scenes, height, width, channels, cp = dims
-    n = height * width
-    keys = n // 4
-    lt = cp // LANE
-    s_id = pl.program_id(0)
-
-    @pl.when(s_id == 0)
-    def _():
-        dwqt[...] = jnp.zeros(dwqt.shape, F32)
-        dwrt[...] = jnp.zeros(dwrt.shape, F32)
-        dvec_ref[...] = jnp.zeros(dvec_ref.shape, F32)
-
-    rhat, rstd = centered(red_ref[0], channels)
-    up = grn_ref[0].astype(F32)
-    dvec_ref[0:1] += jnp.sum(up * rhat, 0, keepdims=True)
-    dvec_ref[1:2] += jnp.sum(up, 0, keepdims=True)
-    gred = norm_back(jnp.where(lanes(up.shape) < channels, up, 0.0), vec_ref[2:3], rhat, rstd, channels)
-    gred = jnp.where(lanes(up.shape) < channels, gred, 0.0).astype(BF16)
-    dvec_ref[2:3] += jnp.sum(gred.astype(F32), 0, keepdims=True)
-    gred_t = gred.T
-
-    x = widen(tok_ref[0].astype(F32), cp)
-    xhat, xstd = centered(x, channels)
-    low = (xhat * vec_ref[0:1] + vec_ref[1:2]).astype(BF16)
-    lowf = low.astype(F32)
-    for t in range(lt):
-        scr[t] = lowf[:, t * LANE : (t + 1) * LANE]
-    for b in range(2):
-        part = [scr[t, pl.ds(b, n // 2, stride=2), :] for t in range(lt)]
-        part = jnp.concatenate(part, -1).reshape(height // 2, 2, width // 2, cp)
-        for a in range(2):
-            ab = 2 * a + b
-            dwrt[ab] += dot(gred_t, part[:, a].reshape(keys, cp).astype(BF16))
-            back = dot_nt(gred, wr_ref[ab])
-            for t in range(lt):
-                for i in range(height // 2):
-                    gscr[t, pl.ds((2 * i + a) * width + b, width // 2, stride=2), :] = back[
-                        i * (width // 2) : (i + 1) * (width // 2), t * LANE : (t + 1) * LANE
-                    ]
-    gqt = gqt_ref[0]
-    dwqt[...] += dot(gqt, low)
-    gn = widen(dot_nt(gqt.T, wq_ref[...]), cp) + jnp.concatenate([gscr[t] for t in range(lt)], -1)
-    dvec_ref[3:4] += jnp.sum(gn * xhat, 0, keepdims=True)
-    dvec_ref[4:5] += jnp.sum(gn, 0, keepdims=True)
-    gx = norm_back(gn, vec_ref[0:1], xhat, xstd, channels)
-    ig_ref[0] = gres_ref[0] + gx[:, :channels]
-
-
-def tail(dims, tok, gqt, gres, grn, red, vec, wqt, wr):
-    scenes, height, width, channels, cp = dims
-    n = height * width
-    keys = n // 4
-    lt = cp // LANE
-    return pl.pallas_call(
-        functools.partial(tail_kernel, dims),
-        grid=(scenes,),
-        in_specs=[
-            per_scene((n, channels)),
-            per_scene((channels, n)),
-            per_scene((n, channels)),
-            per_scene((keys, cp)),
-            per_scene((keys, cp)),
-            whole(vec.shape),
-            whole(wqt.shape),
-            whole(wr.shape),
-        ],
-        out_specs=[
-            per_scene((n, channels)),
-            whole((channels, cp)),
-            whole((4, cp, cp)),
-            whole((8, cp)),
-        ],
-        out_shape=[
-            jax.ShapeDtypeStruct((scenes, n, channels), F32),
-            jax.ShapeDtypeStruct((channels, cp), F32),
-            jax.ShapeDtypeStruct((4, cp, cp), F32),
-            jax.ShapeDtypeStruct((8, cp), F32),
-        ],
-        scratch_shapes=[
-            pltpu.VMEM((lt, n, LANE), F32),
-            pltpu.VMEM((lt, n, LANE), F32),
-        ],
-        compiler_params=pltpu.CompilerParams(vmem_limit_bytes=VMEM),
-    )(tok, gqt, gres, grn, red, vec, wqt, wr)
-
-
-def bit_orders(ndp, nblk):
-    dp_bits, blk_bits = ndp.bit_length() - 1, nblk.bit_length() - 1
-    assert ndp == 1 << dp_bits and nblk == 1 << blk_bits
-    core = [("blk", 0)] if blk_bits else []
-    xs = [("dp", b) for b in range(dp_bits // 2)]
-    ys = [("dp", b) for b in range(dp_bits // 2, dp_bits)]
-    zs = [("blk", b) for b in range(1, blk_bits)]
-    return [core + xs + ys + zs, core + ys + zs + xs, core + zs + xs + ys]
-
-
-def pack_plan(channels, ff, ndev):
-    cp = up_to(channels, LANE)
-    tall = up_to(channels + 2, 16)
-    items = [
-        ("we", tall, ff // LANE), ("ws", channels, ff // LANE), ("wr", channels, 4 * cp // LANE),
-        ("wkv", tall, 2 * cp // LANE), ("wp", channels, cp // LANE), ("wq", channels, cp // LANE),
-    ]
-    plan, at = {}, 0
-    for name, rows, slabs in items:
-        plan[name] = (at, rows, slabs)
-        at += rows * slabs
-    unit = 16 * ndev
-    units = -(-at // unit)
-    last = units // 3 - (1 if units > 6 else 0)
-    mid = (units - last) // 2
-    sizes = [(units - last - mid) * unit, mid * unit, last * unit]
-    return plan, at, sizes
-
-
-def small_plan(channels, ff, ndev):
-    cp = up_to(channels, LANE)
-    plan = {"tap": (0, 16, ff // LANE)}
-    at = 16 * (ff // LANE)
-    plan["vec"] = (at, 16, cp // LANE)
-    at += 16 * (cp // LANE)
-    plan["count"] = (at, 32, 1)
-    at += 32
-    return plan, up_to(at, 8 * ndev)
+    )(q, att, gres, ke, ve, rn, tok, gres, red, vec, wpe, wkv, wq, wr, first)
 
 
 def reduce_kernel(
-    channels, ff, ndp, nblk, dwe, dws, dwr, dwkv, dwp, dwq, dtap, dtb, dvec2, dvec1, dbp, cnt,
+    channels, ff, ndp, nblk, dwr, dwkv, dwp, dwq, dtap, dtb, dvec2, dvec1, dbp, cnt,
     out_hbm, small_hbm, work, recv, done, swork, srecv, sdone, send_sem, recv_sem, out_sem,
 ):
     ndev = ndp * nblk
     cp = up_to(channels, LANE)
-    orders = bit_orders(ndp, nblk)
-    rounds = len(orders[0])
-    plan, used, sizes = pack_plan(channels, ff, ndev)
+    orders = orders_of(ndp, nblk)
+    plan, used, sizes = rest_plan(channels, ndev)
     splan, srows = small_plan(channels, ff, ndev)
-    MESH = pl.DeviceIdType.MESH
-    index = {"dp": lax.axis_index("dp"), "blk": lax.axis_index("blk")}
-
-    def partner(axis, bit):
-        step = 1 << bit
-        value = lax.rem(index[axis] // step, 2)
-        return value, {axis: index[axis] + (1 - 2 * value) * step}
-
     barrier = pltpu.get_barrier_semaphore()
-    for axis, bit in orders[0]:
-        pl.semaphore_signal(barrier, inc=1, device_id=partner(axis, bit)[1], device_id_type=MESH)
-
-    def put(name, ref, rows_from=None):
+    peers = peers_of(orders[0])
+    for peer in peers:
+        pl.semaphore_signal(barrier, inc=1, device_id=peer, device_id_type=pl.DeviceIdType.MESH)
+
+    def put(name, ref):
         at, rows, slabs = plan[name]
         for t in range(slabs):
             work[at + t * rows : at + (t + 1) * rows, :] = ref(t, rows).astype(BF16)
@@ -1099,8 +1305,6 @@
     def lane_slabs(ref):
         return lambda t, rows: ref[:rows, t * LANE : (t + 1) * LANE]
 
-    put("we", lane_slabs(dwe))
-    put("ws", lane_slabs(dws))
     per = cp // LANE
     put("wr", lambda t, rows: dwr[t // per, :rows, (t % per) * LANE : (t % per + 1) * LANE])
     put("wkv", lane_slabs(dwkv))
@@ -1125,77 +1329,12 @@
     at, rows, _ = splan["count"]
     swork[at : at + rows, :] = cnt[...]
 
-    pl.semaphore_wait(barrier, rounds)
-
-    parts, at = [], 0
-    for size, order in zip(sizes, orders):
-        if size:
-            parts.append([work, recv, at, size, order])
-        at += size
-    parts.append([swork, srecv, 0, srows, orders[0]])
-
-    state = [(first, size) for _, _, first, size, _ in parts]
-    landing = [first for _, _, first, _, _ in parts]
-    for i in range(rounds):
-        copies = []
-        for p, (buf, land, _, _, order) in enumerate(parts):
-            start, size = state[p]
-            size //= 2
-            bit, device = partner(*order[i])
-            unit = 16 if buf is work else 8
-            send = pl.multiple_of(start + (1 - bit) * size, unit)
-            keep = pl.multiple_of(start + bit * size, unit)
-            copy = pltpu.make_async_remote_copy(
-                src_ref=buf.at[pl.ds(send, size), :],
-                dst_ref=land.at[pl.ds(landing[p], size), :],
-                send_sem=send_sem.at[p, i],
-                recv_sem=recv_sem.at[p, i],
-                device_id=device,
-                device_id_type=MESH,
-            )
-            copy.start()
-            copies.append((copy, keep, size, landing[p], unit))
-            state[p] = (keep, size)
-            landing[p] += size
-        for p, (copy, keep, size, low, unit) in enumerate(copies):
-            buf, land = parts[p][:2]
-            copy.wait()
-            step = next(c for c in (256, 128, 64, 32, 16, 8) if size % c == 0)
-
-            @pl.loop(0, size // step)
-            def _(j, buf=buf, land=land, keep=keep, low=low, step=step, unit=unit):
-                mine = pl.ds(pl.multiple_of(keep + j * step, unit), step)
-                theirs = pl.ds(pl.multiple_of(low + j * step, unit), step)
-                buf[mine, :] = (buf[mine, :].astype(F32) + land[theirs, :].astype(F32)).astype(buf.dtype)
-
-    for p, (buf, _, _, _, _) in enumerate(parts):
-        start, size = state[p]
-        unit = 16 if buf is work else 8
-        rows = pl.ds(pl.multiple_of(start, unit), size)
-        final = done if buf is work else sdone
-        final[rows, :] = buf[rows, :]
-
-    for i in reversed(range(rounds)):
-        copies = []
-        for p, (buf, _, _, _, order) in enumerate(parts):
-            start, size = state[p]
-            final = done if buf is work else sdone
-            bit, device = partner(*order[i])
-            unit = 16 if buf is work else 8
-            rows = pl.ds(pl.multiple_of(start, unit), size)
-            copy = pltpu.make_async_remote_copy(
-                src_ref=final.at[rows, :],
-                dst_ref=final.at[rows, :],
-                send_sem=send_sem.at[p, rounds + i],
-                recv_sem=recv_sem.at[p, rounds + i],
-                device_id=device,
-                device_id_type=MESH,
-            )
-            copy.start()
-            copies.append(copy)
-            state[p] = (start - bit * size, 2 * size)
-        for copy in copies:
-            copy.wait()
+    pl.semaphore_wait(barrier, len(peers))
+    parts = three_parts(work, recv, done, sizes, orders)
+    parts.append((swork, srecv, sdone, 0, srows, orders[0]))
+    sums = Sums(parts, send_sem, recv_sem)
+    for k in range(sums.ops + 1):
+        sums.advance(k)
 
     a = pltpu.make_async_copy(done, out_hbm, out_sem.at[0])
     b = pltpu.make_async_copy(sdone, small_hbm, out_sem.at[1])
@@ -1207,8 +1346,9 @@
 
 def reduce_all(channels, ff, ndp, nblk, *grads):
     ndev = ndp * nblk
-    rounds = len(bit_orders(ndp, nblk)[0])
-    _, _, sizes = pack_plan(channels, ff, ndev)
+    ops = 2 * len(orders_of(ndp, nblk)[0])
+    wide = widest(ndp, nblk)
+    _, _, sizes = rest_plan(channels, ndev)
     _, srows = small_plan(channels, ff, ndev)
     total = sum(sizes)
     vm = pl.BlockSpec(memory_space=pltpu.VMEM)
@@ -1221,15 +1361,11 @@
             jax.ShapeDtypeStruct((total, LANE), BF16),
             jax.ShapeDtypeStruct((srows, LANE), F32),
         ],
-        scratch_shapes=[
-            pltpu.VMEM((total, LANE), BF16),
-            pltpu.VMEM((total, LANE), BF16),
-            pltpu.VMEM((total, LANE), BF16),
-            pltpu.VMEM((srows, LANE), F32),
-            pltpu.VMEM((srows, LANE), F32),
-            pltpu.VMEM((srows, LANE), F32),
-            pltpu.SemaphoreType.DMA((4, 2 * rounds)),
-            pltpu.SemaphoreType.DMA((4, 2 * rounds)),
+        scratch_shapes=[pltpu.VMEM((total, LANE), BF16)] * 3
+        + [pltpu.VMEM((srows, LANE), F32)] * 3
+        + [
+            pltpu.SemaphoreType.DMA((4, ops, wide)),
+            pltpu.SemaphoreType.DMA((4, ops, wide)),
             pltpu.SemaphoreType.DMA((2,)),
         ],
         compiler_params=pltpu.CompilerParams(
@@ -1238,17 +1374,31 @@
     )(*grads)
 
 
-def unpack_kernel(channels, ff, ndev, packed, small, *outs):
+def unpack_kernel(channels, ff, ndev, out_in, ig_in, first, packed, small, *outs):
     cp = up_to(channels, LANE)
-    plan, _, _ = pack_plan(channels, ff, ndev)
+    plans = ((first, ffn_plan(channels, ff, ndev)[0]), (packed, rest_plan(channels, ndev)[0]))
     splan, _ = small_plan(channels, ff, ndev)
-    (g1, b1, wq, qb, wr, rb, rg, rbn, wkv, vb, wp, pb, g2, b2, we, eb, dt, db, ws, sb, cm) = outs
+    out, ig, g1, b1, wq, qb, wr, rb, rg, rbn, wkv, vb, wp, pb, g2, b2, we, eb, dt, db, ws, sb, cm, out_hold, ig_hold, in_sem, out_sem = (
+        outs
+    )
+    ins, moves = [], []
+    for k, (src, hold, dst) in enumerate(((out_in, out_hold, out), (ig_in, ig_hold, ig))):
+        for s in range(src.shape[0]):
+            ins.append(pltpu.make_async_copy(src.at[s], hold.at[s], in_sem.at[k, s]))
+            moves.append(pltpu.make_async_copy(hold.at[s], dst.at[s], out_sem.at[k, s]))
+    for copy in ins:
+        copy.start()
     lt = cp // LANE
 
+    for copy, move in zip(ins, moves):
+        copy.wait()
+        move.start()
+
     def slab(name, t, first=0, count=None):
+        ref, plan = plans[0] if name in plans[0][1] else plans[1]
         at, rows, _ = plan[name]
         count = rows if count is None else count
-        return packed[at + t * rows + first : at + t * rows + first + count, :].astype(F32)
+        return ref[at + t * rows + first : at + t * rows + first + count, :].astype(F32)
 
     for t in range(ff // LANE):
         cut = slice(t * LANE, (t + 1) * LANE)
@@ -1281,9 +1431,11 @@
             ref[...] = vec[k]
     at, rows, _ = splan["count"]
     cm[...] = small[at : at + rows, :].astype(jnp.int32)[:CLASSES, :CLASSES]
-
-
-def unpack(channels, ff, ndev, packed, small):
+    for move in moves:
+        move.wait()
+
+
+def unpack(channels, ff, ndev, out, ig, first, packed, small):
     one = (channels,)
     shapes = [
         one, one, (channels, channels), one, (channels, 4 * channels), one, one, one,
@@ -1292,11 +1444,21 @@
     ]
     outs = [jax.ShapeDtypeStruct(v, F32) for v in shapes]
     outs.append(jax.ShapeDtypeStruct((CLASSES, CLASSES), jnp.int32))
+    vm = pl.BlockSpec(memory_space=pltpu.VMEM)
+    hbm = pl.BlockSpec(memory_space=pl.ANY)
     return pl.pallas_call(
         functools.partial(unpack_kernel, channels, ff, ndev),
-        out_shape=outs,
+        in_specs=[hbm, hbm, vm, vm, vm],
+        out_specs=[hbm, hbm] + [vm] * len(outs),
+        out_shape=[jax.ShapeDtypeStruct(v.shape, v.dtype) for v in (out, ig)] + outs,
+        scratch_shapes=[
+            pltpu.VMEM(out.shape, out.dtype),
+            pltpu.VMEM(ig.shape, ig.dtype),
+            pltpu.SemaphoreType.DMA((2, out.shape[0])),
+            pltpu.SemaphoreType.DMA((2, out.shape[0])),
+        ],
         compiler_params=pltpu.CompilerParams(vmem_limit_bytes=VMEM),
-    )(packed, small)
+    )(out, ig, first, packed, small)
 
 
 NEG = np.float32(NEGATIVE * LOG2E)
@@ -1468,30 +1630,32 @@
     )
     full = full[0, 0] > 0
 
-    def either(call, cids, *operands):
+    def either(call, cids, sizes, *operands):
         if used == chips:
-            return call(dims, blk, chips, cids[1], *operands)
+            return call(*sizes, chips, cids[1], *operands)
         return lax.cond(
             full,
-            functools.partial(call, dims, blk, chips, cids[1]),
-            functools.partial(call, dims, blk, used, cids[0]),
+            functools.partial(call, *sizes, chips, cids[1]),
+            functools.partial(call, *sizes, used, cids[0]),
             *operands,
         )
 
     tok = tokens.reshape(scenes, n, channels)
     ct = cotangent.reshape(scenes, n, channels)
     red, counts, q, att, ke, ve, rn, res = either(
-        attend, (2, 3), tok, mask, labels, predicted, vec, wr, wq, ones, wk, wv, wp
+        attend, (2, 3), (dims, blk), tok, mask, labels, predicted, vec, wr, wq, ones, wk, wv, wp
     )
-    out, gres, dwe, dwst, dtap, dtb, dvec2 = ffn(
-        dims, blk, res, ct, vec, we, ws, depth_weight, tap_bias
+    out, gres, first, dtap, dtb, dvec2 = ffn(
+        dims, blk, ndp * blk, res, ct, vec, we, ws, depth_weight, tap_bias
     )
-    grn, gqt, dwp, dwkv, dbp = either(attback, (4, 5), q, att, gres, ke, ve, rn, wpe, wkv)
-    ig, dwqt, dwrt, dvec1 = tail(dims, tok, gqt, gres, grn, red, vec, query_weight, wr)
+    ig, dwqt, dwrt, dwp, dwkv, dbp, dvec1, first = either(
+        attback, (4, 5), (dims, ff, ndp, blk), q, att, gres, ke, ve, rn, tok, red, vec, wpe, wkv,
+        query_weight, wr, first,
+    )
     packed, small = reduce_all(
-        channels, ff, ndp, blk, dwe, dwst, dwrt, dwkv, dwp, dwqt, dtap, dtb, dvec2, dvec1, dbp, counts
+        channels, ff, ndp, blk, dwrt, dwkv, dwp, dwqt, dtap, dtb, dvec2, dvec1, dbp, counts
     )
-    grads = list(unpack(channels, ff, ndp * blk, packed, small))
+    out, ig, *grads = unpack(channels, ff, ndp * blk, out, ig, first, packed, small)
     grads[4], grads[18] = grads[4].T, grads[18].T
     return (out.reshape(tokens.shape), ig.reshape(tokens.shape), *grads)
 

time: 404 us -> 355 us (0.88)
  Pallas kernels: 384 us -> 335 us
    pallas_call x1, Pallas kernels: 68.6 us -> 38.6 us  [reduce_all(): pl.pallas_call(functools.partial(reduce_kernel, channels, ff, ndp, nblk),...]
    pallas_call x4 -> x3, Pallas kernels: 223 us -> 203 us  [the longest x1 117 us: attback(): pl.pallas_call(functools.partial(attback_kernel, dims, ff, ndp, blk, used...]
where the time goes in v2:
time: 355 us; the launch traced here: 349 us
  Pallas kernels  335 us (94%)
  loops' own time  11.8 us (3%)
    pallas_call x1, Pallas kernels, attback(): pl.pallas_call(functools.partial(attback_kernel, dims, ff, ndp, blk, used...  117 us
    pallas_call x1, Pallas kernels, attend(): pl.pallas_call(functools.partial(attend_kernel, dims, blk, used), grid=(s...  88.8 us
    pallas_call x1, Pallas kernels, ffn(): pl.pallas_call(functools.partial(ffn_kernel, dims, ff, blk, ndev), in_spe...  74 us
    pallas_call x1, Pallas kernels, reduce_all(): pl.pallas_call(functools.partial(reduce_kernel, channels, ff, ndp, nblk),...  38.6 us
    pallas_call x1, Pallas kernels, unpack(): pl.pallas_call(functools.partial(unpack_kernel, channels, ff, ndev), in_s...  12.1 us
    another operation x2, loops' own time, either(): lax.cond(full, functools.partial(call, *sizes, chips, cids[1]), functools...  11.8 us

profile of v2, /device:TPU:0, one launch (start us, length us, event | category | flops | bytes accessed | tf_op | source)
XLA Modules:
  0.0 348.9 jit_solution(16984005795872946959)
XLA Ops:
  0.7 4.9 %shard_map.416 = (f32[8,384]{1,0:T(8,128)S(1)}, bf16[384,640]{1,0:T(8,128)(2,1)}, bf16[384,640]{1,0:T(8,128)(2,1)}, bf16[384,640]{1,0:T(8,128)(2,1)}, bf16[384,3...) custom-call(f32[320]{0:T(512)} %g1.1, f32[320]{0:T(512)} %b1.1, ...), custom_call_target="tpu_custom_call" | custom-call | tf_op jit(solution)/shard_map/pallas_call | solution.py:1605
  6.2 89.1 %conditional.2 = ((f32[8,128,384]{2,1,0:T(8,128)}, f32[32,128]{1,0:T(8,128)}, bf16[8,512,640]{2,1,0:T(8,128)(2,1)}, f32[8,512,384]{2,1,0:T(8,128)}, bf16[8,1024,...) conditional(s32[]{:T(128)} %bitcast.2, ...), branch_computations={%region_0.0_spmd, %region_1.0_spmd} | conditional | bytes 8 | solution.py:1636
  6.4 88.8 %branch_1_fun.2 = (f32[8,128,384]{2,1,0:T(8,128)}, f32[32,128]{1,0:T(8,128)}, bf16[8,512,640]{2,1,0:T(8,128)(2,1)}, f32[8,512,384]{2,1,0:T(8,128)}, bf16[8,1024,...) custom-call(bf16[8,512,320]{2,1,0:T(8,128)(2,1)} %get-tuple-element., ...), custom_call_target="tpu_custom_call" | custom-call | tf_op jit(solution)/shard_map/cond/branch_1_fun/pallas_call | solution.py:491
  95.3 0.0 copy-start
  95.3 74.0 %shard_map.417 = (bf16[8,512,320]{2,1,0:T(8,128)(2,1)}, f32[8,512,320]{2,1,0:T(8,128)}, bf16[6656,128]{1,0:T(8,128)(2,1)}, f32[9,1280]{1,0:T(8,128)}, f32[8,1280]{1,0:T(8,128)}, /*index=5*/f32[8,384]{1,0:T(8,128)}) custom-call(f32[3,4096,128]{2,1,0:T(8,128)} %get-tuple-element.241.res_hbm, bf16[8,512,320]{2,1,0:T(8,128)(2,1)} %bitcast.13, ...), custom_call_target="tpu_custom_call" | custom-call | tf_op jit(solution)/shard_map/pallas_call | solution.py:908
  169.3 0.0 copy-done
  169.4 128.4 %conditional.3 = ((f32[8,512,320]{2,1,0:T(8,128)}, f32[320,384]{1,0:T(8,128)}, f32[4,384,384]{2,1,0:T(8,128)}, f32[384,384]{1,0:T(8,128)}, f32[384,768]{1,0:T(8,...) conditional(s32[]{:T(128)} %bitcast.2, (bf16[8,512,640]{2,1,0:T(8,128)(2,1)}, ...), branch_computations={%region_2.0_spmd, %region_3.0_spmd} | conditional | bytes 8 | solution.py:1636
  181.0 116.8 %branch_1_fun.3 = (f32[8,512,320]{2,1,0:T(8,128)}, f32[320,384]{1,0:T(8,128)}, f32[4,384,384]{2,1,0:T(8,128)}, f32[384,384]{1,0:T(8,128)}, f32[384,768]{1,0:T(8,...) custom-call(bf16[8,512,640]{2,1,0:T(8,128)(2,1)} %get-tuple-element.136.q_ref, ...), custom_call_target="tpu_custom_call" | custom-call | tf_op jit(solution)/shard_map/cond/branch_1_fun/pallas_call | solution.py:1240
  297.8 0.0 copy-start.1
  297.8 38.6 %shard_map.418 = (bf16[8192,128]{1,0:T(8,128)(2,1)}, f32[256,128]{1,0:T(8,128)}) custom-call(f32[4,384,384]{2,1,0:T(8,128)} %get-tuple-element.258.dwr, f32[384,768]{1,0:T(8,128)} %get-tuple-element.259.dwkv, f32[384,384]{1,0:T(8,128)} %get-tuple-element.260.dwp, f32[320,384]{1,0:T(8,128)} %get-tuple-element.261.dwq, f32[9,1280]{1,0:T(8,128)} %get-tuple-element.262.dtap, ...), custom_call_target="tpu_custom_call" | custom-call | tf_op jit(solution)/shard_map/pallas_call | solution.py:1356
  336.4 0.0 copy-done.1
  336.4 12.1 %shard_map.419 = (bf16[8,512,320]{2,1,0:T(8,128)(2,1)}, f32[8,512,320]{2,1,0:T(8,128)}, f32[320]{0:T(512)}, f32[320]{0:T(512)}, f32[320,320]{1,0:T(8,128)}, /*in...) custom-call(bf16[8,512,320]{2,1,0:T(8,128)(2,1)} %get-tuple-element., ...), custom_call_target="tpu_custom_call" | custom-call | tf_op jit(solution)/shard_map/pallas_call | solution.py:1449
Async XLA Ops:
  95.3 74.0 %copy-start = (bf16[320,320]{1,0:T(8,128)(2,1)S(1)}, bf16[320,320]{1,0:T(8,128)(2,1)}, u32[]{:S(2)}) copy-start(bf16[320,320]{1,0:T(8,128)(2,1)} %qw.1) | copy-start | bytes 614404
  297.8 38.6 %copy-start.1 = (bf16[6656,128]{1,0:T(8,128)(2,1)S(1)}, bf16[6656,128]{1,0:T(8,128)(2,1)}, u32[]{:S(2)}) copy-start(bf16[6656,128]{1,0:T(8,128)(2,1)} %get-tuple-element.257.first) | copy-start | bytes 5111812

commit v3 on v2

--- a/solution.py
+++ b/solution.py
@@ -24,6 +24,10 @@
 VMEM = 62 * 2**20
 FF_CHUNK = 256
 GROUP = 8
+NEG = np.float32(NEGATIVE * LOG2E)
+NEG_HI = np.float32(ml_dtypes.bfloat16(NEG))
+NEG_MID = np.float32(ml_dtypes.bfloat16(NEG - NEG_HI))
+NEG_LO = np.float32(ml_dtypes.bfloat16(NEG - NEG_HI - NEG_MID))
 
 
 def up_to(value, step):
@@ -54,9 +58,35 @@
     return pl.BlockSpec((1,) + shape, lambda s: (s,) + (0,) * len(shape))
 
 
+def inside(value, channels):
+    full = channels // LANE * LANE
+    if full == value.shape[-1]:
+        return value
+    last = value[..., full:]
+    last = jnp.where(lanes(last.shape) < channels - full, last, 0.0)
+    return jnp.concatenate([value[..., :full], last], -1)
+
+
+def head_blocks(value, free):
+    half = lanes((1, LANE)) // HALF
+    fills = [free(0), free(1)]
+    return [
+        jnp.where(half == h % 2, value[:, h // 2 * LANE : (h // 2 + 1) * LANE], fills[h % 2])
+        for h in range(HEADS)
+    ]
+
+
+def free_row(parity, values):
+    lane = lanes((1, LANE))
+    row = jnp.zeros((1, LANE), F32)
+    for k, value in values.items():
+        row = jnp.where(lane == ext_lane(parity) + k, value, row)
+    return row
+
+
 def centered(value, channels):
     mean = jnp.sum(value, -1, keepdims=True) * (1.0 / channels)
-    center = jnp.where(lanes(value.shape) < channels, value - mean, 0.0)
+    center = inside(value - mean, channels)
     var = jnp.sum(center * center, -1, keepdims=True) * (1.0 / channels)
     rstd = lax.rsqrt(var + EPSILON)
     return center * rstd, rstd
@@ -280,9 +310,36 @@
     return max(group[2] for group in orders_of(ndp, nblk)[0]) - 1
 
 
+def packed_rows(keys, cp):
+    return (cp // LANE - 1) * keys + keys // 2 + 16
+
+
+def pack_block(value, unc, keys, cp):
+    full = cp // LANE - 1
+    last = value[:, full * LANE :]
+    turned = pltpu.roll(last[keys // 2 :], HALF, 1)
+    last = jnp.where(lanes((1, LANE)) < HALF, last[: keys // 2], turned)
+    flags = jnp.broadcast_to(unc, (keys, LANE))
+    if keys < LANE:
+        flags = jnp.concatenate([flags, jnp.zeros((LANE - keys, LANE), F32)], 0)
+    parts = [value[:, t * LANE : (t + 1) * LANE] for t in range(full)] + [last, flags.T[:16]]
+    return jnp.concatenate([v.astype(BF16) for v in parts], 0)
+
+
+def unpack_block(block, ones, keys, cp):
+    full = cp // LANE - 1
+    parts = [block[t * keys : (t + 1) * keys] for t in range(full)]
+    last = block[full * keys : full * keys + keys // 2].astype(F32)
+    last = jnp.concatenate([last, pltpu.roll(last, HALF, 1)], 0)
+    last = jnp.where(lanes((1, LANE)) < HALF, last, ones)
+    flags = block[full * keys + keys // 2 :].astype(F32)[0:1]
+    flags = jnp.broadcast_to(flags, (LANE, LANE)).T[:keys]
+    return jnp.concatenate(parts + [last.astype(BF16)], -1), flags
+
+
 def attend_kernel(
     dims, blk, used, tok_ref, mask_ref, label_ref, pred_ref, tok2_ref, vec_ref, wr_ref, wq_ref,
-    one_ref, wk_ref, wv_ref, wp_ref,
+    wkv_ref, wp_ref,
     red_ref, cnt_ref, q_ref, att_ref, ke_ref, ve_ref, rn_ref, res_ref,
     scr, qbuf, oe, rnbuf, up_send, down_send, sib_send, line_recv, sib_recv,
 ):
@@ -340,8 +397,7 @@
             both = m[2 * i : 2 * i + 1] + m[2 * i + 1 : 2 * i + 2]
             flags.append(jnp.sum(jnp.where(near, both, 0.0), -1, keepdims=True))
         unc = jnp.where(jnp.concatenate(flags, 0) > 0.0, 0.0, 1.0)
-        flag = jnp.where(lanes((keys, cp)) == channels, unc, 0.0)
-        own = (rhat * vec_ref[2:3] + vec_ref[3:4] + flag).astype(BF16)
+        own = pack_block(rhat * vec_ref[2:3] + vec_ref[3:4], unc, keys, cp)
 
         @pl.when(chip < used)
         def _():
@@ -356,8 +412,10 @@
             def _():
                 send_down(s, chip).start()
 
-        qf = dot(low, wq_ref[...]) * (LOG2E * head_size**-0.5) + one_ref[...]
-        qbuf[lax.rem(s, lag + 1)] = qf.astype(BF16)
+        qf = dot(low, wq_ref[...]) * (LOG2E * head_size**-0.5)
+        ones = head_blocks(qf, lambda e: free_row(e, {0: 1.0, 1: 1.0, 2: 1.0}))
+        for h in range(HEADS):
+            qbuf[lax.rem(s, lag + 1), :, h * LANE : (h + 1) * LANE] = ones[h].astype(BF16)
         shape = (cnt_ref.shape[0], width)
         classes = lax.broadcasted_iota(jnp.int32, shape, 0)
         wide = lax.broadcasted_iota(jnp.int32, (LANE, width), 0)
@@ -403,10 +461,24 @@
         for origin in range(used):
             send_sib(s, origin).wait_recv()
 
-        rn_all = rnbuf[s].reshape(2 * used * keys, cp)
+        free = vec_ref[3:4, cp - LANE :]
+        blocks = [unpack_block(rnbuf[s, i], free, keys, cp) for i in range(2 * used)]
+        rn_all = jnp.concatenate([v[0] for v in blocks], 0)
         rn_ref[0] = rn_all
-        ke_ref[0] = dot(rn_all, wk_ref[...]).astype(BF16)
-        ve_ref[0] = dot(rn_all, wv_ref[...]).astype(BF16)
+        flag = jnp.concatenate([v[1] for v in blocks], 0)
+        kv = dot(rn_all, wkv_ref[...])
+        negative = {0: float(NEG_HI), 1: float(NEG_MID), 2: float(NEG_LO)}
+        for h, block in enumerate(
+            head_blocks(
+                kv[:, :cp],
+                lambda e: flag * free_row(e, negative) + free_row(e, {3: 1.0, 4: 1.0, 5: 1.0}),
+            )
+        ):
+            ke_ref[0, :, h * LANE : (h + 1) * LANE] = block.astype(BF16)
+        for h, block in enumerate(
+            head_blocks(kv[:, cp:], lambda e: free_row(e, {0: 1.0, 1: 1.0, 2: 1.0}))
+        ):
+            ve_ref[0, :, h * LANE : (h + 1) * LANE] = block.astype(BF16)
         mine = lax.rem(s, lag + 1)
         count = 2 * used * keys // KEY_CHUNK
         for h in range(HEADS):
@@ -470,7 +542,7 @@
                     send_down(s, origin).wait_send()
 
 
-def attend(dims, blk, used, cid, tok, mask, labels, predicted, vec, wr, wq, ones, wk, wv, wp):
+def attend(dims, blk, used, cid, tok, mask, labels, predicted, vec, wr, wq, wkv, wp):
     scenes, height, width, channels, cp = dims
     n = height * width
     keys = n // 4
@@ -494,7 +566,7 @@
         in_specs=[early((n, channels))]
         + [early((height, width))] * 3
         + [late((n, channels))]
-        + [whole(v.shape) for v in (vec, wr, wq, ones, wk, wv, wp)],
+        + [whole(v.shape) for v in (vec, wr, wq, wkv, wp)],
         out_specs=[
             early((keys, cp)),
             whole((32, LANE)),
@@ -519,20 +591,20 @@
             pltpu.VMEM((cp // LANE, n, LANE), F32),
             pltpu.VMEM((lag + 1, n, he), BF16),
             pltpu.VMEM((HEADS, n, LANE), F32),
-            pltpu.VMEM((scenes, 2 * used, keys, cp), BF16),
+            pltpu.VMEM((scenes, 2 * used, packed_rows(keys, cp), LANE), BF16),
         ]
         + [pltpu.SemaphoreType.DMA((scenes, used))] * 5,
         compiler_params=pltpu.CompilerParams(
             vmem_limit_bytes=VMEM, collective_id=cid, has_side_effects=True
         ),
-    )(tok, mask, labels, predicted, tok, vec, wr, wq, ones, wk, wv, wp)
+    )(tok, mask, labels, predicted, tok, vec, wr, wq, wkv, wp)
 
 
 def ffn_kernel(
-    dims, ff, blk, ndev, res_hbm, ct_hbm, vec_ref, we_ref, ws_ref, taps_ref, tb_ref,
+    dims, ff, blk, ndev, res_hbm, ct_hbm, ew_hbm, sw_hbm, vec_ref, eb_ref, taps_ref, tb_ref,
     out_hbm, gres_hbm, pack_hbm, dtap_ref, dtb_ref, dvec_ref,
-    dwe_ref, dwst, packed, res_ref, ct_ref, cn, cnt, ctt, ctx, oacc, gacc, hid, gm, halo, act, back, tapacc, out_stage, gres_stage,
-    pack_sem, res_sem, ct_sem, out_sem, gres_sem, cn_send, cn_recv, gm_send, gm_recv,
+    we_ref, ws_ref, dwe_ref, dwst, packed, res_ref, ct_ref, cn, cnt, ctt, ctx, oacc, gacc, hid, gm, halo, act, back, tapacc, out_stage, gres_stage,
+    weight_sem, pack_sem, res_sem, ct_sem, out_sem, gres_sem, cn_send, cn_recv, gm_send, gm_recv,
 ):
     scenes, height, width, channels, cp = dims
     n = height * width
@@ -556,10 +628,19 @@
     def ct_copy(s):
         return pltpu.make_async_copy(ct_hbm.at[s], ct_ref.at[s], ct_sem.at[s])
 
+    ew_copy = pltpu.make_async_copy(ew_hbm, we_ref.at[:channels, :], weight_sem.at[0])
+    sw_copy = pltpu.make_async_copy(sw_hbm, ws_ref.at[:channels, :], weight_sem.at[1])
     for r in range(height):
         res_copy(r).start()
     for s in range(scenes):
         ct_copy(s).start()
+    ew_copy.start()
+    sw_copy.start()
+    bias_rows = eb_ref.shape[0]
+    we_ref[channels : channels + bias_rows, :] = eb_ref[...]
+    if channels + bias_rows < cp:
+        we_ref[channels + bias_rows :, :] = jnp.zeros((cp - channels - bias_rows, ff), BF16)
+    ws_ref[channels:, :] = jnp.zeros((cp - channels, ff), BF16)
 
     barrier = pltpu.get_barrier_semaphore()
 
@@ -637,6 +718,8 @@
         ctx[:, row(r)] = low.T
         store3(gacc, r, jnp.zeros((rw, cp), F32))
 
+    ew_copy.wait()
+    sw_copy.wait()
     dwe_ref[...] = jnp.zeros(dwe_ref.shape, F32)
     dwst[...] = jnp.zeros(dwst.shape, F32)
 
@@ -695,8 +778,6 @@
         hidden(2)
         sums = jnp.zeros((8, fc), F32)
         for r in range(height):
-            if r + 3 < height + 2:
-                hidden(r + 3)
             back[...] = dot(ctt[r * rw : (r + 1) * rw, :], ws_ref[:, span])
             if r:
                 products(r - 1)
@@ -722,6 +803,8 @@
                     gm[slot, r + 1, cols + 1] = jnp.concatenate([v[0, scenes:], z], 0).astype(BF16)
                 if g + group == cols:
                     gm[slot, r + 1, 0] = jnp.concatenate([z, v[group - 1, :scenes]], 0).astype(BF16)
+            if r + 3 < height + 2:
+                hidden(r + 3)
         products(height - 1)
         dtb_ref[:, span] = sums
 
@@ -767,8 +850,6 @@
                 gacc[t, r * rw : (r + 1) * rw, :] += g[:, t * LANE : (t + 1) * LANE]
 
         for r in range(height):
-            if r:
-                products(r - 1)
             tapsum = [None] * 9
             for g in range(0, cols, group):
                 acc = None
@@ -788,7 +869,8 @@
                 act[r * rw + g * pair : r * rw + (g + group) * pair, :] = acc.reshape(group * pair, fc)
             for i in range(9):
                 tapacc[i] += tapsum[i].astype(F32)
-        products(height - 1)
+        for r in range(height):
+            products(r)
 
         for tap in range(9):
             dtap_ref[pl.ds(tap, 1), span] = jnp.sum(tapacc[tap], 0, keepdims=True)
@@ -869,7 +951,7 @@
     def _(r):
         kept = load3(res_ref, r)
         rstd = kept[:, channels : channels + 1]
-        xhat = jnp.where(lanes(kept.shape) < channels, kept, 0.0)
+        xhat = inside(kept, channels)
         upstream = load3(gacc, r)
         dvec_ref[0:1] += jnp.sum(upstream * xhat, 0, keepdims=True)
         dvec_ref[1:2] += jnp.sum(upstream, 0, keepdims=True)
@@ -893,12 +975,12 @@
     pack_copy.wait()
 
 
-def ffn(dims, blk, ndev, res, ct, vec, we, ws, taps, tb):
+def ffn(dims, blk, ndev, res, ct, ew, sw, vec, eb, taps, tb):
     scenes, height, width, channels, cp = dims
     n = height * width
     total = scenes * n
     rw = scenes * width
-    ff = ws.shape[1]
+    ff = sw.shape[1]
     lt = cp // LANE
     nchunk = ff // FF_CHUNK
     strip = (width // 2 + 2, 2 * scenes, FF_CHUNK)
@@ -907,7 +989,7 @@
     hbm = pl.BlockSpec(memory_space=pl.ANY)
     return pl.pallas_call(
         functools.partial(ffn_kernel, dims, ff, blk, ndev),
-        in_specs=[hbm, hbm] + [vm] * 5,
+        in_specs=[hbm] * 4 + [vm] * 4,
         out_specs=[hbm, hbm, hbm] + [vm] * 3,
         out_shape=[
             jax.ShapeDtypeStruct((scenes, n, channels), BF16),
@@ -918,6 +1000,8 @@
             jax.ShapeDtypeStruct((8, cp), F32),
         ],
         scratch_shapes=[
+            pltpu.VMEM((cp, ff), BF16),
+            pltpu.VMEM((cp, ff), BF16),
             pltpu.VMEM((cp, ff), F32),
             pltpu.VMEM((cp, ff), F32),
             pltpu.VMEM((pack_rows, LANE), BF16),
@@ -937,6 +1021,7 @@
             pltpu.VMEM((9, 2 * scenes, FF_CHUNK), F32),
             pltpu.VMEM((2, n, channels), BF16),
             pltpu.VMEM((2, n, channels), F32),
+            pltpu.SemaphoreType.DMA((2,)),
             pltpu.SemaphoreType.DMA((1,)),
             pltpu.SemaphoreType.DMA((height,)),
             pltpu.SemaphoreType.DMA((scenes,)),
@@ -950,12 +1035,12 @@
         compiler_params=pltpu.CompilerParams(
             vmem_limit_bytes=VMEM, collective_id=0, has_side_effects=True
         ),
-    )(res, ct, vec, we, ws, taps, tb)
+    )(res, ct, ew, sw, vec, eb, taps, tb)
 
 
 def attback_kernel(
     dims, ff, ndp, blk, used, q_ref, att_ref, gres_ref, ke_ref, ve_ref, rn_ref, tok_ref, gres2_ref,
-    red_ref, vec_ref, wpe_ref, wkv_ref, wq_ref, wr_ref, first_hbm,
+    red_ref, vec_ref, wp_ref, wkv_ref, wq_ref, wr_ref, first_hbm,
     ig_ref, dwqt, dwrt, dwp_ref, dwkv_ref, dbp_ref, dvec_ref, sum_hbm,
     ge, dqt, gqt_ref, grn_ref, scr, gscr, own, acc, sib_land, up_land, down_land,
     work, land, done,
@@ -1058,11 +1143,11 @@
         dbp_ref[...] += jnp.sum(gb.astype(F32).reshape(n // 8, 8, cp), 0)
         att = att_ref[0]
         dwp_ref[...] += dot(att.astype(BF16).T, gb)
-        gatt = dot_nt(gb, wpe_ref[...])
+        gatt = head_blocks(dot_nt(gb, wp_ref[...]), lambda e: 0.0)
         lane = lanes((n, LANE))
         for h in range(HEADS):
             e = ext_lane(h)
-            g = gatt[:, h * LANE : (h + 1) * LANE].astype(BF16).astype(F32)
+            g = gatt[h].astype(BF16).astype(F32)
             o = att[:, (h // 2) * LANE : (h // 2 + 1) * LANE]
             inner = jnp.sum(g * o, -1, keepdims=True)
             hi = inner.astype(BF16).astype(F32)
@@ -1141,46 +1226,56 @@
             if t * each <= sums.ops < (t + 1) * each:
                 pltpu.make_async_copy(done, sum_hbm, sum_sem.at[0]).start()
 
-    def tail(i, s):
-        rhat, rstd = centered(red_ref[i], channels)
-        inside = lanes((keys, cp)) < channels
-        upstream = jnp.where(inside, grn_ref[s], 0.0)
-        dvec_ref[0:1] += jnp.sum(upstream * rhat, 0, keepdims=True)
-        dvec_ref[1:2] += jnp.sum(upstream, 0, keepdims=True)
-        gred = norm_back(upstream, vec_ref[2:3], rhat, rstd, channels)
-        gred = jnp.where(inside, gred, 0.0).astype(BF16)
+    def tail(base):
+        gred, low, hats = [], [], []
+        for i in range(together):
+            rhat, rstd = centered(red_ref[i], channels)
+            upstream = inside(grn_ref[base + i], channels)
+            dvec_ref[0:1] += jnp.sum(upstream * rhat, 0, keepdims=True)
+            dvec_ref[1:2] += jnp.sum(upstream, 0, keepdims=True)
+            g = norm_back(upstream, vec_ref[2:3], rhat, rstd, channels)
+            gred.append(inside(g, channels).astype(BF16))
+            x = widen(tok_ref[i].astype(F32), cp)
+            xhat, xstd = centered(x, channels)
+            hats.append((xhat, xstd))
+            low.append((xhat * vec_ref[0:1] + vec_ref[1:2]).astype(BF16))
+            lowf = low[i].astype(F32)
+            for t in range(lt):
+                scr[i, t] = lowf[:, t * LANE : (t + 1) * LANE]
+        gred = jnp.concatenate(gred, 0)
         gred_t = gred.T
-        x = widen(tok_ref[i].astype(F32), cp)
-        xhat, xstd = centered(x, channels)
-        low = (xhat * vec_ref[0:1] + vec_ref[1:2]).astype(BF16)
-        lowf = low.astype(F32)
-        for t in range(lt):
-            scr[i, t] = lowf[:, t * LANE : (t + 1) * LANE]
         for b in range(2):
-            part = [scr[i, t, pl.ds(b, n // 2, stride=2), :] for t in range(lt)]
-            part = jnp.concatenate(part, -1).reshape(height // 2, 2, width // 2, cp)
+            patches = [[], []]
+            for i in range(together):
+                part = [scr[i, t, pl.ds(b, n // 2, stride=2), :] for t in range(lt)]
+                part = jnp.concatenate(part, -1).reshape(height // 2, 2, width // 2, cp)
+                for a in range(2):
+                    patches[a].append(part[:, a].reshape(keys, cp))
             for a in range(2):
                 ab = 2 * a + b
-                dwrt[ab] += dot(gred_t, part[:, a].reshape(keys, cp).astype(BF16))
+                dwrt[ab] += dot(gred_t, jnp.concatenate(patches[a], 0).astype(BF16))
                 back = dot_nt(gred, wr_ref[ab])
-                for t in range(lt):
-                    for r in range(height // 2):
-                        gscr[i, t, pl.ds((2 * r + a) * width + b, width // 2, stride=2), :] = back[
-                            r * (width // 2) : (r + 1) * (width // 2), t * LANE : (t + 1) * LANE
-                        ]
-        gqt = gqt_ref[s]
-        dwqt[...] += dot(gqt, low)
-        gn = widen(dot_nt(gqt.T, wq_ref[...]), cp)
-        gn = gn + jnp.concatenate([gscr[i, t] for t in range(lt)], -1)
-        dvec_ref[3:4] += jnp.sum(gn * xhat, 0, keepdims=True)
-        dvec_ref[4:5] += jnp.sum(gn, 0, keepdims=True)
-        gx = norm_back(gn, vec_ref[0:1], xhat, xstd, channels)
-        ig_ref[i] = gres2_ref[i] + gx[:, :channels]
+                for i in range(together):
+                    for t in range(lt):
+                        for r in range(height // 2):
+                            at = i * keys + r * (width // 2)
+                            gscr[i, t, pl.ds((2 * r + a) * width + b, width // 2, stride=2), :] = back[
+                                at : at + width // 2, t * LANE : (t + 1) * LANE
+                            ]
+        for i in range(together):
+            gqt = gqt_ref[base + i]
+            xhat, xstd = hats[i]
+            dwqt[...] += dot(gqt, low[i])
+            gn = widen(dot_nt(gqt.T, wq_ref[...]), cp)
+            gn = gn + jnp.concatenate([gscr[i, t] for t in range(lt)], -1)
+            dvec_ref[3:4] += jnp.sum(gn * xhat, 0, keepdims=True)
+            dvec_ref[4:5] += jnp.sum(gn, 0, keepdims=True)
+            gx = norm_back(gn, vec_ref[0:1], xhat, xstd, channels)
+            ig_ref[i] = gres2_ref[i] + gx[:, :channels]
 
     @pl.when(step >= scenes)
     def _():
-        for i in range(together):
-            tail(i, (step - scenes) * together + i)
+        tail((step - scenes) * together)
 
     @pl.when(step < scenes)
     def _():
@@ -1211,7 +1306,7 @@
 
 
 def attback(
-    dims, ff, ndp, blk, used, cid, q, att, gres, ke, ve, rn, tok, red, vec, wpe, wkv, wq, wr, first
+    dims, ff, ndp, blk, used, cid, q, att, gres, ke, ve, rn, tok, red, vec, wp, wkv, wq, wr, first
 ):
     scenes, height, width, channels, cp = dims
     n = height * width
@@ -1280,7 +1375,7 @@
         compiler_params=pltpu.CompilerParams(
             vmem_limit_bytes=VMEM, collective_id=cid, has_side_effects=True
         ),
-    )(q, att, gres, ke, ve, rn, tok, gres, red, vec, wpe, wkv, wq, wr, first)
+    )(q, att, gres, ke, ve, rn, tok, gres, red, vec, wp, wkv, wq, wr, first)
 
 
 def reduce_kernel(
@@ -1461,31 +1556,6 @@
     )(out, ig, first, packed, small)
 
 
-NEG = np.float32(NEGATIVE * LOG2E)
-NEG_HI = np.float32(ml_dtypes.bfloat16(NEG))
-NEG_MID = np.float32(ml_dtypes.bfloat16(NEG - NEG_HI))
-NEG_LO = np.float32(ml_dtypes.bfloat16(NEG - NEG_HI - NEG_MID))
-
-
-def ext_row(values):
-    lane = lanes((1, HEADS * LANE))
-    row = jnp.zeros((1, HEADS * LANE), F32)
-    for h in range(HEADS):
-        for k, value in values.items():
-            row = jnp.where(lane == h * LANE + ext_lane(h) + k, value, row)
-    return row
-
-
-def spread(value, cp):
-    value = widen(value, cp)
-    half = lanes((1, LANE)) // HALF
-    blocks = []
-    for h in range(HEADS):
-        tile = value[:, (h // 2) * LANE : (h // 2 + 1) * LANE]
-        blocks.append(jnp.where(half == h % 2, tile, jnp.zeros_like(tile)))
-    return jnp.concatenate(blocks, -1)
-
-
 def split_low(value):
     hi = value.astype(BF16).astype(F32)
     return hi, value - hi
@@ -1501,12 +1571,10 @@
 
 
 def prep_kernel(
-    channels, g1, b1, qw, qb, rw, rb, rg, rbn, kvw, vb, pw, pb, g2, b2, ew, eb, tb, sw, sb,
-    vec, wq, wk, wv, wp, wpe, wkv, wr, we, ws, one, dbias, full,
+    channels, g1, b1, qw, qb, rw, rb, rg, rbn, kvw, vb, pw, pb, g2, b2, eb, tb, sb,
+    vec, wq, wp, wkv, wr, ebias, dbias, full,
 ):
     cp = up_to(channels, LANE)
-    he = HEADS * LANE
-    ff = ew.shape[1]
     head_size = channels // HEADS
     rest = cp - channels - 16
 
@@ -1538,30 +1606,19 @@
         if rest:
             ref[channels + 16 :, :] = jnp.zeros((rest, width), BF16)
 
-    ones = ext_row({0: 1.0, 1: 1.0, 2: 1.0})
-    one[...] = ones
     dbias[...] = row(tb)
-    qs = spread(qw[...], cp)
-    qb_hi, qb_lo = split_low(row(qb))
-    fill(wq, qs, spread(qb_hi, cp), spread(qb_lo, cp))
+    ebias[...] = rows16(*split_low(row(eb)))
+    q = widen(qw[...], cp)
+    qb_wide = widen(row(qb), cp)
+    fill(wq, q, *split_low(qb_wide))
     kw = widen(kvw[:, :channels], cp)
     vw = widen(kvw[:, channels:], cp)
-    ks = spread(kvw[:, :channels], cp)
-    nil = jnp.zeros((1, he), F32)
-    fill(
-        wk, ks, ext_row({0: float(NEG_HI), 1: float(NEG_MID), 2: float(NEG_LO)}),
-        ext_row({3: 1.0, 4: 1.0, 5: 1.0}),
-    )
-    vb_hi, vb_lo = split_low(row(vb))
-    fill(wv, spread(kvw[:, channels:], cp), nil, spread(vb_hi, cp) + ones, spread(vb_lo, cp))
-    p = widen(pw[...], cp)
-    fill(wp, p)
-    zero = jnp.zeros((HALF, cp), BF16)
-    for h in range(HEADS):
-        data, other = (0, HALF) if h % 2 == 0 else (HALF, 0)
-        wpe[h * LANE + data : h * LANE + data + HALF, :] = p[h * HALF : (h + 1) * HALF]
-        wpe[h * LANE + other : h * LANE + other + HALF, :] = zero
-    fill(wkv, jnp.concatenate([kw, vw], -1))
+    nil = jnp.zeros((1, 2 * cp), F32)
+    vb_rows = [
+        jnp.concatenate([jnp.zeros((1, cp), F32), widen(v, cp)], -1) for v in split_low(row(vb))
+    ]
+    fill(wkv, jnp.concatenate([kw, vw], -1), nil, *vb_rows)
+    fill(wp, widen(pw[...], cp))
     rb_rows = [widen(v, cp) for v in split_low(row(rb))]
     rw_rows = rw[...].T
     for ab in range(4):
@@ -1569,8 +1626,6 @@
             wr.at[ab], widen(rw_rows[ab * channels : (ab + 1) * channels, :], cp),
             *rb_rows[ab : ab + 1],
         )
-    fill(we, ew[...], *split_low(row(eb)))
-    fill(ws, sw[...])
 
     def norm(v):
         return jnp.sqrt(jnp.sum(v * v, (0, 1), keepdims=True))
@@ -1581,26 +1636,24 @@
         top = jnp.max(jnp.abs(row(gain)), (0, 1), keepdims=True)
         return root * top + norm(row(bias))
 
+    def head(value, h):
+        tile = value[:, h // 2 * LANE : (h // 2 + 1) * LANE].astype(F32)
+        return jnp.where(lanes((1, LANE)) // HALF == h % 2, tile, 0.0)
+
     query_in, key_in = reach(g1, b1), reach(rg, rbn)
-    qb_wide = spread(row(qb), cp)
     bound = jnp.zeros((1, 1), F32)
     for h in range(HEADS):
-        cut = slice(h * LANE, (h + 1) * LANE)
-        query = query_in * norm(qs[:, cut].astype(F32)) + norm(qb_wide[:, cut])
-        key = key_in * norm(ks[:, cut].astype(F32))
-        bound = jnp.maximum(bound, query * key)
+        query = query_in * norm(head(q, h)) + norm(head(qb_wide, h))
+        bound = jnp.maximum(bound, query * key_in * norm(head(kw, h)))
     bound = bound * (head_size**-0.5 * 1.05)
     full[...] = jnp.where(2.0 * bound + 256.0 < -NEGATIVE, 0, 1).astype(jnp.int32)
 
 
-def prep(channels, *weights):
+def prep(channels, ff, *weights):
     cp = up_to(channels, LANE)
-    he = HEADS * LANE
-    ff = weights[14].shape[1]
     shapes = [
-        ((8, cp), F32), ((cp, he), BF16), ((cp, he), BF16), ((cp, he), BF16), ((cp, cp), BF16),
-        ((he, cp), BF16), ((cp, 2 * cp), BF16), ((4, cp, cp), BF16), ((cp, ff), BF16),
-        ((cp, ff), BF16), ((1, he), F32), ((1, ff), F32), ((1, 1), jnp.int32),
+        ((8, cp), F32), ((cp, cp), BF16), ((cp, cp), BF16), ((cp, 2 * cp), BF16),
+        ((4, cp, cp), BF16), ((16, ff), BF16), ((1, ff), F32), ((1, 1), jnp.int32),
     ]
     return pl.pallas_call(
         functools.partial(prep_kernel, channels),
@@ -1623,10 +1676,10 @@
     chips = blk // 2
     used = min(chips, -(-MASK_ROWS // (2 * height)))
 
-    vec, wq, wk, wv, wp, wpe, wkv, wr, we, ws, ones, tap_bias, full = prep(
-        channels, norm1_gain, norm1_bias, query_weight, query_bias, reduce_weight.T, reduce_bias,
+    vec, wq, wp, wkv, wr, expand_rows, tap_bias, full = prep(
+        channels, ff, norm1_gain, norm1_bias, query_weight, query_bias, reduce_weight.T, reduce_bias,
         rnorm_gain, rnorm_bias, kv_weight, value_bias, proj_weight, proj_bias, norm2_gain,
-        norm2_bias, expand_weight, expand_bias, depth_bias, shrink_weight.T, shrink_bias,
+        norm2_bias, expand_bias, depth_bias, shrink_bias,
     )
     full = full[0, 0] > 0
 
@@ -1643,13 +1696,14 @@
     tok = tokens.reshape(scenes, n, channels)
     ct = cotangent.reshape(scenes, n, channels)
     red, counts, q, att, ke, ve, rn, res = either(
-        attend, (2, 3), (dims, blk), tok, mask, labels, predicted, vec, wr, wq, ones, wk, wv, wp
+        attend, (2, 3), (dims, blk), tok, mask, labels, predicted, vec, wr, wq, wkv, wp
     )
     out, gres, first, dtap, dtb, dvec2 = ffn(
-        dims, blk, ndp * blk, res, ct, vec, we, ws, depth_weight, tap_bias
+        dims, blk, ndp * blk, res, ct, expand_weight, shrink_weight.T, vec, expand_rows, depth_weight,
+        tap_bias,
     )
     ig, dwqt, dwrt, dwp, dwkv, dbp, dvec1, first = either(
-        attback, (4, 5), (dims, ff, ndp, blk), q, att, gres, ke, ve, rn, tok, red, vec, wpe, wkv,
+        attback, (4, 5), (dims, ff, ndp, blk), q, att, gres, ke, ve, rn, tok, red, vec, wp, wkv,
         query_weight, wr, first,
     )
     packed, small = reduce_all(

time: 355 us -> 344 us (0.969)
  Pallas kernels: 335 us -> 325 us
    pallas_call x1, Pallas kernels: 88.8 us -> 83.5 us  [attend(): pl.pallas_call(functools.partial(attend_kernel, dims, blk, used), grid=(s...]
where the time goes in v3:
time: 344 us; the launch traced here: 338 us
  Pallas kernels  325 us (94%)
  loops' own time  12.2 us (4%)
    pallas_call x1, Pallas kernels, attback(): pl.pallas_call(functools.partial(attback_kernel, dims, ff, ndp, blk, used...  116 us
    pallas_call x1, Pallas kernels, attend(): pl.pallas_call(functools.partial(attend_kernel, dims, blk, used), grid=(s...  83.5 us
    pallas_call x1, Pallas kernels, ffn(): pl.pallas_call(functools.partial(ffn_kernel, dims, ff, blk, ndev), in_spe...  71.2 us
    pallas_call x1, Pallas kernels, reduce_all(): pl.pallas_call(functools.partial(reduce_kernel, channels, ff, ndp, nblk),...  38.6 us
    another operation x2, loops' own time, either(): lax.cond(full, functools.partial(call, *sizes, chips, cids[1]), functools...  12.2 us
    pallas_call x1, Pallas kernels, unpack(): pl.pallas_call(functools.partial(unpack_kernel, channels, ff, ndev), in_s...  12.1 us

profile of v3, /device:TPU:0, one launch (start us, length us, event | category | flops | bytes accessed | tf_op | source)
XLA Modules:
  0.0 338.5 jit_solution(12469076608227047442)
XLA Ops:
  0.7 3.1 shard_map.416
  4.4 84.0 %conditional.2 = ((f32[8,128,384]{2,1,0:T(8,128)}, f32[32,128]{1,0:T(8,128)}, bf16[8,512,640]{2,1,0:T(8,128)(2,1)}, f32[8,512,384]{2,1,0:T(8,128)}, bf16[8,1024,...) conditional(s32[]{:T(128)} %bitcast.1, ...), branch_computations={%region_0.0_spmd, %region_1.0_spmd} | conditional | bytes 8 | solution.py:1689
  4.9 83.5 %branch_1_fun.2 = (f32[8,128,384]{2,1,0:T(8,128)}, f32[32,128]{1,0:T(8,128)}, bf16[8,512,640]{2,1,0:T(8,128)(2,1)}, f32[8,512,384]{2,1,0:T(8,128)}, bf16[8,1024,...) custom-call(bf16[8,512,320]{2,1,0:T(8,128)(2,1)} %get-tuple-element., ...), custom_call_target="tpu_custom_call" | custom-call | tf_op jit(solution)/shard_map/cond/branch_1_fun/pallas_call | solution.py:563
  88.4 0.0 copy-start
  88.5 71.2 %shard_map.417 = (bf16[8,512,320]{2,1,0:T(8,128)(2,1)}, f32[8,512,320]{2,1,0:T(8,128)}, bf16[6656,128]{1,0:T(8,128)(2,1)}, f32[9,1280]{1,0:T(8,128)}, f32[8,1280]{1,0:T(8,128)}, /*index=5*/f32[8,384]{1,0:T(8,128)}) custom-call(f32[3,4096,128]{2,1,0:T(8,128)} %get-tuple-element.222.res_hbm, bf16[8,512,320]{2,1,0:T(8,128)(2,1)} %bitcast.13, ...), custom_call_target="tpu_custom_call" | custom-call | tf_op jit(solution)/shard_map/pallas_call | solution.py:990
  159.7 0.0 copy-done
  159.7 127.7 %conditional.3 = ((f32[8,512,320]{2,1,0:T(8,128)}, f32[320,384]{1,0:T(8,128)}, f32[4,384,384]{2,1,0:T(8,128)}, f32[384,384]{1,0:T(8,128)}, f32[384,768]{1,0:T(8,...) conditional(s32[]{:T(128)} %bitcast.1, (bf16[8,512,640]{2,1,0:T(8,128)(2,1)}, ...), branch_computations={%region_2.0_spmd, %region_3.0_spmd} | conditional | bytes 8 | solution.py:1689
  171.4 116.0 %branch_1_fun.3 = (f32[8,512,320]{2,1,0:T(8,128)}, f32[320,384]{1,0:T(8,128)}, f32[4,384,384]{2,1,0:T(8,128)}, f32[384,384]{1,0:T(8,128)}, f32[384,768]{1,0:T(8,...) custom-call(bf16[8,512,640]{2,1,0:T(8,128)(2,1)} %get-tuple-element.124.q_ref, ...), custom_call_target="tpu_custom_call" | custom-call | tf_op jit(solution)/shard_map/cond/branch_1_fun/pallas_call | solution.py:1335
  287.5 0.0 copy-start.1
  287.5 38.6 %shard_map.418 = (bf16[8192,128]{1,0:T(8,128)(2,1)}, f32[256,128]{1,0:T(8,128)}) custom-call(f32[4,384,384]{2,1,0:T(8,128)} %get-tuple-element.236.dwr, f32[384,768]{1,0:T(8,128)} %get-tuple-element.237.dwkv, f32[384,384]{1,0:T(8,128)} %get-tuple-element.238.dwp, f32[320,384]{1,0:T(8,128)} %get-tuple-element.239.dwq, f32[9,1280]{1,0:T(8,128)} %get-tuple-element.240.dtap, ...), custom_call_target="tpu_custom_call" | custom-call | tf_op jit(solution)/shard_map/pallas_call | solution.py:1451
  326.1 0.0 copy-done.1
  326.1 12.1 %shard_map.419 = (bf16[8,512,320]{2,1,0:T(8,128)(2,1)}, f32[8,512,320]{2,1,0:T(8,128)}, f32[320]{0:T(512)}, f32[320]{0:T(512)}, f32[320,320]{1,0:T(8,128)}, /*in...) custom-call(bf16[8,512,320]{2,1,0:T(8,128)(2,1)} %get-tuple-element., ...), custom_call_target="tpu_custom_call" | custom-call | tf_op jit(solution)/shard_map/pallas_call | solution.py:1544
Async XLA Ops:
  88.4 71.3 %copy-start = (bf16[320,320]{1,0:T(8,128)(2,1)S(1)}, bf16[320,320]{1,0:T(8,128)(2,1)}, u32[]{:S(2)}) copy-start(bf16[320,320]{1,0:T(8,128)(2,1)} %qw.1) | copy-start | bytes 614404
  287.5 38.7 %copy-start.1 = (bf16[6656,128]{1,0:T(8,128)(2,1)S(1)}, bf16[6656,128]{1,0:T(8,128)(2,1)}, u32[]{:S(2)}) copy-start(bf16[6656,128]{1,0:T(8,128)(2,1)} %get-tuple-element.235.first) | copy-start | bytes 5111812

commit v4 on v3

--- a/solution.py
+++ b/solution.py
@@ -168,13 +168,19 @@
     return lay_out([("we", tall, ff // LANE), ("ws", channels, ff // LANE)], ndev)
 
 
-def rest_plan(channels, ndev):
-    cp = up_to(channels, LANE)
+def middle_plan(channels, ndev):
     tall = up_to(channels + 2, 16)
     return lay_out(
+        [("wkv", tall, 2 * channels // LANE), ("wp", channels, channels // LANE)], ndev
+    )
+
+
+def rest_plan(channels, ndev):
+    assert 4 * channels % LANE == 0 and 2 * channels % LANE == 0 and channels % LANE == HALF
+    return lay_out(
         [
-            ("wr", channels, 4 * cp // LANE), ("wkv", tall, 2 * cp // LANE),
-            ("wp", channels, cp // LANE), ("wq", channels, cp // LANE),
+            ("wr", channels, 4 * channels // LANE), ("wq", channels, channels // LANE),
+            ("halves", channels, 1),
         ],
         ndev,
     )
@@ -1040,11 +1046,12 @@
 
 def attback_kernel(
     dims, ff, ndp, blk, used, q_ref, att_ref, gres_ref, ke_ref, ve_ref, rn_ref, tok_ref, gres2_ref,
-    red_ref, vec_ref, wp_ref, wkv_ref, wq_ref, wr_ref, first_hbm,
-    ig_ref, dwqt, dwrt, dwp_ref, dwkv_ref, dbp_ref, dvec_ref, sum_hbm,
-    ge, dqt, gqt_ref, grn_ref, scr, gscr, own, acc, sib_land, up_land, down_land,
-    work, land, done,
-    sib_send, sib_recv, up_send, up_recv, down_send, down_recv, sum_send, sum_recv, sum_sem,
+    red_ref, vec_ref, wp_ref, wkv_ref, wq_ref, wr_ref, dtap, dtb, dvec2, cnt, first_hbm,
+    ig_ref, sum_hbm, mid_hbm, rest_hbm, small_hbm,
+    dwqt, dwrt, dwp_ref, dwkv_ref, dbp_ref, dvec_ref, ge, dqt, gqt_ref, grn_ref, scr, gscr, own, acc, sib_land, up_land, down_land,
+    gkv_ref, work, land, done, mid_work, mid_land, mid_done, rest_work, rest_land, rest_done, small_work, small_land, small_done,
+    sib_send, sib_recv, up_send, up_recv, down_send, down_recv, sum_send, sum_recv,
+    mid_send, mid_recv, rest_send, rest_recv, sum_sem,
 ):
     scenes, height, width, channels, cp = dims
     n = height * width
@@ -1062,6 +1069,19 @@
     parts = three_parts(work, land, done, ffn_plan(channels, ff, ndev)[2], [order] * 3)
     sums = Sums(parts, sum_send, sum_recv)
     each = -(-(sums.ops + 1) // (steps - 1))
+    mid_plan, mid_used, mid_sizes = middle_plan(channels, ndev)
+    mid = Sums(
+        three_parts(mid_work, mid_land, mid_done, mid_sizes, [order] * 3), mid_send, mid_recv
+    )
+    early = min(chips, mid.ops)
+
+    def put(buf, plan, name, value):
+        at, rows, slabs = plan[name]
+        for t in range(slabs):
+            buf[at + t * rows : at + (t + 1) * rows, :] = value(t, rows).astype(BF16)
+
+    def cut_of(value):
+        return lambda t, rows: value[:rows, t * LANE : (t + 1) * LANE]
 
     @pl.when(step == 0)
     def _():
@@ -1134,7 +1154,7 @@
             def _(at=at):
                 to_sib(s, at % used).start()
 
-        dwkv_ref[...] += dot(rn_ref[0, span].T, gkv)
+        gkv_ref[span, :] = gkv
 
     @pl.when(step < scenes)
     def _():
@@ -1235,6 +1255,7 @@
             dvec_ref[1:2] += jnp.sum(upstream, 0, keepdims=True)
             g = norm_back(upstream, vec_ref[2:3], rhat, rstd, channels)
             gred.append(inside(g, channels).astype(BF16))
+            dvec_ref[2:3] += jnp.sum(gred[i].astype(F32), 0, keepdims=True)
             x = widen(tok_ref[i].astype(F32), cp)
             xhat, xstd = centered(x, channels)
             hats.append((xhat, xstd))
@@ -1273,6 +1294,20 @@
             gx = norm_back(gn, vec_ref[0:1], xhat, xstd, channels)
             ig_ref[i] = gres2_ref[i] + gx[:, :channels]
 
+    @pl.when(step == scenes)
+    def _():
+        joined = jnp.concatenate([dwkv_ref[:, :channels], dwkv_ref[:, cp : cp + channels]], -1)
+        put(mid_work, mid_plan, "wkv", cut_of(joined))
+        put(mid_work, mid_plan, "wp", cut_of(dwp_ref))
+        if mid_used < mid_work.shape[0]:
+            mid_work[mid_used:, :] = jnp.zeros((mid_work.shape[0] - mid_used, LANE), BF16)
+
+    for t in range(early):
+
+        @pl.when(step == scenes + t)
+        def _(t=t):
+            mid.advance(t)
+
     @pl.when(step >= scenes)
     def _():
         tail((step - scenes) * together)
@@ -1282,6 +1317,7 @@
         s = step
         for j in range(1, count):
             chunk(j)
+        dwkv_ref[...] += dot(rn_ref[0].T, gkv_ref[...])
         for h in range(HEADS):
             base = h * LANE + (0 if h % 2 == 0 else HALF)
             gqt_ref[s, h * HALF : (h + 1) * HALF] = (
@@ -1290,6 +1326,62 @@
 
     @pl.when(step == steps - 1)
     def _():
+        plan, filled, sizes = rest_plan(channels, ndev)
+        splan, srows = small_plan(channels, ff, ndev)
+        full = channels // LANE
+
+        joined = jnp.concatenate([dwrt[ab, :channels, :channels] for ab in range(4)], -1)
+        put(rest_work, plan, "wr", cut_of(joined))
+        put(rest_work, plan, "wq", cut_of(dwqt))
+        last = pltpu.roll(dwqt[:, full * LANE :], HALF, 1)
+        put(
+            rest_work,
+            plan,
+            "halves",
+            lambda t, rows: jnp.where(
+                lanes((1, LANE)) < HALF, dwp_ref[:rows, full * LANE :], last
+            ),
+        )
+        if filled < rest_work.shape[0]:
+            rest_work[filled:, :] = jnp.zeros((rest_work.shape[0] - filled, LANE), BF16)
+        small_work[...] = jnp.zeros(small_work.shape, F32)
+        at, rows, slabs = splan["tap"]
+        db = jnp.sum(dtb[...], 0, keepdims=True)
+        for t in range(slabs):
+            cut = slice(t * LANE, (t + 1) * LANE)
+            small_work[at + t * rows : at + t * rows + 9, :] = dtap[:, cut]
+            small_work[at + t * rows + 9 : at + t * rows + 10, :] = db[:, cut]
+        at, rows, slabs = splan["vec"]
+        pb = jnp.sum(dbp_ref[...], 0, keepdims=True)
+        qb = widen(dwqt[:, full * LANE :].T[HALF : HALF + 1], cp)
+        for t in range(slabs):
+            cut = slice(t * LANE, (t + 1) * LANE)
+            low = at + t * rows
+            small_work[low : low + 3, :] = dvec2[0:3, cut]
+            small_work[low + 3 : low + 8, :] = dvec_ref[0:5, cut]
+            small_work[low + 8 : low + 9, :] = pb[:, cut]
+            small_work[low + 9 : low + 10, :] = qb[:, cut]
+        at, rows, _ = splan["count"]
+        small_work[at : at + rows, :] = cnt[...]
+
+        orders = orders_of(ndp, blk)
+        rest_parts = three_parts(rest_work, rest_land, rest_done, sizes, orders)
+        rest_parts.append((small_work, small_land, small_done, 0, srows, orders[0]))
+        rest = Sums(rest_parts, rest_send, rest_recv)
+        for k in range(max(rest.ops, mid.ops - early) + 1):
+            if k <= rest.ops:
+                rest.advance(k)
+            if k + early <= mid.ops:
+                mid.advance(k + early)
+        leave = [
+            pltpu.make_async_copy(rest_done, rest_hbm, sum_sem.at[1]),
+            pltpu.make_async_copy(small_done, small_hbm, sum_sem.at[2]),
+            pltpu.make_async_copy(mid_done, mid_hbm, sum_sem.at[3]),
+        ]
+        for copy in leave:
+            copy.start()
+        for copy in leave:
+            copy.wait()
         pltpu.make_async_copy(done, sum_hbm, sum_sem.at[0]).wait()
 
         @pl.loop(0, scenes)
@@ -1306,7 +1398,8 @@
 
 
 def attback(
-    dims, ff, ndp, blk, used, cid, q, att, gres, ke, ve, rn, tok, red, vec, wp, wkv, wq, wr, first
+    dims, ff, ndp, blk, used, cid, q, att, gres, ke, ve, rn, tok, red, vec, wp, wkv, wq, wr,
+    dtap, dtb, dvec2, cnt, first
 ):
     scenes, height, width, channels, cp = dims
     n = height * width
@@ -1317,6 +1410,9 @@
     he = HEADS * LANE
     together = -(-scenes // chips)
     assert scenes == together * chips
+    mid_rows = sum(middle_plan(channels, ndp * blk)[2])
+    rest_rows = sum(rest_plan(channels, ndp * blk)[2])
+    small_rows = small_plan(channels, ff, ndp * blk)[1]
     ops = 2 * len(orders_of(ndp, blk)[0])
 
     def early(shape):
@@ -1345,20 +1441,24 @@
             late((n, channels)),
             late((n, channels)),
             late((keys, cp)),
-            vm, vm, vm, vm, vm, hbm,
-        ],
-        out_specs=[late((n, channels))] + [vm] * 6 + [hbm],
+        ]
+        + [vm] * 9
+        + [hbm],
+        out_specs=[late((n, channels))] + [hbm] * 4,
         out_shape=[
             jax.ShapeDtypeStruct((scenes, n, channels), F32),
-            jax.ShapeDtypeStruct((channels, cp), F32),
-            jax.ShapeDtypeStruct((4, cp, cp), F32),
-            jax.ShapeDtypeStruct((cp, cp), F32),
-            jax.ShapeDtypeStruct((cp, 2 * cp), F32),
-            jax.ShapeDtypeStruct((8, cp), F32),
-            jax.ShapeDtypeStruct((8, cp), F32),
             jax.ShapeDtypeStruct(first.shape, BF16),
+            jax.ShapeDtypeStruct((mid_rows, LANE), BF16),
+            jax.ShapeDtypeStruct((rest_rows, LANE), BF16),
+            jax.ShapeDtypeStruct((small_rows, LANE), F32),
         ],
         scratch_shapes=[
+            pltpu.VMEM((channels, cp), F32),
+            pltpu.VMEM((4, cp, cp), F32),
+            pltpu.VMEM((cp, cp), F32),
+            pltpu.VMEM((cp, 2 * cp), F32),
+            pltpu.VMEM((8, cp), F32),
+            pltpu.VMEM((8, cp), F32),
             pltpu.VMEM((n, he), BF16),
             pltpu.VMEM((he, n), F32),
             pltpu.VMEM((scenes, channels, n), BF16),
@@ -1368,169 +1468,106 @@
             pltpu.VMEM((2, 2, used, keys, cp), BF16),
         ]
         + [pltpu.VMEM(land, BF16)] * 4
+        + [pltpu.VMEM((live, 2 * cp), BF16)]
         + [pltpu.VMEM(first.shape, BF16)] * 3
+        + [pltpu.VMEM((mid_rows, LANE), BF16)] * 3
+        + [pltpu.VMEM((rest_rows, LANE), BF16)] * 3
+        + [pltpu.VMEM((small_rows, LANE), F32)] * 3
         + [pltpu.SemaphoreType.DMA((scenes, used))] * 6
-        + [pltpu.SemaphoreType.DMA((3, ops, widest(ndp, blk)))] * 2
-        + [pltpu.SemaphoreType.DMA((1,))],
+        + [pltpu.SemaphoreType.DMA((3, ops, widest(ndp, blk)))] * 4
+        + [pltpu.SemaphoreType.DMA((4, ops, widest(ndp, blk)))] * 2
+        + [pltpu.SemaphoreType.DMA((4,))],
         compiler_params=pltpu.CompilerParams(
             vmem_limit_bytes=VMEM, collective_id=cid, has_side_effects=True
         ),
-    )(q, att, gres, ke, ve, rn, tok, gres, red, vec, wp, wkv, wq, wr, first)
-
-
-def reduce_kernel(
-    channels, ff, ndp, nblk, dwr, dwkv, dwp, dwq, dtap, dtb, dvec2, dvec1, dbp, cnt,
-    out_hbm, small_hbm, work, recv, done, swork, srecv, sdone, send_sem, recv_sem, out_sem,
-):
-    ndev = ndp * nblk
+    )(q, att, gres, ke, ve, rn, tok, gres, red, vec, wp, wkv, wq, wr, dtap, dtb, dvec2, cnt, first)
+
+
+def unpack_kernel(channels, ff, ndev, out_in, ig_in, first_in, middle_in, packed_in, small, *refs):
     cp = up_to(channels, LANE)
-    orders = orders_of(ndp, nblk)
-    plan, used, sizes = rest_plan(channels, ndev)
-    splan, srows = small_plan(channels, ff, ndev)
-    barrier = pltpu.get_barrier_semaphore()
-    peers = peers_of(orders[0])
-    for peer in peers:
-        pl.semaphore_signal(barrier, inc=1, device_id=peer, device_id_type=pl.DeviceIdType.MESH)
-
-    def put(name, ref):
-        at, rows, slabs = plan[name]
-        for t in range(slabs):
-            work[at + t * rows : at + (t + 1) * rows, :] = ref(t, rows).astype(BF16)
-
-    def lane_slabs(ref):
-        return lambda t, rows: ref[:rows, t * LANE : (t + 1) * LANE]
-
-    per = cp // LANE
-    put("wr", lambda t, rows: dwr[t // per, :rows, (t % per) * LANE : (t % per + 1) * LANE])
-    put("wkv", lane_slabs(dwkv))
-    put("wp", lane_slabs(dwp))
-    put("wq", lane_slabs(dwq))
-    if used < sum(sizes):
-        work[used:, :] = jnp.zeros((sum(sizes) - used, LANE), BF16)
-    swork[...] = jnp.zeros(swork.shape, F32)
-    at, rows, slabs = splan["tap"]
-    db = jnp.sum(dtb[...], 0, keepdims=True)
-    for t in range(slabs):
-        cut = slice(t * LANE, (t + 1) * LANE)
-        swork[at + t * rows : at + t * rows + 9, :] = dtap[:, cut]
-        swork[at + t * rows + 9 : at + t * rows + 10, :] = db[:, cut]
-    at, rows, slabs = splan["vec"]
-    pb = jnp.sum(dbp[...], 0, keepdims=True)
-    for t in range(slabs):
-        cut = slice(t * LANE, (t + 1) * LANE)
-        swork[at + t * rows : at + t * rows + 3, :] = dvec2[0:3, cut]
-        swork[at + t * rows + 3 : at + t * rows + 8, :] = dvec1[0:5, cut]
-        swork[at + t * rows + 8 : at + t * rows + 9, :] = pb[:, cut]
-    at, rows, _ = splan["count"]
-    swork[at : at + rows, :] = cnt[...]
-
-    pl.semaphore_wait(barrier, len(peers))
-    parts = three_parts(work, recv, done, sizes, orders)
-    parts.append((swork, srecv, sdone, 0, srows, orders[0]))
-    sums = Sums(parts, send_sem, recv_sem)
-    for k in range(sums.ops + 1):
-        sums.advance(k)
-
-    a = pltpu.make_async_copy(done, out_hbm, out_sem.at[0])
-    b = pltpu.make_async_copy(sdone, small_hbm, out_sem.at[1])
-    a.start()
-    b.start()
-    a.wait()
-    b.wait()
-
-
-def reduce_all(channels, ff, ndp, nblk, *grads):
-    ndev = ndp * nblk
-    ops = 2 * len(orders_of(ndp, nblk)[0])
-    wide = widest(ndp, nblk)
-    _, _, sizes = rest_plan(channels, ndev)
-    _, srows = small_plan(channels, ff, ndev)
-    total = sum(sizes)
-    vm = pl.BlockSpec(memory_space=pltpu.VMEM)
-    hbm = pl.BlockSpec(memory_space=pl.ANY)
-    return pl.pallas_call(
-        functools.partial(reduce_kernel, channels, ff, ndp, nblk),
-        in_specs=[vm] * len(grads),
-        out_specs=[hbm, hbm],
-        out_shape=[
-            jax.ShapeDtypeStruct((total, LANE), BF16),
-            jax.ShapeDtypeStruct((srows, LANE), F32),
-        ],
-        scratch_shapes=[pltpu.VMEM((total, LANE), BF16)] * 3
-        + [pltpu.VMEM((srows, LANE), F32)] * 3
-        + [
-            pltpu.SemaphoreType.DMA((4, ops, wide)),
-            pltpu.SemaphoreType.DMA((4, ops, wide)),
-            pltpu.SemaphoreType.DMA((2,)),
-        ],
-        compiler_params=pltpu.CompilerParams(
-            vmem_limit_bytes=VMEM, collective_id=1, has_side_effects=True
-        ),
-    )(*grads)
-
-
-def unpack_kernel(channels, ff, ndev, out_in, ig_in, first, packed, small, *outs):
-    cp = up_to(channels, LANE)
-    plans = ((first, ffn_plan(channels, ff, ndev)[0]), (packed, rest_plan(channels, ndev)[0]))
     splan, _ = small_plan(channels, ff, ndev)
-    out, ig, g1, b1, wq, qb, wr, rb, rg, rbn, wkv, vb, wp, pb, g2, b2, we, eb, dt, db, ws, sb, cm, out_hold, ig_hold, in_sem, out_sem = (
-        outs
+    names = (
+        ("out", "ig", "g1", "b1", "wq", "qb", "wr", "rb", "rg", "rbn", "wkv", "vb")
+        + ("wp", "pb", "g2", "b2", "we", "eb", "dt", "db", "ws", "sb", "cm")
     )
+    outs = dict(zip(names, refs[: len(names)]))
+    out_hold, ig_hold, first, middle, packed, we, ws, wr, wkv, in_sem, out_sem, sem = refs[len(names) :]
+    lt = cp // LANE
+    full = channels // LANE
+    loads = [
+        pltpu.make_async_copy(first_in, first, sem.at[0]),
+        pltpu.make_async_copy(middle_in, middle, sem.at[1]),
+        pltpu.make_async_copy(packed_in, packed, sem.at[2]),
+    ]
     ins, moves = [], []
-    for k, (src, hold, dst) in enumerate(((out_in, out_hold, out), (ig_in, ig_hold, ig))):
+    pairs = ((out_in, out_hold, outs["out"]), (ig_in, ig_hold, outs["ig"]))
+    for k, (src, hold, dst) in enumerate(pairs):
         for s in range(src.shape[0]):
             ins.append(pltpu.make_async_copy(src.at[s], hold.at[s], in_sem.at[k, s]))
             moves.append(pltpu.make_async_copy(hold.at[s], dst.at[s], out_sem.at[k, s]))
-    for copy in ins:
+    for copy in loads + ins:
         copy.start()
-    lt = cp // LANE
-
-    for copy, move in zip(ins, moves):
-        copy.wait()
-        move.start()
-
-    def slab(name, t, first=0, count=None):
-        ref, plan = plans[0] if name in plans[0][1] else plans[1]
+    plans = (
+        (first, ffn_plan(channels, ff, ndev)[0]), (middle, middle_plan(channels, ndev)[0]),
+        (packed, rest_plan(channels, ndev)[0]),
+    )
+    stores = [
+        pltpu.make_async_copy(src, outs[name], sem.at[3 + k])
+        for k, (src, name) in enumerate(((we, "we"), (ws, "ws"), (wr, "wr"), (wkv, "wkv")))
+    ]
+
+    def slab(name, t, low=0, count=None):
+        ref, plan = next(v for v in plans if name in v[1])
         at, rows, _ = plan[name]
         count = rows if count is None else count
-        return ref[at + t * rows + first : at + t * rows + first + count, :].astype(F32)
-
+        return ref[at + t * rows + low : at + t * rows + low + count, :].astype(F32)
+
+    def move(count):
+        for copy, on in list(zip(ins, moves))[count : count + len(ins) // 2]:
+            copy.wait()
+            on.start()
+
+    loads[0].wait()
     for t in range(ff // LANE):
         cut = slice(t * LANE, (t + 1) * LANE)
         we[:, cut] = slab("we", t, 0, channels)
-        eb[cut] = slab("we", t, channels, 16)[0]
+        outs["eb"][cut] = slab("we", t, channels, 16)[0]
         ws[:, cut] = slab("ws", t)
         at, rows, _ = splan["tap"]
-        dt[:, cut] = small[at + t * rows : at + t * rows + 9, :]
-        db[cut] = small[at + t * rows + 9, :]
-
-    def wide(name, first, count=None, base=0):
-        return jnp.concatenate([slab(name, base + t, first, count) for t in range(lt)], -1)
-
-    parts = [wide("wr", 0, base=ab * lt) for ab in range(4)]
-    wr[...] = jnp.concatenate([v[:, :channels] for v in parts], -1)
-    rb[...] = parts[0].T[channels]
-    turned = wide("wq", 0).T
-    wq[...] = turned[:channels]
-    qb[...] = turned[channels]
-    wp[...] = wide("wp", 0)[:, :channels]
-    wkv[...] = jnp.concatenate(
-        [wide("wkv", 0, channels)[:, :channels], wide("wkv", 0, channels, lt)[:, :channels]], -1
-    )
-    vb[...] = wide("wkv", channels, 16, lt)[1, :channels]
+        outs["dt"][:, cut] = small[at + t * rows : at + t * rows + 9, :]
+        outs["db"][cut] = small[at + t * rows + 9, :]
+    stores[0].start()
+    stores[1].start()
+    move(0)
+    loads[1].wait()
+    loads[2].wait()
+    for t in range(4 * channels // LANE):
+        wr[:, t * LANE : (t + 1) * LANE] = slab("wr", t)
+    stores[2].start()
+    for t in range(2 * channels // LANE):
+        wkv[:, t * LANE : (t + 1) * LANE] = slab("wkv", t, 0, channels)
+    stores[3].start()
+    tall = [slab("wkv", t, channels, 16) for t in range(2 * channels // LANE)]
+    outs["vb"][...] = jnp.concatenate(tall, -1)[1, channels:]
+    halves = slab("halves", 0)
+    wp = [slab("wp", t) for t in range(full)] + [halves]
+    outs["wp"][...] = jnp.concatenate(wp, -1)[:, :channels]
+    wq = [slab("wq", t) for t in range(full)] + [pltpu.roll(halves, HALF, 1)]
+    outs["wq"][...] = jnp.concatenate(wq, -1).T[:channels]
     at, rows, _ = splan["vec"]
     vec = jnp.concatenate([small[at + t * rows : at + (t + 1) * rows, :] for t in range(lt)], -1)
     vec = vec[:, :channels]
-    for k, ref in enumerate((g2, b2, sb, rg, rbn, None, g1, b1, pb)):
-        if ref is not None:
-            ref[...] = vec[k]
+    order = ("g2", "b2", "sb", "rg", "rbn", "rb", "g1", "b1", "pb", "qb")
+    for k, name in enumerate(order):
+        outs[name][...] = vec[k]
     at, rows, _ = splan["count"]
-    cm[...] = small[at : at + rows, :].astype(jnp.int32)[:CLASSES, :CLASSES]
-    for move in moves:
-        move.wait()
-
-
-def unpack(channels, ff, ndev, out, ig, first, packed, small):
+    outs["cm"][...] = small[at : at + rows, :].astype(jnp.int32)[:CLASSES, :CLASSES]
+    move(len(ins) // 2)
+    for copy in moves + stores:
+        copy.wait()
+
+
+def unpack(channels, ff, ndev, out, ig, first, middle, packed, small):
     one = (channels,)
     shapes = [
         one, one, (channels, channels), one, (channels, 4 * channels), one, one, one,
@@ -1541,19 +1578,28 @@
     outs.append(jax.ShapeDtypeStruct((CLASSES, CLASSES), jnp.int32))
     vm = pl.BlockSpec(memory_space=pltpu.VMEM)
     hbm = pl.BlockSpec(memory_space=pl.ANY)
+    big = {4, 8, 14, 18}
     return pl.pallas_call(
         functools.partial(unpack_kernel, channels, ff, ndev),
-        in_specs=[hbm, hbm, vm, vm, vm],
-        out_specs=[hbm, hbm] + [vm] * len(outs),
+        in_specs=[hbm] * 5 + [vm],
+        out_specs=[hbm, hbm] + [hbm if k in big else vm for k in range(len(outs))],
         out_shape=[jax.ShapeDtypeStruct(v.shape, v.dtype) for v in (out, ig)] + outs,
         scratch_shapes=[
             pltpu.VMEM(out.shape, out.dtype),
             pltpu.VMEM(ig.shape, ig.dtype),
+            pltpu.VMEM(first.shape, first.dtype),
+            pltpu.VMEM(middle.shape, middle.dtype),
+            pltpu.VMEM(packed.shape, packed.dtype),
+            pltpu.VMEM((channels, ff), F32),
+            pltpu.VMEM((channels, ff), F32),
+            pltpu.VMEM((channels, 4 * channels), F32),
+            pltpu.VMEM((channels, 2 * channels), F32),
             pltpu.SemaphoreType.DMA((2, out.shape[0])),
             pltpu.SemaphoreType.DMA((2, out.shape[0])),
+            pltpu.SemaphoreType.DMA((7,)),
         ],
         compiler_params=pltpu.CompilerParams(vmem_limit_bytes=VMEM),
-    )(out, ig, first, packed, small)
+    )(out, ig, first, middle, packed, small)
 
 
 def split_low(value):
@@ -1702,14 +1748,11 @@
         dims, blk, ndp * blk, res, ct, expand_weight, shrink_weight.T, vec, expand_rows, depth_weight,
         tap_bias,
     )
-    ig, dwqt, dwrt, dwp, dwkv, dbp, dvec1, first = either(
+    ig, first, middle, packed, small = either(
         attback, (4, 5), (dims, ff, ndp, blk), q, att, gres, ke, ve, rn, tok, red, vec, wp, wkv,
-        query_weight, wr, first,
+        query_weight, wr, dtap, dtb, dvec2, counts, first,
     )
-    packed, small = reduce_all(
-        channels, ff, ndp, blk, dwrt, dwkv, dwp, dwqt, dtap, dtb, dvec2, dvec1, dbp, counts
-    )
-    out, ig, *grads = unpack(channels, ff, ndp * blk, out, ig, first, packed, small)
+    out, ig, *grads = unpack(channels, ff, ndp * blk, out, ig, first, middle, packed, small)
     grads[4], grads[18] = grads[4].T, grads[18].T
     return (out.reshape(tokens.shape), ig.reshape(tokens.shape), *grads)
 

time: 344 us -> 332 us (0.965)
  Pallas kernels: 325 us -> 313 us
    pallas_call x1 -> x0, Pallas kernels: 38.6 us -> none  [reduce_all(): pl.pallas_call(functools.partial(reduce_kernel, channels, ff, ndp, nblk),...]
    pallas_call x1, Pallas kernels: 116 us -> 143 us  [attback(): pl.pallas_call(functools.partial(attback_kernel, dims, ff, ndp, blk, used...]
where the time goes in v4:
time: 332 us; the launch traced here: 326 us
  Pallas kernels  313 us (94%)
  loops' own time  12 us (4%)
    pallas_call x1, Pallas kernels, attback(): pl.pallas_call(functools.partial(attback_kernel, dims, ff, ndp, blk, used...  143 us
    pallas_call x1, Pallas kernels, attend(): pl.pallas_call(functools.partial(attend_kernel, dims, blk, used), grid=(s...  83.4 us
    pallas_call x1, Pallas kernels, ffn(): pl.pallas_call(functools.partial(ffn_kernel, dims, ff, blk, ndev), in_spe...  71.4 us
    another operation x2, loops' own time, either(): lax.cond(full, functools.partial(call, *sizes, chips, cids[1]), functools...  12 us
    pallas_call x1, Pallas kernels, unpack(): pl.pallas_call(functools.partial(unpack_kernel, channels, ff, ndev), in_s...  11.5 us

profile of v4, /device:TPU:0, one launch (start us, length us, event | category | flops | bytes accessed | tf_op | source)
XLA Modules:
  0.0 326.3 jit_solution(15326409144855250396)
XLA Ops:
  0.7 3.1 shard_map.416
  4.4 83.6 %conditional.2 = ((f32[8,128,384]{2,1,0:T(8,128)}, f32[32,128]{1,0:T(8,128)}, bf16[8,512,640]{2,1,0:T(8,128)(2,1)}, f32[8,512,384]{2,1,0:T(8,128)}, bf16[8,1024,...) conditional(s32[]{:T(128)} %bitcast.1, ...), branch_computations={%region_0.0_spmd, %region_1.0_spmd} | conditional | bytes 8 | solution.py:1735
  4.6 83.4 %branch_1_fun.2 = (f32[8,128,384]{2,1,0:T(8,128)}, f32[32,128]{1,0:T(8,128)}, bf16[8,512,640]{2,1,0:T(8,128)(2,1)}, f32[8,512,384]{2,1,0:T(8,128)}, bf16[8,1024,...) custom-call(bf16[8,512,320]{2,1,0:T(8,128)(2,1)} %get-tuple-element., ...), custom_call_target="tpu_custom_call" | custom-call | tf_op jit(solution)/shard_map/cond/branch_1_fun/pallas_call | solution.py:569
  88.1 0.0 copy-start
  88.1 71.4 %shard_map.417 = (bf16[8,512,320]{2,1,0:T(8,128)(2,1)}, f32[8,512,320]{2,1,0:T(8,128)}, bf16[6656,128]{1,0:T(8,128)(2,1)}, f32[9,1280]{1,0:T(8,128)}, f32[8,1280]{1,0:T(8,128)}, /*index=5*/f32[8,384]{1,0:T(8,128)}) custom-call(f32[3,4096,128]{2,1,0:T(8,128)} %get-tuple-element.241.res_hbm, bf16[8,512,320]{2,1,0:T(8,128)(2,1)} %bitcast.13, ...), custom_call_target="tpu_custom_call" | custom-call | tf_op jit(solution)/shard_map/pallas_call | solution.py:996
  159.5 0.0 copy-done
  159.5 154.8 %conditional.3 = ((f32[8,512,320]{2,1,0:T(8,128)}, bf16[6656,128]{1,0:T(8,128)(2,1)}, bf16[2560,128]{1,0:T(8,128)(2,1)}, bf16[4608,128]{1,0:T(8,128)(2,1)}, f32[256,128]{1,0:T(8,128)})) conditional(s32[]{:T(128)} %bitcast.1, (bf16[8,512,640]{2,1,0:T(8,128)(2,1)}, f32[8,512,384]{2,1,0:T(8,128)}, f32[8,512,320]{2,1,0:T(8,128)}, ...), branch_computations={%region_2.0_spmd, %region_3.0_spmd} | conditional | bytes 8 | solution.py:1735
  171.3 143.1 %branch_1_fun.3 = (f32[8,512,320]{2,1,0:T(8,128)}, bf16[6656,128]{1,0:T(8,128)(2,1)}, bf16[2560,128]{1,0:T(8,128)(2,1)}, bf16[4608,128]{1,0:T(8,128)(2,1)}, f32[256,128]{1,0:T(8,128)}) custom-call(bf16[8,512,640]{2,1,0:T(8,128)(2,1)} %get-tuple-element.144.q_ref, f32[8,512,384]{2,1,0:T(8,128)} %get-tuple-element.145.att_ref, ...), custom_call_target="tpu_custom_call" | custom-call | tf_op jit(solution)/shard_map/cond/branch_1_fun/pallas_call | solution.py:1431
  314.4 11.5 %shard_map.418 = (bf16[8,512,320]{2,1,0:T(8,128)(2,1)}, f32[8,512,320]{2,1,0:T(8,128)}, f32[320]{0:T(512)}, f32[320]{0:T(512)}, f32[320,320]{1,0:T(8,128)}, /*in...) custom-call(bf16[8,512,320]{2,1,0:T(8,128)(2,1)} %get-tuple-element., ...), custom_call_target="tpu_custom_call" | custom-call | tf_op jit(solution)/shard_map/pallas_call | solution.py:1582
Async XLA Ops:
  88.1 71.5 %copy-start = (bf16[320,320]{1,0:T(8,128)(2,1)S(1)}, bf16[320,320]{1,0:T(8,128)(2,1)}, u32[]{:S(2)}) copy-start(bf16[320,320]{1,0:T(8,128)(2,1)} %qw.1) | copy-start | bytes 614404

commit v5 on v4

--- a/solution.py
+++ b/solution.py
@@ -386,7 +386,7 @@
         low = (xhat * vec_ref[0:1] + vec_ref[1:2]).astype(BF16)
         lowf = low.astype(F32)
         for t in range(cp // LANE):
-            scr[t] = lowf[:, t * LANE : (t + 1) * LANE]
+            scr[t, :n] = lowf[:, t * LANE : (t + 1) * LANE]
         total = jnp.zeros((keys, cp), F32)
         for b in range(2):
             part = [scr[t, pl.ds(b, n // 2, stride=2), :] for t in range(cp // LANE)]
@@ -581,7 +581,7 @@
             late((live, he)),
             late((live, he)),
             late((live, cp)),
-            whole((cp // LANE, scenes * n, LANE)),
+            whole((cp // LANE, scenes * n + 2 * scenes, LANE)),
         ],
         out_shape=[
             jax.ShapeDtypeStruct((scenes, keys, cp), F32),
@@ -591,10 +591,10 @@
             jax.ShapeDtypeStruct((scenes, k, he), BF16),
             jax.ShapeDtypeStruct((scenes, k, he), BF16),
             jax.ShapeDtypeStruct((scenes, k, cp), BF16),
-            jax.ShapeDtypeStruct((cp // LANE, scenes * n, LANE), F32),
+            jax.ShapeDtypeStruct((cp // LANE, scenes * n + 2 * scenes, LANE), F32),
         ],
         scratch_shapes=[
-            pltpu.VMEM((cp // LANE, n, LANE), F32),
+            pltpu.VMEM((cp // LANE, n + 8, LANE), F32),
             pltpu.VMEM((lag + 1, n, he), BF16),
             pltpu.VMEM((HEADS, n, LANE), F32),
             pltpu.VMEM((scenes, 2 * used, packed_rows(keys, cp), LANE), BF16),
@@ -1017,8 +1017,8 @@
             pltpu.VMEM((cp, total), BF16),
             pltpu.VMEM((total, cp), BF16),
             pltpu.VMEM((cp, total), BF16),
-            pltpu.VMEM((lt, total, LANE), F32),
-            pltpu.VMEM((lt, total, LANE), F32),
+            pltpu.VMEM((lt, total + 2 * scenes, LANE), F32),
+            pltpu.VMEM((lt, total + 2 * scenes, LANE), F32),
             pltpu.VMEM((2, height + 2) + strip, BF16),
             pltpu.VMEM((2, height + 2) + strip, BF16),
             pltpu.VMEM((nchunk, 2) + strip, BF16),
@@ -1262,7 +1262,7 @@
             low.append((xhat * vec_ref[0:1] + vec_ref[1:2]).astype(BF16))
             lowf = low[i].astype(F32)
             for t in range(lt):
-                scr[i, t] = lowf[:, t * LANE : (t + 1) * LANE]
+                scr[i, t, :n] = lowf[:, t * LANE : (t + 1) * LANE]
         gred = jnp.concatenate(gred, 0)
         gred_t = gred.T
         for b in range(2):
@@ -1288,7 +1288,7 @@
             xhat, xstd = hats[i]
             dwqt[...] += dot(gqt, low[i])
             gn = widen(dot_nt(gqt.T, wq_ref[...]), cp)
-            gn = gn + jnp.concatenate([gscr[i, t] for t in range(lt)], -1)
+            gn = gn + jnp.concatenate([gscr[i, t, :n] for t in range(lt)], -1)
             dvec_ref[3:4] += jnp.sum(gn * xhat, 0, keepdims=True)
             dvec_ref[4:5] += jnp.sum(gn, 0, keepdims=True)
             gx = norm_back(gn, vec_ref[0:1], xhat, xstd, channels)
@@ -1463,8 +1463,8 @@
             pltpu.VMEM((he, n), F32),
             pltpu.VMEM((scenes, channels, n), BF16),
             pltpu.VMEM((scenes, keys, cp), F32),
-            pltpu.VMEM((together, lt, n, LANE), F32),
-            pltpu.VMEM((together, lt, n, LANE), F32),
+            pltpu.VMEM((together, lt, n + 8, LANE), F32),
+            pltpu.VMEM((together, lt, n + 8, LANE), F32),
             pltpu.VMEM((2, 2, used, keys, cp), BF16),
         ]
         + [pltpu.VMEM(land, BF16)] * 4

time: 332 us -> 333 us (level)
  no operation moved by 1% of the time
where the time goes in v5:
time: 333 us; the launch traced here: 328 us
  Pallas kernels  314 us (94%)
  loops' own time  12 us (4%)
    pallas_call x1, Pallas kernels, attback(): pl.pallas_call(functools.partial(attback_kernel, dims, ff, ndp, blk, used...  143 us
    pallas_call x1, Pallas kernels, attend(): pl.pallas_call(functools.partial(attend_kernel, dims, blk, used), grid=(s...  84.4 us
    pallas_call x1, Pallas kernels, ffn(): pl.pallas_call(functools.partial(ffn_kernel, dims, ff, blk, ndev), in_spe...  71.8 us
    another operation x2, loops' own time, either(): lax.cond(full, functools.partial(call, *sizes, chips, cids[1]), functools...  12 us
    pallas_call x1, Pallas kernels, unpack(): pl.pallas_call(functools.partial(unpack_kernel, channels, ff, ndev), in_s...  11.5 us

profile of v5, /device:TPU:0, one launch (start us, length us, event | category | flops | bytes accessed | tf_op | source)
XLA Modules:
  0.0 327.8 jit_solution(7609818660487364566)
XLA Ops:
  0.7 3.1 shard_map.416
  4.4 84.6 %conditional.2 = ((f32[8,128,384]{2,1,0:T(8,128)}, f32[32,128]{1,0:T(8,128)}, bf16[8,512,640]{2,1,0:T(8,128)(2,1)}, f32[8,512,384]{2,1,0:T(8,128)}, bf16[8,1024,...) conditional(s32[]{:T(128)} %bitcast.1, ...), branch_computations={%region_0.0_spmd, %region_1.0_spmd} | conditional | bytes 8 | solution.py:1735
  4.6 84.4 %branch_1_fun.2 = (f32[8,128,384]{2,1,0:T(8,128)}, f32[32,128]{1,0:T(8,128)}, bf16[8,512,640]{2,1,0:T(8,128)(2,1)}, f32[8,512,384]{2,1,0:T(8,128)}, bf16[8,1024,...) custom-call(bf16[8,512,320]{2,1,0:T(8,128)(2,1)} %get-tuple-element., ...), custom_call_target="tpu_custom_call" | custom-call | tf_op jit(solution)/shard_map/cond/branch_1_fun/pallas_call | solution.py:569
  89.1 0.0 copy-start
  89.1 71.8 %shard_map.417 = (bf16[8,512,320]{2,1,0:T(8,128)(2,1)}, f32[8,512,320]{2,1,0:T(8,128)}, bf16[6656,128]{1,0:T(8,128)(2,1)}, f32[9,1280]{1,0:T(8,128)}, f32[8,1280]{1,0:T(8,128)}, /*index=5*/f32[8,384]{1,0:T(8,128)}) custom-call(f32[3,4112,128]{2,1,0:T(8,128)} %get-tuple-element.241.res_hbm, bf16[8,512,320]{2,1,0:T(8,128)(2,1)} %bitcast.13, ...), custom_call_target="tpu_custom_call" | custom-call | tf_op jit(solution)/shard_map/pallas_call | solution.py:996
  160.9 0.0 copy-done
  160.9 154.9 %conditional.3 = ((f32[8,512,320]{2,1,0:T(8,128)}, bf16[6656,128]{1,0:T(8,128)(2,1)}, bf16[2560,128]{1,0:T(8,128)(2,1)}, bf16[4608,128]{1,0:T(8,128)(2,1)}, f32[256,128]{1,0:T(8,128)})) conditional(s32[]{:T(128)} %bitcast.1, (bf16[8,512,640]{2,1,0:T(8,128)(2,1)}, f32[8,512,384]{2,1,0:T(8,128)}, f32[8,512,320]{2,1,0:T(8,128)}, ...), branch_computations={%region_2.0_spmd, %region_3.0_spmd} | conditional | bytes 8 | solution.py:1735
  172.7 143.2 %branch_1_fun.3 = (f32[8,512,320]{2,1,0:T(8,128)}, bf16[6656,128]{1,0:T(8,128)(2,1)}, bf16[2560,128]{1,0:T(8,128)(2,1)}, bf16[4608,128]{1,0:T(8,128)(2,1)}, f32[256,128]{1,0:T(8,128)}) custom-call(bf16[8,512,640]{2,1,0:T(8,128)(2,1)} %get-tuple-element.144.q_ref, f32[8,512,384]{2,1,0:T(8,128)} %get-tuple-element.145.att_ref, ...), custom_call_target="tpu_custom_call" | custom-call | tf_op jit(solution)/shard_map/cond/branch_1_fun/pallas_call | solution.py:1431
  315.9 11.5 %shard_map.418 = (bf16[8,512,320]{2,1,0:T(8,128)(2,1)}, f32[8,512,320]{2,1,0:T(8,128)}, f32[320]{0:T(512)}, f32[320]{0:T(512)}, f32[320,320]{1,0:T(8,128)}, /*in...) custom-call(bf16[8,512,320]{2,1,0:T(8,128)(2,1)} %get-tuple-element., ...), custom_call_target="tpu_custom_call" | custom-call | tf_op jit(solution)/shard_map/pallas_call | solution.py:1582
Async XLA Ops:
  89.1 71.9 %copy-start = (bf16[320,320]{1,0:T(8,128)(2,1)S(1)}, bf16[320,320]{1,0:T(8,128)(2,1)}, u32[]{:S(2)}) copy-start(bf16[320,320]{1,0:T(8,128)(2,1)} %qw.1) | copy-start | bytes 614404

commit v6 on v5

--- a/solution.py
+++ b/solution.py
@@ -408,7 +408,6 @@
         @pl.when(chip < used)
         def _():
             rnbuf[s, slot(chip, core)] = own
-            send_sib(s, chip).start()
 
             @pl.when(chip < chips - 1)
             def _():
@@ -417,6 +416,8 @@
             @pl.when(chip > 0)
             def _():
                 send_down(s, chip).start()
+
+            send_sib(s, chip).start()
 
         qf = dot(low, wq_ref[...]) * (LOG2E * head_size**-0.5)
         ones = head_blocks(qf, lambda e: free_row(e, {0: 1.0, 1: 1.0, 2: 1.0}))
@@ -443,22 +444,24 @@
             @pl.when(jnp.logical_and(below >= 0, below < used))
             def _():
                 send_up(s, below).wait_recv()
-                send_sib(s, below).start()
 
                 @pl.when(chip < chips - 1)
                 def _():
                     send_up(s, below).start()
 
+                send_sib(s, below).start()
+
             above = chip + age
 
             @pl.when(above < used)
             def _():
                 send_down(s, above).wait_recv()
-                send_sib(s, above).start()
 
                 @pl.when(chip > 0)
                 def _():
                     send_down(s, above).start()
+
+                send_sib(s, above).start()
 
     @pl.when(step >= lag)
     def _():

time: 333 us -> 333 us (level)
  no operation moved by 1% of the time
where the time goes in v6:
time: 333 us; the launch traced here: 328 us
  Pallas kernels  314 us (94%)
  loops' own time  12 us (4%)
    pallas_call x1, Pallas kernels, attback(): pl.pallas_call(functools.partial(attback_kernel, dims, ff, ndp, blk, used...  143 us
    pallas_call x1, Pallas kernels, attend(): pl.pallas_call(functools.partial(attend_kernel, dims, blk, used), grid=(s...  84.4 us
    pallas_call x1, Pallas kernels, ffn(): pl.pallas_call(functools.partial(ffn_kernel, dims, ff, blk, ndev), in_spe...  71.8 us
    another operation x2, loops' own time, either(): lax.cond(full, functools.partial(call, *sizes, chips, cids[1]), functools...  12 us
    pallas_call x1, Pallas kernels, unpack(): pl.pallas_call(functools.partial(unpack_kernel, channels, ff, ndev), in_s...  11.5 us

profile of v6, /device:TPU:0, one launch (start us, length us, event | category | flops | bytes accessed | tf_op | source)
XLA Modules:
  0.0 327.8 jit_solution(9047027974079827307)
XLA Ops:
  0.7 3.1 shard_map.416
  4.4 84.7 %conditional.2 = ((f32[8,128,384]{2,1,0:T(8,128)}, f32[32,128]{1,0:T(8,128)}, bf16[8,512,640]{2,1,0:T(8,128)(2,1)}, f32[8,512,384]{2,1,0:T(8,128)}, bf16[8,1024,...) conditional(s32[]{:T(128)} %bitcast.1, ...), branch_computations={%region_0.0_spmd, %region_1.0_spmd} | conditional | bytes 8 | solution.py:1738
  4.6 84.4 %branch_1_fun.2 = (f32[8,128,384]{2,1,0:T(8,128)}, f32[32,128]{1,0:T(8,128)}, bf16[8,512,640]{2,1,0:T(8,128)(2,1)}, f32[8,512,384]{2,1,0:T(8,128)}, bf16[8,1024,...) custom-call(bf16[8,512,320]{2,1,0:T(8,128)(2,1)} %get-tuple-element., ...), custom_call_target="tpu_custom_call" | custom-call | tf_op jit(solution)/shard_map/cond/branch_1_fun/pallas_call | solution.py:572
  89.1 0.0 copy-start
  89.1 71.8 %shard_map.417 = (bf16[8,512,320]{2,1,0:T(8,128)(2,1)}, f32[8,512,320]{2,1,0:T(8,128)}, bf16[6656,128]{1,0:T(8,128)(2,1)}, f32[9,1280]{1,0:T(8,128)}, f32[8,1280]{1,0:T(8,128)}, /*index=5*/f32[8,384]{1,0:T(8,128)}) custom-call(f32[3,4112,128]{2,1,0:T(8,128)} %get-tuple-element.241.res_hbm, bf16[8,512,320]{2,1,0:T(8,128)(2,1)} %bitcast.13, ...), custom_call_target="tpu_custom_call" | custom-call | tf_op jit(solution)/shard_map/pallas_call | solution.py:999
  160.9 0.0 copy-done
  160.9 154.9 %conditional.3 = ((f32[8,512,320]{2,1,0:T(8,128)}, bf16[6656,128]{1,0:T(8,128)(2,1)}, bf16[2560,128]{1,0:T(8,128)(2,1)}, bf16[4608,128]{1,0:T(8,128)(2,1)}, f32[256,128]{1,0:T(8,128)})) conditional(s32[]{:T(128)} %bitcast.1, (bf16[8,512,640]{2,1,0:T(8,128)(2,1)}, f32[8,512,384]{2,1,0:T(8,128)}, f32[8,512,320]{2,1,0:T(8,128)}, ...), branch_computations={%region_2.0_spmd, %region_3.0_spmd} | conditional | bytes 8 | solution.py:1738
  172.7 143.1 %branch_1_fun.3 = (f32[8,512,320]{2,1,0:T(8,128)}, bf16[6656,128]{1,0:T(8,128)(2,1)}, bf16[2560,128]{1,0:T(8,128)(2,1)}, bf16[4608,128]{1,0:T(8,128)(2,1)}, f32[256,128]{1,0:T(8,128)}) custom-call(bf16[8,512,640]{2,1,0:T(8,128)(2,1)} %get-tuple-element.144.q_ref, f32[8,512,384]{2,1,0:T(8,128)} %get-tuple-element.145.att_ref, ...), custom_call_target="tpu_custom_call" | custom-call | tf_op jit(solution)/shard_map/cond/branch_1_fun/pallas_call | solution.py:1434
  315.8 11.5 %shard_map.418 = (bf16[8,512,320]{2,1,0:T(8,128)(2,1)}, f32[8,512,320]{2,1,0:T(8,128)}, f32[320]{0:T(512)}, f32[320]{0:T(512)}, f32[320,320]{1,0:T(8,128)}, /*in...) custom-call(bf16[8,512,320]{2,1,0:T(8,128)(2,1)} %get-tuple-element., ...), custom_call_target="tpu_custom_call" | custom-call | tf_op jit(solution)/shard_map/pallas_call | solution.py:1585
Async XLA Ops:
  89.1 71.8 %copy-start = (bf16[320,320]{1,0:T(8,128)(2,1)S(1)}, bf16[320,320]{1,0:T(8,128)(2,1)}, u32[]{:S(2)}) copy-start(bf16[320,320]{1,0:T(8,128)(2,1)} %qw.1) | copy-start | bytes 614404
